TPU v7x, 512 devices: a whole 4x4x16 slice. The times are simulated.
512 devices in a mesh: tile: 64 (over z, y_hi, core), mem: 8 (over x, y_lo).
Axes of the slice: x: 4, y: 4 (y_hi: 2, y_lo: 2; y = y_hi * 2 + y_lo), z: 16, core: 2. Of those that a mesh axis runs over, the one named last changes fastest.
Arguments:
- member_tracer_state: float32 [64, 8, 16, 16384], P('mem', None, None, 'tile'), may hold values from -6 to 6
- diffusivity: float32 [4, 16, 16384], P(None, None, 'tile'), may hold values from 0.02 to 0.15
- velocity: float32 [4, 16, 16384], P(None, None, 'tile'), may hold values from -0.4 to 0.4
- wet_mask: int32 [16, 16384], P(None, 'tile'), may hold values from 0 to 1, as said below
- obs_cell: int32 [8192], P('tile'), may hold values from 0 to 4095, as said below
- obs_count: int32 [64], P('tile'), may hold values from 1 to 128, as said below
- obs_value: float32 [8192], P('tile'), may hold values from -6 to 6
- obs_error: float32 [8192], P('tile'), may hold values from 0.2 to 1
Outputs:
- analysis: float32 [64, 8, 16, 16384], P('mem', None, None, 'tile')
Inputs may be any that keep to these rules, and one draw needn't show every extreme that they name: `wet_mask`: 1 marks an ocean cell, 0 land; every block of 256 columns has some ocean cells and at least one block is all ocean. `obs_count`: how many of a block's 128 slots are in use; one block uses all of them. `obs_cell`: a cell of the block as row * 256 + column; the slots of a block are distinct cells, and those in use are ocean cells.
All inputs are finite; a program needn't handle non-finite values.
Results may differ from a plain program's by a relative error of at most 0.00018.
Values sent between devices are 32-bit elements; how exact they have to be, the bound alone decides.
No kernel may reach another device: no remote copies, remote signals or barrier semaphores. Data moves between devices by JAX's collectives and lax.ppermute only.
A program may use at most 64 MiB of HBM per device.

v0:
```python
import jax
import jax.numpy as jnp
from jax import lax
from jax.sharding import PartitionSpec as P


def padded(block, sides, width):
    for axis, dim in sides:
        count = lax.axis_size(axis)
        forward = [(i, i + 1) for i in range(count - 1)]
        forward.append((count - 1, 0))
        backward = [(target, source) for source, target in forward]
        low = lax.ppermute(
            lax.slice_in_dim(block, block.shape[dim] - width, None, axis=dim), axis, forward
        )
        high = lax.ppermute(lax.slice_in_dim(block, 0, width, axis=dim), axis, backward)
        block = jnp.concatenate([low, block, high], axis=dim)
    return block


def advect_tracers(padded_state, statics):
    levels = (statics.shape[0] - 1) // 2
    diffuse = statics[:levels]
    velocity = statics[levels : 2 * levels]
    wet_flag = statics[2 * levels]
    member_index = padded_state.shape[0]
    latitude_rows = padded_state.shape[2]
    grid_columns = padded_state.shape[3]
    tracer_field = padded_state.reshape(member_index, 2, levels, latitude_rows, grid_columns)
    west_cells = tracer_field[..., :-1]
    east_cells = tracer_field[..., 1:]
    face_diffuse = 0.5 * (diffuse[..., :-1] + diffuse[..., 1:])
    face_speed = 0.5 * (velocity[..., :-1] + velocity[..., 1:])
    face_wet = wet_flag[:, :-1] * wet_flag[:, 1:]
    zonal_flux = face_wet * (
        jnp.maximum(face_speed, 0.0) * west_cells
        + jnp.minimum(face_speed, 0.0) * east_cells
        - face_diffuse * (east_cells - west_cells)
    )
    middle = tracer_field[..., 1:-1]
    inner_diffuse = diffuse[..., 1:-1]
    inner_wet = wet_flag[:, 1:-1]
    north_diffuse = 0.5 * (inner_diffuse[:, :-1] + inner_diffuse[:, 1:])
    north_wet = inner_wet[:-1] * inner_wet[1:]
    north_flux = -north_wet * north_diffuse * (middle[..., 1:, :] - middle[..., :-1, :])
    zero_row = jnp.zeros_like(middle[..., :1, :])
    outflow = jnp.concatenate([north_flux, zero_row], 3)
    inflow = jnp.concatenate([zero_row, north_flux], 3)
    change = zonal_flux[..., :-1] - zonal_flux[..., 1:] + inflow - outflow
    updated = middle + inner_wet * change
    return updated.reshape(member_index, 2 * levels, latitude_rows, grid_columns - 2)


def coefficients(observed, obs_value, obs_error, in_use, locality):
    ens_size = observed.shape[0]
    ens_mean = jnp.sum(observed, 0) / ens_size
    anomaly = (observed - ens_mean) * in_use
    innovation = (obs_value - ens_mean) * in_use
    system = jnp.dot(anomaly.T, anomaly, precision=lax.Precision.HIGHEST) + (
        ens_size - 1
    ) * jnp.diag(obs_error / locality)
    factor = jnp.linalg.cholesky(system)
    right_sides = jnp.concatenate([innovation[:, None], anomaly.T], 1)
    solved = jax.scipy.linalg.cho_solve((factor, True), right_sides)
    mixed = jnp.dot(anomaly, solved, precision=lax.Precision.HIGHEST)
    return mixed[:, :1] - 0.5 * mixed[:, 1:]


def local(
    member_tracer_state, diffusivity, velocity, wet_mask, obs_cell, obs_count, obs_value, obs_error
):
    statics = jnp.concatenate([diffusivity, velocity, wet_mask.astype(jnp.float32)[None]], 0)
    halo_depth = 1
    static_padding = padded(statics, (("tile", 2),), halo_depth)
    prior_state = member_tracer_state
    for sweep_number in range(2):
        padded_state = padded(prior_state, (("tile", 3),), 1)
        prior_state = advect_tracers(padded_state, static_padding)
    member_index = prior_state.shape[0]
    latitude_rows = prior_state.shape[2]
    grid_columns = prior_state.shape[3]
    obs_slots = obs_cell.shape[0]
    surface_level = prior_state[:, 0].reshape(member_index, latitude_rows * grid_columns)
    observed = jnp.take(surface_level, obs_cell, axis=1)
    in_use = (jnp.arange(obs_slots, dtype=jnp.int32) < obs_count[0]).astype(jnp.float32)
    packed = jnp.concatenate([observed, obs_value[None], obs_error[None], in_use[None]], 0)
    widened = padded(packed, (("tile", 1),), obs_slots)
    everyone = lax.all_gather(widened[:member_index], "mem", axis=0, tiled=True)
    locality = jnp.concatenate(
        [
            jnp.full((obs_slots,), 0.5, jnp.float32),
            jnp.ones((obs_slots,), jnp.float32),
            jnp.full((obs_slots,), 0.5, jnp.float32),
        ]
    )
    weights = coefficients(
        everyone,
        widened[member_index],
        widened[member_index + 1],
        widened[member_index + 2],
        locality,
    )
    flattened_state = prior_state.reshape(member_index, -1)
    group_start = lax.axis_index("mem") * member_index
    own_columns = lax.dynamic_slice_in_dim(weights, group_start, member_index, 1)
    analysis_change = jnp.zeros_like(flattened_state) + jnp.dot(
        own_columns.T,
        lax.all_gather(flattened_state, "mem", axis=0, tiled=True),
        precision=lax.Precision.HIGHEST,
    )
    return (flattened_state + analysis_change).reshape(prior_state.shape)


def solution(mesh):
    in_specs = (
        P("mem", None, None, "tile"),
        P(None, None, "tile"),
        P(None, None, "tile"),
        P(None, "tile"),
        P("tile"),
        P("tile"),
        P("tile"),
        P("tile"),
    )
    out_specs = P("mem", None, None, "tile")
    return jax.shard_map(local, mesh=mesh, in_specs=in_specs, out_specs=out_specs, check_vma=False)
```

profile of v0, /device:TPU:5, one launch (start us, length us, event | category | flops | bytes accessed | tf_op | source)
XLA Modules:
  0.0 265.4 jit_solution(17902989379323050687)
XLA Ops:
  6.5 0.8 convert_bitcast_fusion
  7.3 0.9 pad_maximum_fusion.3
  8.3 5.4 %collective-permute-start.2 = (f32[9,16,1]{2,1,0:T(8,128)S(1)}, f32[9,16,1]{2,1,0:T(8,128)S(1)}, u32[]{:S(2)}, u32[]{:S(2)}) collective-permute-start(f32[9,16,1]{2,1,0:T(8,128)S(1)} %get-tuple-element.35), channel_id=1, source_target_pairs={{0,8},{8,16},{16,24},{24,32},{32,40},{40,48},{48,56},{56,64},{64,7... | collective-permute-start | bytes 1736 | tf_op jit(solution)/shard_map/ppermute | solution.py:13
  13.7 2.1 collective-permute-start.3
  15.7 1.4 fusion.73
  17.1 5.1 %collective-permute-start = (f32[8,8,16,1]{3,2,1,0:T(8,128)S(1)}, f32[8,8,16,1]{3,2,1,0:T(8,128)S(1)}, u32[]{:S(2)}, u32[]{:S(2)}) collective-permute-start(f32[8,8,16,1]{3,2,1,0:T(8,128)S(1)} %get-tuple-element.31), channel_id=1, source_target_pairs={{0,8},{8,16},{16,24},{24,32},{32,40},{40,48},{48,56},{56,64},{64,7... | collective-permute-start | bytes 12296 | tf_op jit(solution)/shard_map/ppermute | solution.py:13
  22.3 7.4 %collective-permute-start.1 = (f32[8,8,16,1]{3,2,1,0:T(8,128)S(1)}, f32[8,8,16,1]{3,2,1,0:T(8,128)S(1)}, u32[]{:S(2)}, u32[]{:S(2)}) collective-permute-start(f32[8,8,16,1]{3,2,1,0:T(8,128)S(1)} %get-tuple-element.32), channel_id=1, source_target_pairs={{8,0},{16,8},{24,16},{32,24},{40,32},{48,40},{56,48},{64,56},{72,6... | collective-permute-start | bytes 12296 | tf_op jit(solution)/shard_map/ppermute | solution.py:16
  30.3 9.6 %collective-permute-done.1 = f32[8,8,16,1]{3,2,1,0:T(8,128)S(1)} collective-permute-done((f32[8,8,16,1]{3,2,1,0:T(8,128)S(1)}, f32[8,8,16,1]{3,2,1,0:T(8,128)S(1)}, u32[]{:S(2)}, u32[]{:S(2)}) %collective-permute-start.1) | collective-permute-done | bytes 4128 | tf_op jit(solution)/shard_map/ppermute | solution.py:16
  39.9 0.6 pad_maximum_fusion
  40.5 0.6 fusion.72
  41.1 0.6 fusion.71
  41.7 0.3 slice.308
  42.0 1.6 fusion.9
  43.6 1.9 subtract_multiply_fusion.1
  45.5 1.1 fusion.7
  46.6 7.5 %copy.39 = f32[8,2,4,16,256]{3,0,2,1,4:T(8,128)} copy(f32[8,2,4,16,256]{4,0,3,2,1:T(8,128)S(1)} %fusion.7) | data formatting | bytes 2097152 | tf_op jit(solution)/shard_map/add | solution.py:50
  54.1 0.8 fusion.70
  54.9 1.9 collective-permute-start.4
  56.8 3.8 %collective-permute-start.5 = (f32[8,8,16,1]{2,0,1,3:T(8,128)S(1)}, f32[8,8,16,1]{2,0,1,3:T(8,128)S(1)}, u32[]{:S(2)}, u32[]{:S(2)}) collective-permute-start(f32[8,8,16,1]{2,0,1,3:T(8,128)S(1)} %get-tuple-element.26), channel_id=1, source_target_pairs={{8,0},{16,8},{24,16},{32,24},{40,32},{48,40},{56,48},{64,56},{72,6... | collective-permute-start | bytes 12296 | tf_op jit(solution)/shard_map/ppermute | solution.py:16
  60.7 0.5 copy.40
  61.2 2.4 collective-permute-done.5
  63.5 0.5 copy.41
  64.0 0.5 subtract_multiply_fusion
  64.6 1.4 fusion.3
  66.7 0.9 slice.328
  67.7 0.6 copy.51
  68.3 0.6 gather_fusion
  69.1 1.9 collective-permute-start.6
  71.0 6.0 %collective-permute-start.7 = (f32[11,128]{1,0:T(8,128)S(1)}, f32[11,128]{1,0:T(8,128)S(1)}, u32[]{:S(2)}, u32[]{:S(2)}) collective-permute-start(f32[11,128]{1,0:T(8,128)S(1)} %pad_maximum_fusion.16), channel_id=1, source_target_pairs={{8,0},{16,8},{24,16},{32,24},{40,32},{48,40},{56,48},{64,56},{72,6... | collective-permute-start | bytes 16904 | tf_op jit(solution)/shard_map/ppermute | solution.py:16
  77.1 0.8 collective-permute-done.7
  77.9 32.3 %all_gather.6 = f32[64,384]{1,0:T(8,128)S(1)} all-gather(f32[8,384]{1,0:T(8,128)S(1)} %slice.329), channel_id=1, replica_groups=mesh['tile'=64,'mem'=8] {'mem'}, dimensions={0}, use_global_device_ids=true | all-gather | bytes 110592 | tf_op jit(solution)/shard_map/all_gather | solution.py:88
  110.2 0.7 fusion.27
  110.9 0.2 copy.44
  111.4 11.7 %cholesky.76 = f32[128,128]{1,0:T(8,128)S(1)} custom-call(f32[128,128]{1,0:T(8,128)S(1)} %cholesky.189), custom_call_target="Cholesky" | custom-call | tf_op jit(solution)/shard_map/jit(cholesky)/cholesky | solution.py:62
  123.1 9.8 %custom-call.26 = f32[1,128,128]{1,2,0:T(8,128)S(1)} custom-call(f32[1,128,128]{2,1,0:T(8,128)S(1)} %get-tuple-element.43), custom_call_target="InvertDiagBlocksLowerTriangular" | custom-call | tf_op jit(solution)/shard_map/jit(cholesky)/cholesky | solution.py:62
  133.0 0.3 constant_dynamic-update-slice_fusion.2
  133.2 0.3 convolution_subtract_fusion
  133.5 11.7 %cholesky.160 = f32[128,128]{1,0:T(8,128)S(1)} custom-call(f32[128,128]{1,0:T(8,128)S(1)} %cholesky.193), custom_call_target="Cholesky" | custom-call | tf_op jit(solution)/shard_map/jit(cholesky)/cholesky | solution.py:62
  145.3 10.0 %custom-call.27 = f32[1,128,128]{1,2,0:T(8,128)S(1)} custom-call(f32[1,128,128]{2,1,0:T(8,128)S(1)} %get-tuple-element.40), custom_call_target="InvertDiagBlocksLowerTriangular" | custom-call | tf_op jit(solution)/shard_map/jit(cholesky)/cholesky | solution.py:62
  155.5 0.3 convolution_subtract_fusion.1
  155.8 11.7 %cholesky.179 = f32[128,128]{1,0:T(8,128)S(1)} custom-call(f32[128,128]{1,0:T(8,128)S(1)} %convolution_subtract_fusion.1), custom_call_target="Cholesky" | custom-call | tf_op jit(solution)/shard_map/jit(cholesky)/cholesky | solution.py:62
  167.5 0.7 compare_reduce_fusion.1
  169.5 0.7 compare_reduce_fusion
  171.0 6.5 %while.1 = (s32[]{:T(128)}, f32[384,384]{1,0:T(8,128)S(1)}, s32[3,2]{0,1:T(2,128)S(1)}, f32[3,128,128]{2,1,0:T(8,128)S(1)}, s32[]{:T(128)}) while((s32[]{:T(128)}, f32[384,384]{1,0:T(8,128)S(1)}, s32[3,2]{0,1:T(2,128)S(1)}, f32[3,128,128]{2,1,0:T(8,128)S(1)}, s32[]{:T(128)}) %tuple.32), condition=%wide.while_cond, body=%wide.while_body.sunk | while | flops 2 | bytes 131181 | solution.py:64
  171.3 0.6 fusion.85
  171.9 1.4 bitcast_dynamic-update-slice_fusion.2
  173.4 0.6 fusion.85
  174.0 1.4 bitcast_dynamic-update-slice_fusion.2
  175.5 0.6 fusion.85
  176.1 1.4 bitcast_dynamic-update-slice_fusion.2
  177.5 29.5 %custom-call.28 = f32[3,128,128]{1,2,0:T(8,128)S(1)} custom-call(f32[3,128,128]{2,1,0:T(8,128)S(1)} %get-tuple-element.12), custom_call_target="InvertDiagBlocksLowerTriangular" | custom-call | tf_op jit(solution)/shard_map/jit(_cho_solve)/triangular_solve | solution.py:64
  207.2 0.3 convolution_subtract_fusion.5
  207.5 0.2 fusion.43
  207.7 0.3 convolution_subtract_fusion.4
  208.0 0.2 fusion.45
  208.2 0.3 fusion.44
  208.4 0.2 convolution_subtract_fusion.3
  208.7 0.3 fusion.42
  208.9 0.2 convolution_subtract_fusion.2
  209.2 0.3 fusion.40
  209.4 0.3 fusion.17
  209.9 40.8 %all-gather.2.cloned.1.call-done = f32[64,32768]{1,0:T(8,128)} async-done(((f32[8,32768]{1,0:T(8,128)}), f32[64,32768]{1,0:T(8,128)}) %all-gather.2.cloned.1.call-update) | async-done | bytes 8388624 | tf_op jit(solution)/shard_map/all_gather | solution.py:108
  250.7 6.5 %convolution_add_fusion = f32[8,32768]{1,0:T(8,128)S(1)} fusion(f32[8,32768]{1,0:T(8,128)S(1)} %bitcast.82, f32[64,32768]{1,0:T(8,128)} %all-gather.2.cloned.1.call-done, f32[64,64]{1,0:T(8,128)S(1)} %slice.331, s32[]{:T(128)S(6)} %select_n.29, f32[64]{0:T(128)S(1)} %slice_reduce_fusion), kind=kOutput, calls=%fused_computation.3 | convolution fusion | flops 201589760 | bytes 10502404 | tf_op jit(solution)/shard_map/dot_general | solution.py:106
  257.2 1.3 copy.45
  (65 shorter events, 2.3 us)
Async XLA Ops:
  6.5 23.2 %copy-start.3 = (f32[4,16,256]{2,1,0:T(8,128)S(1)}, f32[4,16,256]{2,1,0:T(8,128)}, u32[]{:S(2)}) copy-start(f32[4,16,256]{2,1,0:T(8,128)} %param.10) | copy-start | bytes 196612
  6.5 23.2 %copy-start.2 = (f32[4,16,256]{2,1,0:T(8,128)S(1)}, f32[4,16,256]{2,1,0:T(8,128)}, u32[]{:S(2)}) copy-start(f32[4,16,256]{2,1,0:T(8,128)} %param.9) | copy-start | bytes 196612
  6.5 244.1 %all-gather.2.cloned.1.call-start = ((), (), s32[]{:S(2)}) async-start(), calls=%async_computation | async-start | bytes 9437184 | tf_op jit(solution)/shard_map/all_gather | solution.py:108
  8.3 21.5 %collective-permute-start.2 = (f32[9,16,1]{2,1,0:T(8,128)S(1)}, f32[9,16,1]{2,1,0:T(8,128)S(1)}, u32[]{:S(2)}, u32[]{:S(2)}) collective-permute-start(f32[9,16,1]{2,1,0:T(8,128)S(1)} %get-tuple-element.35), channel_id=1, source_target_pairs={{0,8},{8,16},{16,24},{24,32},{32,40},{40,48},{48,56},{56,64},{64,7... | collective-permute-start | bytes 1736 | tf_op jit(solution)/shard_map/ppermute | solution.py:13
  13.7 26.3 %copy-start.1 = (f32[8,8,16,256]{3,2,1,0:T(8,128)S(1)}, f32[8,8,16,256]{3,2,1,0:T(8,128)}, u32[]{:S(2)}) copy-start(f32[8,8,16,256]{3,2,1,0:T(8,128)} %param.8) | copy-start | bytes 3145732
  13.7 16.1 %collective-permute-start.3 = (f32[9,16,1]{2,1,0:T(8,128)S(1)}, f32[9,16,1]{2,1,0:T(8,128)S(1)}, u32[]{:S(2)}, u32[]{:S(2)}) collective-permute-start(f32[9,16,1]{2,1,0:T(8,128)S(1)} %get-tuple-element.36), channel_id=1, source_target_pairs={{8,0},{16,8},{24,16},{32,24},{40,32},{48,40},{56,48},{64,56},{72,6... | collective-permute-start | bytes 1736 | tf_op jit(solution)/shard_map/ppermute | solution.py:16
  17.1 13.2 %collective-permute-start = (f32[8,8,16,1]{3,2,1,0:T(8,128)S(1)}, f32[8,8,16,1]{3,2,1,0:T(8,128)S(1)}, u32[]{:S(2)}, u32[]{:S(2)}) collective-permute-start(f32[8,8,16,1]{3,2,1,0:T(8,128)S(1)} %get-tuple-element.31), channel_id=1, source_target_pairs={{0,8},{8,16},{16,24},{24,32},{32,40},{40,48},{48,56},{56,64},{64,7... | collective-permute-start | bytes 12296 | tf_op jit(solution)/shard_map/ppermute | solution.py:13
  22.3 17.6 %collective-permute-start.1 = (f32[8,8,16,1]{3,2,1,0:T(8,128)S(1)}, f32[8,8,16,1]{3,2,1,0:T(8,128)S(1)}, u32[]{:S(2)}, u32[]{:S(2)}) collective-permute-start(f32[8,8,16,1]{3,2,1,0:T(8,128)S(1)} %get-tuple-element.32), channel_id=1, source_target_pairs={{8,0},{16,8},{24,16},{32,24},{40,32},{48,40},{56,48},{64,56},{72,6... | collective-permute-start | bytes 12296 | tf_op jit(solution)/shard_map/ppermute | solution.py:16
  54.9 5.8 %collective-permute-start.4 = (f32[8,8,16,1]{2,0,1,3:T(8,128)S(1)}, f32[8,8,16,1]{2,0,1,3:T(8,128)S(1)}, u32[]{:S(2)}, u32[]{:S(2)}) collective-permute-start(f32[8,8,16,1]{2,0,1,3:T(8,128)S(1)} %get-tuple-element.25), channel_id=1, source_target_pairs={{0,8},{8,16},{16,24},{24,32},{32,40},{40,48},{48,56},{56,64},{64,7... | collective-permute-start | bytes 12296 | tf_op jit(solution)/shard_map/ppermute | solution.py:13
  56.8 6.7 %collective-permute-start.5 = (f32[8,8,16,1]{2,0,1,3:T(8,128)S(1)}, f32[8,8,16,1]{2,0,1,3:T(8,128)S(1)}, u32[]{:S(2)}, u32[]{:S(2)}) collective-permute-start(f32[8,8,16,1]{2,0,1,3:T(8,128)S(1)} %get-tuple-element.26), channel_id=1, source_target_pairs={{8,0},{16,8},{24,16},{32,24},{40,32},{48,40},{56,48},{64,56},{72,6... | collective-permute-start | bytes 12296 | tf_op jit(solution)/shard_map/ppermute | solution.py:16
  64.5 2.1 copy-start.7
  66.0 3.1 %copy-start.4 = (f32[128]{0:T(128)S(1)}, f32[128]{0:T(128)}, u32[]{:S(2)}) copy-start(f32[128]{0:T(128)} %param.15) | copy-start | bytes 1540
  66.0 3.1 %copy-start.5 = (f32[128]{0:T(128)S(1)}, f32[128]{0:T(128)}, u32[]{:S(2)}) copy-start(f32[128]{0:T(128)} %param.14) | copy-start | bytes 1540
  68.3 42.9 %copy-start.6 = (f32[1,384]{1,0:T(1,128)S(1)}, f32[1,384]{1,0:T(1,128)}, u32[]{:S(2)}) copy-start(f32[1,384]{1,0:T(1,128)} %constant.158.clone.1) | copy-start | bytes 4612
  69.1 8.0 %collective-permute-start.6 = (f32[11,128]{1,0:T(8,128)S(1)}, f32[11,128]{1,0:T(8,128)S(1)}, u32[]{:S(2)}, u32[]{:S(2)}) collective-permute-start(f32[11,128]{1,0:T(8,128)S(1)} %pad_maximum_fusion.16), channel_id=1, source_target_pairs={{0,8},{8,16},{16,24},{24,32},{32,40},{40,48},{48,56},{56,64},{64,7... | collective-permute-start | bytes 16904 | tf_op jit(solution)/shard_map/ppermute | solution.py:13
  71.0 6.9 %collective-permute-start.7 = (f32[11,128]{1,0:T(8,128)S(1)}, f32[11,128]{1,0:T(8,128)S(1)}, u32[]{:S(2)}, u32[]{:S(2)}) collective-permute-start(f32[11,128]{1,0:T(8,128)S(1)} %pad_maximum_fusion.16), channel_id=1, source_target_pairs={{8,0},{16,8},{24,16},{32,24},{40,32},{48,40},{56,48},{64,56},{72,6... | collective-permute-start | bytes 16904 | tf_op jit(solution)/shard_map/ppermute | solution.py:16
  171.0 79.7 %copy-start = (f32[8,2,4,16,256]{4,0,3,2,1:T(8,128)S(1)}, f32[8,2,4,16,256]{4,0,3,2,1:T(8,128)}, u32[]{:S(2)}) copy-start(f32[8,2,4,16,256]{4,0,3,2,1:T(8,128)} %fusion.3) | copy-start | bytes 3145732
Sparse Core Ops, SparseCore 0:
  66.1 184.5 all-gather.1
where the time goes:
time: 266 us; the launch traced here: 265 us
  other arithmetic  95.7 us (36%)
  waiting for transfers between devices  53.6 us (20%)
  starting transfers between devices  33.7 us (13%)
  blocking collectives  32.3 us (12%)
  local copies, waits for them, and re-layouts  22.4 us (8%)
  between operations  16.6 us (6%)
  matrix products  10.9 us (4%)
    another operation x10, other arithmetic, coefficients(): factor = jnp.linalg.cholesky(system)  56.4 us
    all_gather x1, waiting for transfers between devices, local(): lax.all_gather(flattened_state, 'mem', axis=0, tiled=True)  40.8 us
    all_gather x1, blocking collectives, local(): everyone = lax.all_gather(widened[:member_index], 'mem', axis=0, tiled=True)  32.3 us
    another operation x3, other arithmetic, coefficients(): solved = jax.scipy.linalg.cho_solve((factor, True), right_sides)  29.5 us
    ppermute x4, starting transfers between devices, padded(): lax.ppermute(lax.slice_in_dim(block, 0, width, axis=dim), axis, backward)  19.3 us
    ppermute x4, starting transfers between devices, padded(): lax.ppermute(lax.slice_in_dim(block, block.shape[dim] - width, None, axis...  14.4 us
    ppermute x4, waiting for transfers between devices, padded(): lax.ppermute(lax.slice_in_dim(block, 0, width, axis=dim), axis, backward)  12.7 us
    add x1, local copies, waits for them, and re-layouts, advect_tracers(): updated = middle + inner_wet * change  7.51 us
  transfers between devices with their start and end apart: 9, of which 4 were waited for; matrix products, arithmetic and copies ran while one was open for 38% of the time, Pallas kernels for 0%

commit v1 on v0

v1 whole, which is shorter than its diff:
```python
import jax
import jax.numpy as jnp
from jax import lax
from jax.experimental import pallas as pl
from jax.experimental.pallas import tpu as pltpu
from jax.sharding import PartitionSpec as P

LEVELS = 4
PLANES = 8
MEMBERS = 8
ENSEMBLE = 64
ROWS = 16
COLUMNS = 256
SLOTS = 128
LANES = 128
HALF_ROWS = ROWS * MEMBERS
CELL_ROWS = 2 * HALF_ROWS
CHUNK_ROWS = CELL_ROWS + MEMBERS
SYSTEM_ROWS = ENSEMBLE + 8
HIGHEST = lax.Precision.HIGHEST
PARAMS = pltpu.CompilerParams(vmem_limit_bytes=32 * 1024 * 1024)


def lane_index(shape):
    return lax.broadcasted_iota(jnp.int32, shape, 1)


def pack_edges(state, diffusivity, velocity, wet, first, last):
    pair = lane_index((ROWS, LANES)) >> 1

    def put(low, high, index, kept):
        first_kept, last_kept = kept
        first_kept = jnp.where(pair == index, pltpu.roll(low, 2 * index, 1), first_kept)
        last_kept = jnp.where(
            pair == index, pltpu.roll(high, (2 * index + 2) % LANES, 1), last_kept
        )
        return first_kept, last_kept

    zeros = jnp.zeros((ROWS, LANES), jnp.float32)

    def member(e, kept):
        for q in range(PLANES):
            kept = put(state[e, q, :, :LANES], state[e, q, :, LANES:], e * PLANES + q, kept)
        return kept

    kept = lax.fori_loop(0, MEMBERS, member, (zeros, zeros))
    first[:, :LANES], last[:, :LANES] = kept
    kept = (zeros, zeros)
    for level in range(LEVELS):
        kept = put(diffusivity[level, :, :LANES], diffusivity[level, :, LANES:], level, kept)
        kept = put(velocity[level, :, :LANES], velocity[level, :, LANES:], LEVELS + level, kept)
    flags = wet[...].astype(jnp.float32)
    kept = put(flags[:, :LANES], flags[:, LANES:], 2 * LEVELS, kept)
    first[:, LANES:], last[:, LANES:] = kept


def from_west(tiles):
    lane = lane_index((ROWS, LANES))
    turned = [pltpu.roll(tile, 1, 1) for tile in tiles]
    return [jnp.where(lane == 0, turned[i - 1], turned[i]) for i in range(3)]


def from_east(tiles):
    lane = lane_index((ROWS, LANES))
    turned = [pltpu.roll(tile, LANES - 1, 1) for tile in tiles]
    return [jnp.where(lane == LANES - 1, turned[(i + 1) % 3], turned[i]) for i in range(3)]


def halo_tile(west, east, index):
    lane = lane_index((ROWS, LANES))
    east = pltpu.roll(east, (LANES - 2 * index) % LANES, 1)
    west = pltpu.roll(west, LANES - 2 - 2 * index, 1)
    return jnp.where(lane < 2, east, jnp.where(lane >= LANES - 2, west, 0.0))


def transport(
    state, diffusivity, velocity, wet, west_halo, east_halo, obs_cell, chunks
):
    row = lax.broadcasted_iota(jnp.int32, (ROWS, LANES), 0)
    flags = wet[...].astype(jnp.float32)

    def widened(block, index, lanes):
        return [
            block[:, :LANES],
            block[:, LANES:],
            halo_tile(west_halo[:, lanes], east_halo[:, lanes], index),
        ]

    tracer_lanes, static_lanes = slice(0, LANES), slice(LANES, 2 * LANES)
    ocean = widened(flags, 2 * LEVELS, static_lanes)
    ocean_west = from_west(ocean)
    ocean_south = [pltpu.roll(x, ROWS - 1, 0) for x in ocean]

    def level_step(level, carry):
        diffuse = widened(diffusivity[level], level, static_lanes)
        speed = widened(velocity[level], LEVELS + level, static_lanes)
        diffuse_west, speed_west = from_west(diffuse), from_west(speed)
        face_west, face_east, north = [], [], []
        for i in range(3):
            face = ocean_west[i] * ocean[i]
            a = 0.5 * (speed_west[i] + speed[i])
            k = 0.5 * (diffuse_west[i] + diffuse[i])
            face_west.append(face * (jnp.maximum(a, 0.0) + k))
            face_east.append(face * (jnp.minimum(a, 0.0) - k))
            k = 0.5 * (diffuse[i] + pltpu.roll(diffuse[i], ROWS - 1, 0))
            north.append(jnp.where(row < ROWS - 1, ocean[i] * ocean_south[i] * k, 0.0))
        next_west, next_east = from_east(face_west), from_east(face_east)
        above = [pltpu.roll(x, 1, 0) for x in north]
        centre = [
            1.0 + (face_east[i] - next_west[i] - above[i] - north[i]) * ocean[i]
            for i in range(3)
        ]

        def advance(tiles, count):
            west, east = from_west(tiles), from_east(tiles)
            return [
                centre[i] * tiles[i]
                + face_west[i] * west[i]
                - next_east[i] * east[i]
                + above[i] * pltpu.roll(tiles[i], 1, 0)
                + north[i] * pltpu.roll(tiles[i], ROWS - 1, 0)
                for i in range(count)
            ]

        def member_step(e, carry):
            for tracer in range(2):
                q = tracer * LEVELS + level
                tiles = widened(state[e, q], e * PLANES + q, tracer_lanes)
                done = advance(advance(tiles, 3), 2)
                for half in range(2):
                    rows = pl.ds(half * HALF_ROWS + e, ROWS, stride=MEMBERS)
                    chunks[q, rows, :] = done[half]
            return carry

        return lax.fori_loop(0, MEMBERS, member_step, carry)

    lax.fori_loop(0, LEVELS, level_step, 0)
    cell = obs_cell[...]
    column = lax.broadcasted_iota(jnp.int32, (COLUMNS, SLOTS), 0)
    pick = (column == (cell & (COLUMNS - 1))).astype(jnp.float32)
    surface = jnp.concatenate([chunks[0, :HALF_ROWS, :], chunks[0, HALF_ROWS:CELL_ROWS, :]], 1)
    near = jnp.dot(
        surface, pick, precision=HIGHEST, preferred_element_type=jnp.float32
    ).reshape(ROWS, MEMBERS, SLOTS)
    layer = lax.broadcasted_iota(jnp.int32, (ROWS, MEMBERS, SLOTS), 0)
    observed = jnp.sum(jnp.where(layer == (cell >> 8)[None], near, 0.0), 0)
    for q in range(PLANES):
        chunks[q, CELL_ROWS:, :] = observed


def block_system(observed, obs_count, obs_value, obs_error, out):
    members = observed[...].reshape(ENSEMBLE, SLOTS)
    slot = lane_index((1, SLOTS))
    in_use = (slot < obs_count[0]).astype(jnp.float32)
    mean = jnp.sum(members, 0, keepdims=True) / ENSEMBLE
    anomaly = (members - mean) * in_use
    innovation = (obs_value[...] - mean) * in_use
    scaled = anomaly / ((ENSEMBLE - 1) * obs_error[...])
    first = lax.broadcasted_iota(jnp.int32, (8, SLOTS), 0) == 0
    left = jnp.concatenate([anomaly, jnp.where(first, innovation, 0.0)], 0)
    right = jnp.concatenate([scaled, jnp.zeros((LANES - ENSEMBLE, SLOTS), jnp.float32)], 0)
    out[...] = lax.dot_general(
        left, right, (((1,), (1,)), ((), ())), precision=HIGHEST,
        preferred_element_type=jnp.float32,
    )


def inverse(system):
    row = lax.broadcasted_iota(jnp.int32, (SYSTEM_ROWS, LANES), 0)
    lane = lane_index((SYSTEM_ROWS, LANES))
    for k in range(ENSEMBLE):
        pivot_row = system[k : k + 1, :]
        scale = 1.0 / pivot_row[:, k : k + 1]
        scaled = jnp.where(lane[:1] == k, scale, pivot_row * scale)
        column = system[:, k : k + 1]
        rest = jnp.where(lane == k, 0.0, system)
        system = jnp.where(row == k, scaled, rest - column * scaled)
    return system


def update(own, west, east, received, out):
    row = lax.broadcasted_iota(jnp.int32, (SYSTEM_ROWS, LANES), 0)
    diagonal = row == lane_index((SYSTEM_ROWS, LANES))
    identity = jnp.where(diagonal & (row < ENSEMBLE), 1.0, 0.0)
    solved = inverse(identity + own[...] + 0.5 * (west[...] + east[...]))
    weights = 0.5 * (identity + solved)[:ENSEMBLE] - solved[ENSEMBLE : ENSEMBLE + 1]
    weights = weights[:, :ENSEMBLE]
    for r in range(ROWS):
        halves = [
            received[:, first : first + MEMBERS, :].reshape(ENSEMBLE, LANES)
            for first in (r * MEMBERS, HALF_ROWS + r * MEMBERS)
        ]
        result = jnp.dot(
            weights, jnp.concatenate(halves, 1), precision=HIGHEST,
            preferred_element_type=jnp.float32,
        )
        for m in range(ENSEMBLE // MEMBERS):
            rows = result[m * MEMBERS : (m + 1) * MEMBERS]
            out[m, pl.ds(r, MEMBERS, stride=ROWS), :] = rows[:, :LANES]
            out[m, pl.ds(HALF_ROWS + r, MEMBERS, stride=ROWS), :] = rows[:, LANES:]


def unpack(planes, out):
    for q in range(planes.shape[0]):
        out[:, q, :, :LANES] = planes[q, :HALF_ROWS, :].reshape(MEMBERS, ROWS, LANES)
        out[:, q, :, LANES:] = planes[q, HALF_ROWS:, :].reshape(MEMBERS, ROWS, LANES)


def vmem():
    return pl.BlockSpec(memory_space=pltpu.VMEM)


def shifted(value, step):
    count = lax.axis_size("tile")
    return lax.ppermute(value, "tile", [(i, (i + step) % count) for i in range(count)])


def local(
    member_tracer_state, diffusivity, velocity, wet_mask, obs_cell, obs_count, obs_value, obs_error
):
    edge = jax.ShapeDtypeStruct((ROWS, COLUMNS), jnp.float32)
    first, last = pl.pallas_call(
        pack_edges,
        out_shape=(edge, edge),
        in_specs=[vmem()] * 4,
        out_specs=(vmem(), vmem()),
        compiler_params=PARAMS,
        name="pack_edges",
    )(member_tracer_state, diffusivity, velocity, wet_mask)
    west_halo = shifted(last, 1)
    east_halo = shifted(first, -1)
    chunks = pl.pallas_call(
        transport,
        out_shape=jax.ShapeDtypeStruct((PLANES, CHUNK_ROWS, LANES), jnp.float32),
        in_specs=[vmem()] * 7,
        out_specs=vmem(),
        compiler_params=PARAMS,
        name="transport",
    )(
        member_tracer_state, diffusivity, velocity, wet_mask, west_halo, east_halo,
        obs_cell.reshape(1, SLOTS),
    )
    received = lax.all_to_all(chunks, "mem", split_axis=0, concat_axis=0, tiled=True)
    share = pl.pallas_call(
        block_system,
        out_shape=jax.ShapeDtypeStruct((SYSTEM_ROWS, LANES), jnp.float32),
        grid=(1,),
        in_specs=[
            pl.BlockSpec((PLANES, MEMBERS, SLOTS), lambda i: (0, CELL_ROWS // MEMBERS, 0)),
            pl.BlockSpec(memory_space=pltpu.SMEM),
            pl.BlockSpec((1, SLOTS), lambda i: (0, 0)),
            pl.BlockSpec((1, SLOTS), lambda i: (0, 0)),
        ],
        out_specs=pl.BlockSpec((SYSTEM_ROWS, LANES), lambda i: (0, 0)),
        compiler_params=PARAMS,
        name="block_system",
    )(received, obs_count, obs_value.reshape(1, SLOTS), obs_error.reshape(1, SLOTS))
    west_share = shifted(share, 1)
    east_share = shifted(share, -1)
    updated = pl.pallas_call(
        update,
        out_shape=jax.ShapeDtypeStruct((PLANES, CELL_ROWS, LANES), jnp.float32),
        in_specs=[vmem()] * 4,
        out_specs=vmem(),
        compiler_params=PARAMS,
        name="update",
    )(share, west_share, east_share, received)
    back = lax.all_to_all(updated, "mem", split_axis=0, concat_axis=0, tiled=True)
    return pl.pallas_call(
        unpack,
        out_shape=jax.ShapeDtypeStruct(member_tracer_state.shape, jnp.float32),
        grid=(2,),
        in_specs=[pl.BlockSpec((PLANES // 2, CELL_ROWS, LANES), lambda i: (i, 0, 0))],
        out_specs=pl.BlockSpec(
            (MEMBERS, PLANES // 2, ROWS, COLUMNS), lambda i: (0, i, 0, 0)
        ),
        compiler_params=PARAMS,
        name="unpack",
    )(back)


def solution(mesh):
    in_specs = (
        P("mem", None, None, "tile"),
        P(None, None, "tile"),
        P(None, None, "tile"),
        P(None, "tile"),
        P("tile"),
        P("tile"),
        P("tile"),
        P("tile"),
    )
    out_specs = P("mem", None, None, "tile")
    return jax.shard_map(local, mesh=mesh, in_specs=in_specs, out_specs=out_specs, check_vma=False)
```

time: 266 us -> 90.9 us (0.34)
  the two profiles are of different devices: /device:TPU:5 before, /device:TPU:8 now
where the time goes in v1:
time: 90.9 us; the launch traced here: 90.4 us
  starting transfers between devices  34.4 us (38%)
  Pallas kernels  19.1 us (21%)
  waiting for transfers between devices  18.5 us (20%)
  blocking collectives  14 us (15%)
  local copies, waits for them, and re-layouts  3.63 us (4%)
    ppermute x4, starting transfers between devices, shifted(): lax.ppermute(value, 'tile', [(i, (i + step) % count) for i in range(count)])  28.5 us
    all_to_all x1, blocking collectives, local(): lax.all_to_all(updated, 'mem', split_axis=0, concat_axis=0, tiled=True)  14 us
    pallas_call x1, Pallas kernels, local(): pl.pallas_call(transport, out_shape=jax.ShapeDtypeStruct((PLANES, CHUNK_R...  10.3 us
    all_to_all x1, waiting for transfers between devices, local(): lax.all_to_all(chunks, 'mem', split_axis=0, concat_axis=0, tiled=True)  10.1 us
    ppermute x4, waiting for transfers between devices, shifted(): lax.ppermute(value, 'tile', [(i, (i + step) % count) for i in range(count)])  8.37 us
    pallas_call x1, Pallas kernels, local(): pl.pallas_call(update, out_shape=jax.ShapeDtypeStruct((PLANES, CELL_ROWS,...  6.67 us
    all_to_all x1, starting transfers between devices, local(): lax.all_to_all(chunks, 'mem', split_axis=0, concat_axis=0, tiled=True)  5.89 us
    unnamed x14, local copies, waits for them, and re-layouts  3.63 us
  transfers between devices with their start and end apart: 5, of which 3 were waited for; matrix products, arithmetic and copies ran while one was open for 0% of the time, Pallas kernels for 0%

profile of v1, /device:TPU:8, one launch (start us, length us, event | category | flops | bytes accessed | tf_op | source)
XLA Modules:
  0.0 90.4 jit_solution(14425140237598219178)
XLA Ops:
  0.0 0.0 copy-start
  0.0 1.2 %copy-done = f32[8,8,16,256]{3,2,1,0:T(8,128)S(1)} copy-done((f32[8,8,16,256]{3,2,1,0:T(8,128)S(1)}, f32[8,8,16,256]{3,2,1,0:T(8,128)}, u32[]{:S(2)}) %copy-start) | copy-done | bytes 1048600
  1.2 0.0 copy-start.1
  1.2 0.8 copy-done.1
  2.1 0.0 copy-start.2
  2.1 0.8 copy-done.2
  2.9 0.0 copy-start.3
  2.9 0.7 copy-done.3
  3.6 0.0 copy-start.4
  3.6 0.9 pack_edges.1
  4.5 1.9 %collective-permute-start = (f32[16,256]{1,0:T(8,128)S(1)}, f32[16,256]{1,0:T(8,128)S(1)}, u32[]{:S(2)}, u32[]{:S(2)}) collective-permute-start(f32[16,256]{1,0:T(8,128)S(1)} %get-tuple-element.7), channel_id=1, source_target_pairs={{0,8},{8,16},{16,24},{24,32},{32,40},{40,48},{48,56},{56,64},{64,7... | collective-permute-start | bytes 49160 | tf_op jit(solution)/shard_map/ppermute | solution.py:215
  6.5 12.6 %collective-permute-start.1 = (f32[16,256]{1,0:T(8,128)S(1)}, f32[16,256]{1,0:T(8,128)S(1)}, u32[]{:S(2)}, u32[]{:S(2)}) collective-permute-start(f32[16,256]{1,0:T(8,128)S(1)} %get-tuple-element.8), channel_id=1, source_target_pairs={{0,504},{8,0},{16,8},{24,16},{32,24},{40,32},{48,40},{56,48},{64,5... | collective-permute-start | bytes 49160 | tf_op jit(solution)/shard_map/ppermute | solution.py:215
  19.0 0.0 collective-permute-done.west_halo
  19.1 1.4 %collective-permute-done.1.east_halo = f32[16,256]{1,0:T(8,128)S(1)} collective-permute-done((f32[16,256]{1,0:T(8,128)S(1)}, f32[16,256]{1,0:T(8,128)S(1)}, u32[]{:S(2)}, u32[]{:S(2)}) %collective-permute-start.1) | collective-permute-done | bytes 16416 | tf_op jit(solution)/shard_map/ppermute | solution.py:215
  20.5 0.0 copy-done.4
  20.5 10.3 %transport.1 = f32[8,264,128]{2,1,0:T(8,128)} custom-call(f32[8,8,16,256]{3,2,1,0:T(8,128)S(1)} %copy-done, f32[4,16,256]{2,1,0:T(8,128)S(1)} %copy-done.1, f32[4,16,256]{2,1,0:T(8,128)S(1)} %copy-done.2, s32[16,256]{1,0:T(8,128)S(1)} %copy-done.3, f32[16,256]{1,0:T(8,128)S(1)} %collective-permute-done.west_halo, ...), custom_call_target="tpu_custom_call" | custom-call | tf_op jit(solution)/shard_map/transport/pallas_call | solution.py:232
  30.8 0.0 copy-start.5
  30.8 0.0 copy-start.6
  30.8 5.9 %all-to-all-start = ((f32[8,264,128]{2,1,0:T(8,128)}), f32[8,264,128]{2,1,0:T(8,128)S(1)}, u32[]{:S(2)}, u32[]{:S(2)}) async-start(f32[8,264,128]{2,1,0:T(8,128)} %transport.1), calls=%async_computation | async-start | bytes 2162688 | tf_op jit(solution)/shard_map/all_to_all | solution.py:243
  37.3 10.1 %all-to-all-done.observed.received = f32[8,264,128]{2,1,0:T(8,128)S(1)} async-done(((f32[8,264,128]{2,1,0:T(8,128)}), f32[8,264,128]{2,1,0:T(8,128)S(1)}, u32[]{:S(2)}, u32[]{:S(2)}) %all-to-all-start) | async-done | bytes 1081376 | tf_op jit(solution)/shard_map/all_to_all | solution.py:243
  47.4 0.0 copy-done.5
  47.5 0.0 copy-done.6
  47.5 0.2 block_system.1.own
  47.7 12.1 %collective-permute-start.3 = (f32[72,128]{1,0:T(8,128)S(1)}, f32[72,128]{1,0:T(8,128)S(1)}, u32[]{:S(2)}, u32[]{:S(2)}) collective-permute-start(f32[72,128]{1,0:T(8,128)S(1)} %block_system.1.own), channel_id=1, source_target_pairs={{0,504},{8,0},{16,8},{24,16},{32,24},{40,32},{48,40},{56,48},{64,5... | collective-permute-start | bytes 110600 | tf_op jit(solution)/shard_map/ppermute | solution.py:215
  59.8 1.9 %collective-permute-start.2 = (f32[72,128]{1,0:T(8,128)S(1)}, f32[72,128]{1,0:T(8,128)S(1)}, u32[]{:S(2)}, u32[]{:S(2)}) collective-permute-start(f32[72,128]{1,0:T(8,128)S(1)} %block_system.1.own), channel_id=1, source_target_pairs={{0,8},{8,16},{16,24},{24,32},{32,40},{40,48},{48,56},{56,64},{64,7... | collective-permute-start | bytes 110600 | tf_op jit(solution)/shard_map/ppermute | solution.py:215
  61.7 0.0 collective-permute-done.3.east
  61.7 7.0 %collective-permute-done.2.west = f32[72,128]{1,0:T(8,128)S(1)} collective-permute-done((f32[72,128]{1,0:T(8,128)S(1)}, f32[72,128]{1,0:T(8,128)S(1)}, u32[]{:S(2)}, u32[]{:S(2)}) %collective-permute-start.2) | collective-permute-done | bytes 36896 | tf_op jit(solution)/shard_map/ppermute | solution.py:215
  68.7 6.7 %update.1 = f32[8,256,128]{2,1,0:T(8,128)S(1)} custom-call(f32[72,128]{1,0:T(8,128)S(1)} %block_system.1.own, f32[72,128]{1,0:T(8,128)S(1)} %collective-permute-done.2.west, f32[72,128]{1,0:T(8,128)S(1)} %collective-permute-done.3.east, f32[8,264,128]{2,1,0:T(8,128)S(1)} %all-to-all-done.observed.received), custom_call_target="tpu_custom_call" | custom-call | tf_op jit(solution)/shard_map/update/pallas_call | solution.py:260
  75.4 14.0 %all_to_all.10.planes = f32[8,256,128]{2,1,0:T(8,128)S(1)} all-to-all(f32[8,256,128]{2,1,0:T(8,128)S(1)} %update.1), channel_id=1, replica_groups=mesh['tile'=64,'mem'=8] {'mem'}, dimensions={0} | all-to-all | bytes 2097152 | tf_op jit(solution)/shard_map/all_to_all | solution.py:268
  89.4 1.0 %unpack.1 = f32[8,8,16,256]{3,2,1,0:T(8,128)} custom-call(f32[8,256,128]{2,1,0:T(8,128)S(1)} %all_to_all.10.planes), custom_call_target="tpu_custom_call" | custom-call | tf_op jit(solution)/shard_map/unpack/pallas_call | solution.py:269
Async XLA Ops:
  0.0 1.2 %copy-start = (f32[8,8,16,256]{3,2,1,0:T(8,128)S(1)}, f32[8,8,16,256]{3,2,1,0:T(8,128)}, u32[]{:S(2)}) copy-start(f32[8,8,16,256]{3,2,1,0:T(8,128)} %state.3) | copy-start | bytes 3145732
  1.2 0.8 copy-start.1
  2.1 0.8 copy-start.2
  2.9 0.7 copy-start.3
  3.6 16.8 %copy-start.4 = (s32[128]{0:T(128)S(1)}, s32[128]{0:T(128)}, u32[]{:S(2)}) copy-start(s32[128]{0:T(128)} %param.12) | copy-start | bytes 1540
  4.5 14.5 %collective-permute-start = (f32[16,256]{1,0:T(8,128)S(1)}, f32[16,256]{1,0:T(8,128)S(1)}, u32[]{:S(2)}, u32[]{:S(2)}) collective-permute-start(f32[16,256]{1,0:T(8,128)S(1)} %get-tuple-element.7), channel_id=1, source_target_pairs={{0,8},{8,16},{16,24},{24,32},{32,40},{40,48},{48,56},{56,64},{64,7... | collective-permute-start | bytes 49160 | tf_op jit(solution)/shard_map/ppermute | solution.py:215
  6.5 14.0 %collective-permute-start.1 = (f32[16,256]{1,0:T(8,128)S(1)}, f32[16,256]{1,0:T(8,128)S(1)}, u32[]{:S(2)}, u32[]{:S(2)}) collective-permute-start(f32[16,256]{1,0:T(8,128)S(1)} %get-tuple-element.8), channel_id=1, source_target_pairs={{0,504},{8,0},{16,8},{24,16},{32,24},{40,32},{48,40},{56,48},{64,5... | collective-permute-start | bytes 49160 | tf_op jit(solution)/shard_map/ppermute | solution.py:215
  30.8 16.7 %copy-start.5 = (f32[128]{0:T(128)S(1)}, f32[128]{0:T(128)}, u32[]{:S(2)}) copy-start(f32[128]{0:T(128)} %param.14) | copy-start | bytes 1540
  30.8 16.7 %copy-start.6 = (f32[128]{0:T(128)S(1)}, f32[128]{0:T(128)}, u32[]{:S(2)}) copy-start(f32[128]{0:T(128)} %param.15) | copy-start | bytes 1540
  30.8 16.7 %all-to-all-start = ((f32[8,264,128]{2,1,0:T(8,128)}), f32[8,264,128]{2,1,0:T(8,128)S(1)}, u32[]{:S(2)}, u32[]{:S(2)}) async-start(f32[8,264,128]{2,1,0:T(8,128)} %transport.1), calls=%async_computation | async-start | bytes 2162688 | tf_op jit(solution)/shard_map/all_to_all | solution.py:243
  47.7 14.1 %collective-permute-start.3 = (f32[72,128]{1,0:T(8,128)S(1)}, f32[72,128]{1,0:T(8,128)S(1)}, u32[]{:S(2)}, u32[]{:S(2)}) collective-permute-start(f32[72,128]{1,0:T(8,128)S(1)} %block_system.1.own), channel_id=1, source_target_pairs={{0,504},{8,0},{16,8},{24,16},{32,24},{40,32},{48,40},{56,48},{64,5... | collective-permute-start | bytes 110600 | tf_op jit(solution)/shard_map/ppermute | solution.py:215
  59.8 8.9 %collective-permute-start.2 = (f32[72,128]{1,0:T(8,128)S(1)}, f32[72,128]{1,0:T(8,128)S(1)}, u32[]{:S(2)}, u32[]{:S(2)}) collective-permute-start(f32[72,128]{1,0:T(8,128)S(1)} %block_system.1.own), channel_id=1, source_target_pairs={{0,8},{8,16},{16,24},{24,32},{32,40},{40,48},{48,56},{56,64},{64,7... | collective-permute-start | bytes 110600 | tf_op jit(solution)/shard_map/ppermute | solution.py:215

commit v2 on v1

v2 whole, which is shorter than its diff:
```python
import jax
import jax.numpy as jnp
from jax import lax
from jax.experimental import pallas as pl
from jax.experimental.pallas import tpu as pltpu
from jax.sharding import PartitionSpec as P

LEVELS = 4
PLANES = 8
MEMBERS = 8
ENSEMBLE = 64
ROWS = 16
COLUMNS = 256
SLOTS = 128
LANES = 128
HALF_ROWS = ROWS * MEMBERS
CELL_ROWS = 2 * HALF_ROWS
SYSTEM_ROWS = ENSEMBLE + 8
HIGHEST = lax.Precision.HIGHEST
PARAMS = pltpu.CompilerParams(vmem_limit_bytes=32 * 1024 * 1024)


def lane_index(shape):
    return lax.broadcasted_iota(jnp.int32, shape, 1)


def pack_edges(
    state, diffusivity, velocity, wet, first, last, own_state, own_statics, own_wet, arrived
):
    copies = [
        pltpu.make_async_copy(diffusivity, own_statics.at[:LEVELS], arrived.at[0]),
        pltpu.make_async_copy(velocity, own_statics.at[LEVELS:], arrived.at[1]),
        pltpu.make_async_copy(wet, own_wet, arrived.at[2]),
    ]
    for part in range(2):
        rows = slice(part * MEMBERS // 2, (part + 1) * MEMBERS // 2)
        copies.append(
            pltpu.make_async_copy(state.at[rows], own_state.at[rows], arrived.at[3 + part])
        )
    for copy in copies:
        copy.start()
    pair = lane_index((ROWS, LANES)) >> 1

    def put(low, high, index, kept):
        first_kept, last_kept = kept
        first_kept = jnp.where(pair == index, pltpu.roll(low, 2 * index, 1), first_kept)
        last_kept = jnp.where(
            pair == index, pltpu.roll(high, (2 * index + 2) % LANES, 1), last_kept
        )
        return first_kept, last_kept

    zeros = jnp.zeros((ROWS, LANES), jnp.float32)
    kept = (zeros, zeros)
    for copy in copies[:3]:
        copy.wait()
    for i in range(2 * LEVELS):
        kept = put(own_statics[i, :, :LANES], own_statics[i, :, LANES:], i, kept)
    flags = own_wet[...].astype(jnp.float32)
    kept = put(flags[:, :LANES], flags[:, LANES:], 2 * LEVELS, kept)
    first[:, LANES:], last[:, LANES:] = kept

    def member(e, kept):
        for q in range(PLANES):
            low, high = own_state[e, q, :, :LANES], own_state[e, q, :, LANES:]
            kept = put(low, high, e * PLANES + q, kept)
        return kept

    kept = (zeros, zeros)
    for part in range(2):
        copies[3 + part].wait()
        kept = lax.fori_loop(part * MEMBERS // 2, (part + 1) * MEMBERS // 2, member, kept)
    first[:, :LANES], last[:, :LANES] = kept


def from_west(tiles):
    lane = lane_index((ROWS, LANES))
    turned = [pltpu.roll(tile, 1, 1) for tile in tiles]
    return [jnp.where(lane == 0, turned[i - 1], turned[i]) for i in range(3)]


def from_east(tiles):
    lane = lane_index((ROWS, LANES))
    turned = [pltpu.roll(tile, LANES - 1, 1) for tile in tiles]
    return [jnp.where(lane == LANES - 1, turned[(i + 1) % 3], turned[i]) for i in range(3)]


def halo_tile(west, east, index):
    lane = lane_index((ROWS, LANES))
    east = pltpu.roll(east, (LANES - 2 * index) % LANES, 1)
    west = pltpu.roll(west, LANES - 2 - 2 * index, 1)
    return jnp.where(lane < 2, east, jnp.where(lane >= LANES - 2, west, 0.0))


TRACER_LANES, STATIC_LANES = slice(0, LANES), slice(LANES, 2 * LANES)


def widened(block, west_halo, east_halo, lanes, index):
    halo = halo_tile(west_halo[:, lanes], east_halo[:, lanes], index)
    return [block[:, :LANES], block[:, LANES:], halo]


def stepper(level, statics, wet, west_halo, east_halo):
    row = lax.broadcasted_iota(jnp.int32, (ROWS, LANES), 0)
    halos = (west_halo, east_halo, STATIC_LANES)
    ocean = widened(wet[...].astype(jnp.float32), *halos, 2 * LEVELS)
    diffuse = widened(statics[level], *halos, level)
    speed = widened(statics[LEVELS + level], *halos, LEVELS + level)
    ocean_west, diffuse_west, speed_west = map(from_west, (ocean, diffuse, speed))
    face_west, face_east, north = [], [], []
    for i in range(3):
        face = ocean_west[i] * ocean[i]
        a = 0.5 * (speed_west[i] + speed[i])
        k = 0.5 * (diffuse_west[i] + diffuse[i])
        face_west.append(face * (jnp.maximum(a, 0.0) + k))
        face_east.append(face * (jnp.minimum(a, 0.0) - k))
        k = 0.5 * (diffuse[i] + pltpu.roll(diffuse[i], ROWS - 1, 0))
        both = ocean[i] * pltpu.roll(ocean[i], ROWS - 1, 0)
        north.append(jnp.where(row < ROWS - 1, both * k, 0.0))
    next_west, next_east = from_east(face_west), from_east(face_east)
    above = [pltpu.roll(x, 1, 0) for x in north]
    centre = [
        1.0 + (face_east[i] - next_west[i] - above[i] - north[i]) * ocean[i] for i in range(3)
    ]

    def advance(tiles, count):
        west, east = from_west(tiles), from_east(tiles)
        return [
            centre[i] * tiles[i]
            + face_west[i] * west[i]
            - next_east[i] * east[i]
            + above[i] * pltpu.roll(tiles[i], 1, 0)
            + north[i] * pltpu.roll(tiles[i], ROWS - 1, 0)
            for i in range(count)
        ]

    return lambda tiles: advance(advance(tiles, 3), 2)


def transport(state, statics, wet, west_halo, east_halo, chunks):
    def level_step(level, carry):
        steps = stepper(level, statics, wet, west_halo, east_halo)

        def member_step(e, carry):
            for tracer in range(2):
                q = tracer * LEVELS + level
                done = steps(
                    widened(state[e, q], west_halo, east_halo, TRACER_LANES, e * PLANES + q)
                )
                for half in range(2):
                    rows = pl.ds(half * HALF_ROWS + e, ROWS, stride=MEMBERS)
                    chunks[q, rows, :] = done[half]
            return carry

        return lax.fori_loop(0, MEMBERS, member_step, carry, unroll=4)

    lax.fori_loop(0, LEVELS, level_step, 0)


def observe(
    state, statics, wet, west_halo, east_halo, count, cell, value, error, out, slots,
    own_cell, own_value, own_error, arrived
):
    copies = [
        pltpu.make_async_copy(cell, own_cell, arrived.at[0]),
        pltpu.make_async_copy(value, own_value, arrived.at[1]),
        pltpu.make_async_copy(error, own_error, arrived.at[2]),
    ]
    for copy in copies:
        copy.start()
    steps = stepper(0, statics, wet, west_halo, east_halo)
    surface = []
    for e in range(MEMBERS):
        done = steps(widened(state[e, 0], west_halo, east_halo, TRACER_LANES, e * PLANES))
        surface.append(jnp.concatenate(done, 1))
    for copy in copies:
        copy.wait()
    in_use = (lane_index((1, SLOTS)) < count[0]).astype(jnp.float32)
    scale = 1.0 / ((ENSEMBLE - 1) * own_error[...])
    unused = jnp.zeros((5, SLOTS), jnp.float32)
    slots[...] = jnp.concatenate([in_use, own_value[...], scale, unused], 0)
    cell = own_cell[...]
    column = lax.broadcasted_iota(jnp.int32, (COLUMNS, SLOTS), 0)
    pick = (column == (cell & (COLUMNS - 1))).astype(jnp.float32)
    near = jnp.dot(
        jnp.concatenate(surface, 0), pick, precision=HIGHEST, preferred_element_type=jnp.float32
    )
    layer = lax.broadcasted_iota(jnp.int32, (ROWS, SLOTS), 0)
    chosen = layer == (cell >> 8)
    for e in range(MEMBERS):
        kept = jnp.where(chosen, near[e * ROWS : (e + 1) * ROWS], 0.0)
        picked = jnp.sum(kept, 0, keepdims=True)
        for m in range(ENSEMBLE // MEMBERS):
            out[m, e : e + 1, :] = picked


def block_system(observed, slots, out):
    members = observed[...].reshape(ENSEMBLE, SLOTS)
    in_use, value, scale = slots[0:1], slots[1:2], slots[2:3]
    mean = jnp.sum(members, 0, keepdims=True) / ENSEMBLE
    anomaly = (members - mean) * in_use
    innovation = (value - mean) * in_use
    first = lax.broadcasted_iota(jnp.int32, (8, SLOTS), 0) == 0
    left = jnp.concatenate([anomaly, jnp.where(first, innovation, 0.0)], 0)
    unused = jnp.zeros((LANES - ENSEMBLE, SLOTS), jnp.float32)
    right = jnp.concatenate([anomaly * scale, unused], 0)
    out[...] = lax.dot_general(
        left, right, (((1,), (1,)), ((), ())), precision=HIGHEST,
        preferred_element_type=jnp.float32,
    )


def symmetric_inverse(a, b, c):
    scale = 1.0 / (a * c - b * b)
    return c * scale, -b * scale, a * scale


def pivot_inverse(e):
    a0, a1, a2 = symmetric_inverse(e[0][0], e[0][1], e[1][1])
    b00, b01, b10, b11 = e[0][2], e[0][3], e[1][2], e[1][3]
    f00, f01 = a0 * b00 + a1 * b10, a0 * b01 + a1 * b11
    f10, f11 = a1 * b00 + a2 * b10, a1 * b01 + a2 * b11
    s0, s1, s2 = symmetric_inverse(
        e[2][2] - (b00 * f00 + b10 * f10),
        e[2][3] - (b00 * f01 + b10 * f11),
        e[3][3] - (b01 * f01 + b11 * f11),
    )
    t00, t01 = f00 * s0 + f01 * s1, f00 * s1 + f01 * s2
    t10, t11 = f10 * s0 + f11 * s1, f10 * s1 + f11 * s2
    x01 = a1 + t00 * f10 + t01 * f11
    return [
        [a0 + t00 * f00 + t01 * f01, x01, -t00, -t01],
        [x01, a2 + t10 * f10 + t11 * f11, -t10, -t11],
        [-t00, -t10, s0, s1],
        [-t01, -t11, s1, s2],
    ]


def inverse(tiles):
    row = lax.broadcasted_iota(jnp.int32, (8, LANES), 0)
    lane = lane_index((8, LANES))
    size = 4

    def everywhere(block):
        return jnp.broadcast_to(block, (8, LANES))

    for k in range(0, ENSEMBLE, size):
        home, start = k // 8, k % 8
        columns = [[everywhere(tile[:, k + j : k + j + 1]) for tile in tiles] for j in range(size)]
        rows = [everywhere(tiles[home][start + i : start + i + 1]) for i in range(size)]
        pivots = pivot_inverse(
            [
                [everywhere(columns[j][home][start + i : start + i + 1]) for j in range(size)]
                for i in range(size)
            ]
        )
        scaled = []
        for i in range(size):
            value = (pivots[i][0] * rows[0] + pivots[i][1] * rows[1]) + (
                pivots[i][2] * rows[2] + pivots[i][3] * rows[3]
            )
            for j in range(size):
                value = jnp.where(lane == k + j, pivots[i][j], value)
            scaled.append(value)
        inside = (lane >= k) & (lane < k + size)
        rest = []
        for t, tile in enumerate(tiles):
            value = jnp.where(inside, 0.0, tile)
            for j in range(size):
                value = value - columns[j][t] * scaled[j]
            rest.append(value)
        for i in range(size):
            rest[home] = jnp.where(row == start + i, scaled[i], rest[home])
        tiles = rest
    return jnp.concatenate(tiles, 0)


def solve(own, west, east, out):
    row = lax.broadcasted_iota(jnp.int32, (SYSTEM_ROWS, LANES), 0)
    diagonal = row == lane_index((SYSTEM_ROWS, LANES))
    identity = jnp.where(diagonal & (row < ENSEMBLE), 1.0, 0.0)
    system = identity + own[...] + 0.5 * (west[...] + east[...])
    solved = inverse([system[8 * t : 8 * t + 8] for t in range(SYSTEM_ROWS // 8)])
    out[...] = 0.5 * (identity + solved)[:ENSEMBLE] - solved[ENSEMBLE : ENSEMBLE + 1]


def update(weights, received, out):
    left = weights[:, :ENSEMBLE]
    for r in range(ROWS):
        halves = [
            received[:, first : first + MEMBERS, :].reshape(ENSEMBLE, LANES)
            for first in (r * MEMBERS, HALF_ROWS + r * MEMBERS)
        ]
        result = jnp.dot(
            left, jnp.concatenate(halves, 1), precision=HIGHEST,
            preferred_element_type=jnp.float32,
        )
        for m in range(ENSEMBLE // MEMBERS):
            rows = result[m * MEMBERS : (m + 1) * MEMBERS]
            out[m, pl.ds(r, MEMBERS, stride=ROWS), :] = rows[:, :LANES]
            out[m, pl.ds(HALF_ROWS + r, MEMBERS, stride=ROWS), :] = rows[:, LANES:]


def unpack(planes, out, left):
    copies = []
    for q in range(PLANES):
        for half in range(2):
            copies.append(
                pltpu.make_async_copy(
                    planes.at[q, half],
                    out.at[:, q, :, half * LANES : (half + 1) * LANES],
                    left.at[q, half],
                )
            )
    for copy in copies:
        copy.start()
    for copy in copies:
        copy.wait()


def vmem():
    return pl.BlockSpec(memory_space=pltpu.VMEM)


def hbm():
    return pl.BlockSpec(memory_space=pltpu.HBM)


def kernel(body, operands, *shapes, scalars=(), fetched=(), scratch=(), out_spec=vmem):
    fetched = [pltpu.with_memory_space_constraint(x, pltpu.HBM) for x in fetched]
    shapes = [s if hasattr(s, "dtype") else jax.ShapeDtypeStruct(s, jnp.float32) for s in shapes]
    return pl.pallas_call(
        body,
        out_shape=shapes,
        in_specs=[vmem()] * len(operands)
        + [pl.BlockSpec(memory_space=pltpu.SMEM)] * len(scalars)
        + [hbm()] * len(fetched),
        out_specs=[out_spec() for _ in shapes],
        scratch_shapes=scratch,
        compiler_params=PARAMS,
        name=body.__name__,
    )(*operands, *scalars, *fetched)


def shifted(value, step):
    count = lax.axis_size("tile")
    return lax.ppermute(value, "tile", [(i, (i + step) % count) for i in range(count)])


def exchanged(value):
    return lax.all_to_all(value, "mem", split_axis=0, concat_axis=0, tiled=True)


def local(
    member_tracer_state, diffusivity, velocity, wet_mask, obs_cell, obs_count, obs_value, obs_error
):
    first, last, *blocks = kernel(
        pack_edges,
        (),
        (ROWS, COLUMNS),
        (ROWS, COLUMNS),
        member_tracer_state.shape,
        (2 * LEVELS, ROWS, COLUMNS),
        jax.ShapeDtypeStruct((ROWS, COLUMNS), jnp.int32),
        fetched=(member_tracer_state, diffusivity, velocity, wet_mask),
        scratch=[pltpu.SemaphoreType.DMA((5,))],
    )
    halos = (shifted(last, 1), shifted(first, -1))
    observed, slots = kernel(
        observe,
        (*blocks, *halos),
        (PLANES, MEMBERS, SLOTS),
        (8, SLOTS),
        scalars=(obs_count,),
        fetched=[x.reshape(1, SLOTS) for x in (obs_cell, obs_value, obs_error)],
        scratch=[
            pltpu.VMEM((1, SLOTS), jnp.int32),
            pltpu.VMEM((1, SLOTS), jnp.float32),
            pltpu.VMEM((1, SLOTS), jnp.float32),
            pltpu.SemaphoreType.DMA((3,)),
        ],
    )
    observed = exchanged(observed)
    (chunks,) = kernel(transport, (*blocks, *halos), (PLANES, CELL_ROWS, LANES))
    (share,) = kernel(block_system, (observed, slots), (SYSTEM_ROWS, LANES))
    share, chunks = lax.optimization_barrier((share, chunks))
    received = exchanged(chunks)
    shares = (share, shifted(share, 1), shifted(share, -1))
    (weights,) = kernel(solve, shares, (ENSEMBLE, LANES))
    (updated,) = kernel(update, (weights, received), (PLANES, CELL_ROWS, LANES))
    back = exchanged(updated)
    (analysis,) = kernel(
        unpack,
        (back.reshape(PLANES, 2, MEMBERS, ROWS, LANES),),
        member_tracer_state.shape,
        scratch=[pltpu.SemaphoreType.DMA((PLANES, 2))],
        out_spec=hbm,
    )
    return analysis


def solution(mesh):
    in_specs = (
        P("mem", None, None, "tile"),
        P(None, None, "tile"),
        P(None, None, "tile"),
        P(None, "tile"),
        P("tile"),
        P("tile"),
        P("tile"),
        P("tile"),
    )
    out_specs = P("mem", None, None, "tile")
    return jax.shard_map(local, mesh=mesh, in_specs=in_specs, out_specs=out_specs, check_vma=False)
```

time: 90.9 us -> 72.3 us (0.80)
  the two profiles are of different devices: /device:TPU:8 before, /device:TPU:249 now
where the time goes in v2:
time: 72.3 us; the launch traced here: 71.9 us
  starting transfers between devices  23.2 us (32%)
  blocking collectives  19.6 us (27%)
  Pallas kernels  15.2 us (21%)
  waiting for transfers between devices  13 us (18%)
  between operations  0.74 us (1%)
    all_to_all x1, blocking collectives, exchanged(): return lax.all_to_all(value, 'mem', split_axis=0, concat_axis=0, tiled=True)  19.6 us
    pallas_call x7, Pallas kernels, kernel(): pl.pallas_call(body, out_shape=shapes, in_specs=[vmem()] * len(operands)...  15.2 us
    ppermute x4, waiting for transfers between devices, shifted(): lax.ppermute(value, 'tile', [(i, (i + step) % count) for i in range(count)])  13 us
    ppermute x4, starting transfers between devices, shifted(): lax.ppermute(value, 'tile', [(i, (i + step) % count) for i in range(count)])  12.9 us
    all_to_all x2, starting transfers between devices, exchanged(): return lax.all_to_all(value, 'mem', split_axis=0, concat_axis=0, tiled=True)  10.4 us
  transfers between devices with their start and end apart: 6, of which 2 were waited for; matrix products, arithmetic and copies ran while one was open for 0% of the time, Pallas kernels for 12%

profile of v2, /device:TPU:249, one launch (start us, length us, event | category | flops | bytes accessed | tf_op | source)
XLA Modules:
  0.0 71.9 jit_solution(1803379358774483023)
XLA Ops:
  0.0 2.0 %pack_edges.1 = (f32[16,256]{1,0:T(8,128)S(1)}, f32[16,256]{1,0:T(8,128)S(1)}, f32[8,8,16,256]{3,2,1,0:T(8,128)S(1)}, f32[8,16,256]{2,1,0:T(8,128)S(1)}, s32[16,256]{1,0:T(8,128)S(1)}) custom-call(f32[8,8,16,256]{3,2,1,0:T(8,128)} %state.1, f32[4,16,256]{2,1,0:T(8,128)} %diffusivity.1, f32[4,16,256]{2,1,0:T(8,128)} %velocity.1, s32[16,256]{1,0:T(8,128)} %wet.1), custom_call_target="tpu_custom_call" | custom-call | tf_op jit(solution)/shard_map/pack_edges/pallas_call | solution.py:331
  2.0 6.0 %collective-permute-start = (f32[16,256]{1,0:T(8,128)S(1)}, f32[16,256]{1,0:T(8,128)S(1)}, u32[]{:S(2)}, u32[]{:S(2)}) collective-permute-start(f32[16,256]{1,0:T(8,128)S(1)} %get-tuple-element.17), channel_id=1, source_target_pairs={{0,8},{8,16},{16,24},{24,32},{32,40},{40,48},{48,56},{56,64},{64,7... | collective-permute-start | bytes 49160 | tf_op jit(solution)/shard_map/ppermute | solution.py:346
  8.0 1.9 %collective-permute-start.1 = (f32[16,256]{1,0:T(8,128)S(1)}, f32[16,256]{1,0:T(8,128)S(1)}, u32[]{:S(2)}, u32[]{:S(2)}) collective-permute-start(f32[16,256]{1,0:T(8,128)S(1)} %get-tuple-element.18), channel_id=1, source_target_pairs={{0,504},{8,0},{16,8},{24,16},{32,24},{40,32},{48,40},{56,48},{64,5... | collective-permute-start | bytes 49160 | tf_op jit(solution)/shard_map/ppermute | solution.py:346
  10.6 0.0 collective-permute-done.west_halo
  10.6 6.1 %collective-permute-done.1.east_halo = f32[16,256]{1,0:T(8,128)S(1)} collective-permute-done((f32[16,256]{1,0:T(8,128)S(1)}, f32[16,256]{1,0:T(8,128)S(1)}, u32[]{:S(2)}, u32[]{:S(2)}) %collective-permute-start.1) | collective-permute-done | bytes 16416 | tf_op jit(solution)/shard_map/ppermute | solution.py:346
  16.7 2.1 %observe.1 = (f32[8,8,128]{2,1,0:T(8,128)}, f32[8,128]{1,0:T(8,128)S(1)}) custom-call(f32[8,8,16,256]{3,2,1,0:T(8,128)S(1)} %get-tuple-element.14.state, f32[8,16,256]{2,1,0:T(8,128)S(1)} %get-tuple-element.15.statics, s32[16,256]{1,0:T(8,128)S(1)} %get-tuple-element.16.wet, f32[16,256]{1,0:T(8,128)S(1)} %collective-permute-done.west_halo, ...), custom_call_target="tpu_custom_call" | custom-call | tf_op jit(solution)/shard_map/observe/pallas_call | solution.py:331
  18.8 5.2 %all-to-all-start = ((f32[8,8,128]{2,1,0:T(8,128)}), f32[8,8,128]{2,1,0:T(8,128)S(1)}, u32[]{:S(2)}, u32[]{:S(2)}) async-start(f32[8,8,128]{2,1,0:T(8,128)} %get-tuple-element.19), calls=%async_computation | async-start | bytes 65536 | tf_op jit(solution)/shard_map/all_to_all | solution.py:350
  24.0 5.6 %transport.1 = f32[8,256,128]{2,1,0:T(8,128)} custom-call(f32[8,8,16,256]{3,2,1,0:T(8,128)S(1)} %get-tuple-element.14.state, f32[8,16,256]{2,1,0:T(8,128)S(1)} %get-tuple-element.15.statics, s32[16,256]{1,0:T(8,128)S(1)} %get-tuple-element.16.wet, f32[16,256]{1,0:T(8,128)S(1)} %collective-permute-done.west_halo, f32[16,256]{1,0:T(8,128)S(1)} %collective-permute-done.1.east_halo), custom_call_target="tpu_custom_call" | custom-call | tf_op jit(solution)/shard_map/transport/pallas_call | solution.py:331
  29.6 0.0 all-to-all-done.observed
  29.6 0.2 block_system.1.own
  29.8 5.2 %all-to-all-start.1 = ((f32[8,256,128]{2,1,0:T(8,128)}), f32[8,256,128]{2,1,0:T(8,128)S(1)}, u32[]{:S(2)}, u32[]{:S(2)}) async-start(f32[8,256,128]{2,1,0:T(8,128)} %transport.1), calls=%async_computation.1 | async-start | bytes 2097152 | tf_op jit(solution)/shard_map/all_to_all | solution.py:350
  35.0 3.0 %collective-permute-start.2 = (f32[72,128]{1,0:T(8,128)S(1)}, f32[72,128]{1,0:T(8,128)S(1)}, u32[]{:S(2)}, u32[]{:S(2)}) collective-permute-start(f32[72,128]{1,0:T(8,128)S(1)} %block_system.1.own), channel_id=1, source_target_pairs={{0,8},{8,16},{16,24},{24,32},{32,40},{40,48},{48,56},{56,64},{64,7... | collective-permute-start | bytes 110600 | tf_op jit(solution)/shard_map/ppermute | solution.py:346
  38.0 1.9 %collective-permute-start.3 = (f32[72,128]{1,0:T(8,128)S(1)}, f32[72,128]{1,0:T(8,128)S(1)}, u32[]{:S(2)}, u32[]{:S(2)}) collective-permute-start(f32[72,128]{1,0:T(8,128)S(1)} %block_system.1.own), channel_id=1, source_target_pairs={{0,504},{8,0},{16,8},{24,16},{32,24},{40,32},{48,40},{56,48},{64,5... | collective-permute-start | bytes 110600 | tf_op jit(solution)/shard_map/ppermute | solution.py:346
  40.0 0.0 collective-permute-done.2.west
  40.0 7.0 %collective-permute-done.3.east = f32[72,128]{1,0:T(8,128)S(1)} collective-permute-done((f32[72,128]{1,0:T(8,128)S(1)}, f32[72,128]{1,0:T(8,128)S(1)}, u32[]{:S(2)}, u32[]{:S(2)}) %collective-permute-start.3) | collective-permute-done | bytes 36896 | tf_op jit(solution)/shard_map/ppermute | solution.py:346
  46.9 3.0 %solve.1.weights = f32[64,128]{1,0:T(8,128)S(1)} custom-call(f32[72,128]{1,0:T(8,128)S(1)} %block_system.1.own, f32[72,128]{1,0:T(8,128)S(1)} %collective-permute-done.2.west, f32[72,128]{1,0:T(8,128)S(1)} %collective-permute-done.3.east), custom_call_target="tpu_custom_call" | custom-call | tf_op jit(solution)/shard_map/solve/pallas_call | solution.py:331
  49.9 0.0 all-to-all-done.1.received
  49.9 1.2 %update.1 = f32[8,256,128]{2,1,0:T(8,128)S(1)} custom-call(f32[64,128]{1,0:T(8,128)S(1)} %solve.1.weights, f32[8,256,128]{2,1,0:T(8,128)S(1)} %all-to-all-done.1.received), custom_call_target="tpu_custom_call" | custom-call | tf_op jit(solution)/shard_map/update/pallas_call | solution.py:331
  51.2 19.6 %all_to_all.15 = f32[8,256,128]{2,1,0:T(8,128)S(1)} all-to-all(f32[8,256,128]{2,1,0:T(8,128)S(1)} %update.1), channel_id=1, replica_groups=mesh['tile'=64,'mem'=8] {'mem'}, dimensions={0} | all-to-all | bytes 2097152 | tf_op jit(solution)/shard_map/all_to_all | solution.py:350
  70.8 1.1 %unpack.1 = f32[8,8,16,256]{3,2,1,0:T(8,128)} custom-call(f32[8,2,8,16,128]{4,3,2,1,0:T(8,128)S(1)} %bitcast.4), custom_call_target="tpu_custom_call" | custom-call | tf_op jit(solution)/shard_map/unpack/pallas_call | solution.py:331
Async XLA Ops:
  2.0 8.6 %collective-permute-start = (f32[16,256]{1,0:T(8,128)S(1)}, f32[16,256]{1,0:T(8,128)S(1)}, u32[]{:S(2)}, u32[]{:S(2)}) collective-permute-start(f32[16,256]{1,0:T(8,128)S(1)} %get-tuple-element.17), channel_id=1, source_target_pairs={{0,8},{8,16},{16,24},{24,32},{32,40},{40,48},{48,56},{56,64},{64,7... | collective-permute-start | bytes 49160 | tf_op jit(solution)/shard_map/ppermute | solution.py:346
  8.0 8.7 %collective-permute-start.1 = (f32[16,256]{1,0:T(8,128)S(1)}, f32[16,256]{1,0:T(8,128)S(1)}, u32[]{:S(2)}, u32[]{:S(2)}) collective-permute-start(f32[16,256]{1,0:T(8,128)S(1)} %get-tuple-element.18), channel_id=1, source_target_pairs={{0,504},{8,0},{16,8},{24,16},{32,24},{40,32},{48,40},{56,48},{64,5... | collective-permute-start | bytes 49160 | tf_op jit(solution)/shard_map/ppermute | solution.py:346
  18.8 10.8 %all-to-all-start = ((f32[8,8,128]{2,1,0:T(8,128)}), f32[8,8,128]{2,1,0:T(8,128)S(1)}, u32[]{:S(2)}, u32[]{:S(2)}) async-start(f32[8,8,128]{2,1,0:T(8,128)} %get-tuple-element.19), calls=%async_computation | async-start | bytes 65536 | tf_op jit(solution)/shard_map/all_to_all | solution.py:350
  29.8 20.1 %all-to-all-start.1 = ((f32[8,256,128]{2,1,0:T(8,128)}), f32[8,256,128]{2,1,0:T(8,128)S(1)}, u32[]{:S(2)}, u32[]{:S(2)}) async-start(f32[8,256,128]{2,1,0:T(8,128)} %transport.1), calls=%async_computation.1 | async-start | bytes 2097152 | tf_op jit(solution)/shard_map/all_to_all | solution.py:350
  35.0 5.0 %collective-permute-start.2 = (f32[72,128]{1,0:T(8,128)S(1)}, f32[72,128]{1,0:T(8,128)S(1)}, u32[]{:S(2)}, u32[]{:S(2)}) collective-permute-start(f32[72,128]{1,0:T(8,128)S(1)} %block_system.1.own), channel_id=1, source_target_pairs={{0,8},{8,16},{16,24},{24,32},{32,40},{40,48},{48,56},{56,64},{64,7... | collective-permute-start | bytes 110600 | tf_op jit(solution)/shard_map/ppermute | solution.py:346
  38.0 8.9 %collective-permute-start.3 = (f32[72,128]{1,0:T(8,128)S(1)}, f32[72,128]{1,0:T(8,128)S(1)}, u32[]{:S(2)}, u32[]{:S(2)}) collective-permute-start(f32[72,128]{1,0:T(8,128)S(1)} %block_system.1.own), channel_id=1, source_target_pairs={{0,504},{8,0},{16,8},{24,16},{32,24},{40,32},{48,40},{56,48},{64,5... | collective-permute-start | bytes 110600 | tf_op jit(solution)/shard_map/ppermute | solution.py:346

commit v3 on v2

--- a/solution.py
+++ b/solution.py
@@ -8,6 +8,7 @@
 LEVELS = 4
 PLANES = 8
 MEMBERS = 8
+PARTS = 4
 ENSEMBLE = 64
 ROWS = 16
 COLUMNS = 256
@@ -15,7 +16,9 @@
 LANES = 128
 HALF_ROWS = ROWS * MEMBERS
 CELL_ROWS = 2 * HALF_ROWS
+CHUNK_ROWS = CELL_ROWS + 3 * MEMBERS
 SYSTEM_ROWS = ENSEMBLE + 8
+TRACER_LANES, STATIC_LANES = slice(0, LANES), slice(LANES, 2 * LANES)
 HIGHEST = lax.Precision.HIGHEST
 PARAMS = pltpu.CompilerParams(vmem_limit_bytes=32 * 1024 * 1024)
 
@@ -25,18 +28,31 @@
 
 
 def pack_edges(
-    state, diffusivity, velocity, wet, first, last, own_state, own_statics, own_wet, arrived
+    state, diffusivity, velocity, wet, cell, value, error, off_chip, on_chip, own_state, own_statics,
+    own_wet, own_cell, own_value, own_error, arrived
 ):
+    odd = lax.axis_index("tile") % 2 == 1
+
+    def hand_out(lanes, first, last):
+        on_chip[:, lanes] = jnp.where(odd, first, last)
+        off_chip[:, lanes] = jnp.where(odd, last, first)
+
+    copies = []
+    for part in range(PARTS):
+        rows = slice(part * MEMBERS // PARTS, (part + 1) * MEMBERS // PARTS)
+        copies.append((state.at[rows], own_state.at[rows]))
+    copies += [
+        (diffusivity, own_statics.at[:LEVELS]),
+        (velocity, own_statics.at[LEVELS:]),
+        (wet, own_wet),
+        (cell, own_cell),
+        (value, own_value),
+        (error, own_error),
+    ]
     copies = [
-        pltpu.make_async_copy(diffusivity, own_statics.at[:LEVELS], arrived.at[0]),
-        pltpu.make_async_copy(velocity, own_statics.at[LEVELS:], arrived.at[1]),
-        pltpu.make_async_copy(wet, own_wet, arrived.at[2]),
+        pltpu.make_async_copy(source, target, arrived.at[i])
+        for i, (source, target) in enumerate(copies)
     ]
-    for part in range(2):
-        rows = slice(part * MEMBERS // 2, (part + 1) * MEMBERS // 2)
-        copies.append(
-            pltpu.make_async_copy(state.at[rows], own_state.at[rows], arrived.at[3 + part])
-        )
     for copy in copies:
         copy.start()
     pair = lane_index((ROWS, LANES)) >> 1
@@ -49,27 +65,32 @@
         )
         return first_kept, last_kept
 
-    zeros = jnp.zeros((ROWS, LANES), jnp.float32)
-    kept = (zeros, zeros)
-    for copy in copies[:3]:
-        copy.wait()
-    for i in range(2 * LEVELS):
-        kept = put(own_statics[i, :, :LANES], own_statics[i, :, LANES:], i, kept)
-    flags = own_wet[...].astype(jnp.float32)
-    kept = put(flags[:, :LANES], flags[:, LANES:], 2 * LEVELS, kept)
-    first[:, LANES:], last[:, LANES:] = kept
-
     def member(e, kept):
         for q in range(PLANES):
             low, high = own_state[e, q, :, :LANES], own_state[e, q, :, LANES:]
             kept = put(low, high, e * PLANES + q, kept)
         return kept
 
+    zeros = jnp.zeros((ROWS, LANES), jnp.float32)
     kept = (zeros, zeros)
-    for part in range(2):
-        copies[3 + part].wait()
-        kept = lax.fori_loop(part * MEMBERS // 2, (part + 1) * MEMBERS // 2, member, kept)
-    first[:, :LANES], last[:, :LANES] = kept
+    for part in range(PARTS):
+        copies[part].wait()
+        kept = lax.fori_loop(part * MEMBERS // PARTS, (part + 1) * MEMBERS // PARTS, member, kept)
+    hand_out(TRACER_LANES, *kept)
+    for copy in copies[PARTS:]:
+        copy.wait()
+    kept = (zeros, zeros)
+    for i in range(2 * LEVELS):
+        kept = put(own_statics[i, :, :LANES], own_statics[i, :, LANES:], i, kept)
+    flags = own_wet[...].astype(jnp.float32)
+    kept = put(flags[:, :LANES], flags[:, LANES:], 2 * LEVELS, kept)
+    hand_out(STATIC_LANES, *kept)
+
+
+def halos(off_chip, on_chip):
+    odd = lax.axis_index("tile") % 2 == 1
+    one, other = on_chip[...], off_chip[...]
+    return jnp.where(odd, one, other), jnp.where(odd, other, one)
 
 
 def from_west(tiles):
@@ -89,9 +110,6 @@
     east = pltpu.roll(east, (LANES - 2 * index) % LANES, 1)
     west = pltpu.roll(west, LANES - 2 - 2 * index, 1)
     return jnp.where(lane < 2, east, jnp.where(lane >= LANES - 2, west, 0.0))
-
-
-TRACER_LANES, STATIC_LANES = slice(0, LANES), slice(LANES, 2 * LANES)
 
 
 def widened(block, west_halo, east_halo, lanes, index):
@@ -136,7 +154,9 @@
     return lambda tiles: advance(advance(tiles, 3), 2)
 
 
-def transport(state, statics, wet, west_halo, east_halo, chunks):
+def transport(state, statics, wet, off_chip, on_chip, chunks):
+    west_halo, east_halo = halos(off_chip, on_chip)
+
     def level_step(level, carry):
         steps = stepper(level, statics, wet, west_halo, east_halo)
 
@@ -156,29 +176,18 @@
     lax.fori_loop(0, LEVELS, level_step, 0)
 
 
-def observe(
-    state, statics, wet, west_halo, east_halo, count, cell, value, error, out, slots,
-    own_cell, own_value, own_error, arrived
-):
-    copies = [
-        pltpu.make_async_copy(cell, own_cell, arrived.at[0]),
-        pltpu.make_async_copy(value, own_value, arrived.at[1]),
-        pltpu.make_async_copy(error, own_error, arrived.at[2]),
-    ]
-    for copy in copies:
-        copy.start()
+def observe(state, statics, wet, off_chip, on_chip, cell, value, error, count, out):
+    west_halo, east_halo = halos(off_chip, on_chip)
     steps = stepper(0, statics, wet, west_halo, east_halo)
     surface = []
     for e in range(MEMBERS):
         done = steps(widened(state[e, 0], west_halo, east_halo, TRACER_LANES, e * PLANES))
         surface.append(jnp.concatenate(done, 1))
-    for copy in copies:
-        copy.wait()
     in_use = (lane_index((1, SLOTS)) < count[0]).astype(jnp.float32)
-    scale = 1.0 / ((ENSEMBLE - 1) * own_error[...])
+    scale = 1.0 / ((ENSEMBLE - 1) * error[...])
     unused = jnp.zeros((5, SLOTS), jnp.float32)
-    slots[...] = jnp.concatenate([in_use, own_value[...], scale, unused], 0)
-    cell = own_cell[...]
+    out[MEMBERS:, :] = jnp.concatenate([in_use, value[...], scale, unused], 0)
+    cell = cell[...]
     column = lax.broadcasted_iota(jnp.int32, (COLUMNS, SLOTS), 0)
     pick = (column == (cell & (COLUMNS - 1))).astype(jnp.float32)
     near = jnp.dot(
@@ -188,24 +197,32 @@
     chosen = layer == (cell >> 8)
     for e in range(MEMBERS):
         kept = jnp.where(chosen, near[e * ROWS : (e + 1) * ROWS], 0.0)
-        picked = jnp.sum(kept, 0, keepdims=True)
-        for m in range(ENSEMBLE // MEMBERS):
-            out[m, e : e + 1, :] = picked
-
-
-def block_system(observed, slots, out):
-    members = observed[...].reshape(ENSEMBLE, SLOTS)
-    in_use, value, scale = slots[0:1], slots[1:2], slots[2:3]
-    mean = jnp.sum(members, 0, keepdims=True) / ENSEMBLE
-    anomaly = (members - mean) * in_use
-    innovation = (value - mean) * in_use
+        out[e : e + 1, :] = jnp.sum(kept, 0, keepdims=True)
+
+
+def attach(chunks, own, off_chip, on_chip, out):
+    for i, block in enumerate((own, off_chip, on_chip)):
+        values = block[:MEMBERS]
+        for q in range(PLANES):
+            out[q, pl.ds(CELL_ROWS + i * MEMBERS, MEMBERS), :] = values
+
+
+def gram(received, blocks):
     first = lax.broadcasted_iota(jnp.int32, (8, SLOTS), 0) == 0
-    left = jnp.concatenate([anomaly, jnp.where(first, innovation, 0.0)], 0)
     unused = jnp.zeros((LANES - ENSEMBLE, SLOTS), jnp.float32)
-    right = jnp.concatenate([anomaly * scale, unused], 0)
-    out[...] = lax.dot_general(
-        left, right, (((1,), (1,)), ((), ())), precision=HIGHEST,
-        preferred_element_type=jnp.float32,
+    left, right = [], []
+    for i, (block, locality) in enumerate(zip(blocks, (1.0, 0.5, 0.5))):
+        rows = pl.ds(CELL_ROWS + i * MEMBERS, MEMBERS)
+        members = received[:, rows, :].reshape(ENSEMBLE, SLOTS)
+        in_use, value, scale = (block[MEMBERS + j : MEMBERS + j + 1] for j in range(3))
+        mean = jnp.sum(members, 0, keepdims=True) / ENSEMBLE
+        anomaly = (members - mean) * in_use
+        innovation = (value - mean) * in_use
+        left.append(jnp.concatenate([anomaly, jnp.where(first, innovation, 0.0)], 0))
+        right.append(jnp.concatenate([anomaly * (scale * locality), unused], 0))
+    return lax.dot_general(
+        jnp.concatenate(left, 1), jnp.concatenate(right, 1), (((1,), (1,)), ((), ())),
+        precision=HIGHEST, preferred_element_type=jnp.float32,
     )
 
 
@@ -274,24 +291,21 @@
     return jnp.concatenate(tiles, 0)
 
 
-def solve(own, west, east, out):
+def analyse(received, own, off_chip, on_chip, out):
     row = lax.broadcasted_iota(jnp.int32, (SYSTEM_ROWS, LANES), 0)
     diagonal = row == lane_index((SYSTEM_ROWS, LANES))
     identity = jnp.where(diagonal & (row < ENSEMBLE), 1.0, 0.0)
-    system = identity + own[...] + 0.5 * (west[...] + east[...])
+    system = identity + gram(received, (own, off_chip, on_chip))
     solved = inverse([system[8 * t : 8 * t + 8] for t in range(SYSTEM_ROWS // 8)])
-    out[...] = 0.5 * (identity + solved)[:ENSEMBLE] - solved[ENSEMBLE : ENSEMBLE + 1]
-
-
-def update(weights, received, out):
-    left = weights[:, :ENSEMBLE]
+    weights = 0.5 * (identity + solved)[:ENSEMBLE] - solved[ENSEMBLE : ENSEMBLE + 1]
+    weights = weights[:, :ENSEMBLE]
     for r in range(ROWS):
         halves = [
             received[:, first : first + MEMBERS, :].reshape(ENSEMBLE, LANES)
             for first in (r * MEMBERS, HALF_ROWS + r * MEMBERS)
         ]
         result = jnp.dot(
-            left, jnp.concatenate(halves, 1), precision=HIGHEST,
+            weights, jnp.concatenate(halves, 1), precision=HIGHEST,
             preferred_element_type=jnp.float32,
         )
         for m in range(ENSEMBLE // MEMBERS):
@@ -325,7 +339,9 @@
     return pl.BlockSpec(memory_space=pltpu.HBM)
 
 
-def kernel(body, operands, *shapes, scalars=(), fetched=(), scratch=(), out_spec=vmem):
+def kernel(
+    body, operands, *shapes, scalars=(), fetched=(), scratch=(), out_spec=vmem, aliases={}
+):
     fetched = [pltpu.with_memory_space_constraint(x, pltpu.HBM) for x in fetched]
     shapes = [s if hasattr(s, "dtype") else jax.ShapeDtypeStruct(s, jnp.float32) for s in shapes]
     return pl.pallas_call(
@@ -336,14 +352,21 @@
         + [hbm()] * len(fetched),
         out_specs=[out_spec() for _ in shapes],
         scratch_shapes=scratch,
+        input_output_aliases=aliases,
         compiler_params=PARAMS,
         name=body.__name__,
     )(*operands, *scalars, *fetched)
 
 
-def shifted(value, step):
+def swapped(value, start):
     count = lax.axis_size("tile")
-    return lax.ppermute(value, "tile", [(i, (i + step) % count) for i in range(count)])
+    pairs = [((i + start) % count, (i + 1 + start) % count) for i in range(0, count, 2)]
+    return lax.ppermute(value, "tile", pairs + [(b, a) for a, b in pairs])
+
+
+def both_neighbours(off_chip, on_chip):
+    far = swapped(off_chip, 1)
+    return far, swapped(on_chip, 0)
 
 
 def exchanged(value):
@@ -353,7 +376,8 @@
 def local(
     member_tracer_state, diffusivity, velocity, wet_mask, obs_cell, obs_count, obs_value, obs_error
 ):
-    first, last, *blocks = kernel(
+    slot_rows = [x.reshape(1, SLOTS) for x in (obs_cell, obs_value, obs_error)]
+    off_chip, on_chip, *blocks, cell, value, error = kernel(
         pack_edges,
         (),
         (ROWS, COLUMNS),
@@ -361,32 +385,21 @@
         member_tracer_state.shape,
         (2 * LEVELS, ROWS, COLUMNS),
         jax.ShapeDtypeStruct((ROWS, COLUMNS), jnp.int32),
-        fetched=(member_tracer_state, diffusivity, velocity, wet_mask),
-        scratch=[pltpu.SemaphoreType.DMA((5,))],
-    )
-    halos = (shifted(last, 1), shifted(first, -1))
-    observed, slots = kernel(
-        observe,
-        (*blocks, *halos),
-        (PLANES, MEMBERS, SLOTS),
-        (8, SLOTS),
-        scalars=(obs_count,),
-        fetched=[x.reshape(1, SLOTS) for x in (obs_cell, obs_value, obs_error)],
-        scratch=[
-            pltpu.VMEM((1, SLOTS), jnp.int32),
-            pltpu.VMEM((1, SLOTS), jnp.float32),
-            pltpu.VMEM((1, SLOTS), jnp.float32),
-            pltpu.SemaphoreType.DMA((3,)),
-        ],
-    )
-    observed = exchanged(observed)
-    (chunks,) = kernel(transport, (*blocks, *halos), (PLANES, CELL_ROWS, LANES))
-    (share,) = kernel(block_system, (observed, slots), (SYSTEM_ROWS, LANES))
-    share, chunks = lax.optimization_barrier((share, chunks))
+        jax.ShapeDtypeStruct((1, SLOTS), jnp.int32),
+        (1, SLOTS),
+        (1, SLOTS),
+        fetched=(member_tracer_state, diffusivity, velocity, wet_mask, *slot_rows),
+        scratch=[pltpu.SemaphoreType.DMA((PARTS + 6,))],
+    )
+    edges = both_neighbours(off_chip, on_chip)
+    (own,) = kernel(
+        observe, (*blocks, *edges, cell, value, error), (2 * MEMBERS, SLOTS), scalars=(obs_count,)
+    )
+    near = (own, *both_neighbours(own, own))
+    (chunks,) = kernel(transport, (*blocks, *edges), (PLANES, CHUNK_ROWS, LANES))
+    (chunks,) = kernel(attach, (chunks, *near), chunks.shape, aliases={0: 0})
     received = exchanged(chunks)
-    shares = (share, shifted(share, 1), shifted(share, -1))
-    (weights,) = kernel(solve, shares, (ENSEMBLE, LANES))
-    (updated,) = kernel(update, (weights, received), (PLANES, CELL_ROWS, LANES))
+    (updated,) = kernel(analyse, (received, *near), (PLANES, CELL_ROWS, LANES))
     back = exchanged(updated)
     (analysis,) = kernel(
         unpack,

time: 72.3 us -> 68.9 us (0.953)
  the two profiles are of different devices: /device:TPU:249 before, /device:TPU:8 now
where the time goes in v3:
time: 68.9 us; the launch traced here: 68.6 us
  blocking collectives  32.2 us (47%)
  starting transfers between devices  22 us (32%)
  Pallas kernels  13.2 us (19%)
  between operations  0.74 us (1%)
    all_to_all x2, blocking collectives, exchanged(): return lax.all_to_all(value, 'mem', split_axis=0, concat_axis=0, tiled=True)  32.2 us
    ppermute x4, starting transfers between devices, swapped(): return lax.ppermute(value, 'tile', pairs + [(b, a) for a, b in pairs])  22 us
    pallas_call x6, Pallas kernels, kernel(): pl.pallas_call(body, out_shape=shapes, in_specs=[vmem()] * len(operands)...  13.2 us
  transfers between devices with their start and end apart: 4, of which 1 were waited for; matrix products, arithmetic and copies ran while one was open for 0% of the time, Pallas kernels for 7%

profile of v3, /device:TPU:8, one launch (start us, length us, event | category | flops | bytes accessed | tf_op | source)
XLA Modules:
  0.0 68.6 jit_solution(8012582761418016716)
XLA Ops:
  0.0 2.0 %pack_edges.1 = (f32[16,256]{1,0:T(8,128)S(1)}, f32[16,256]{1,0:T(8,128)S(1)}, f32[8,8,16,256]{3,2,1,0:T(8,128)S(1)}, f32[8,16,256]{2,1,0:T(8,128)S(1)}, s32[16,...) custom-call(f32[8,8,16,256]{3,2,1,0:T(8,128)} %state.1, ...), custom_call_target="tpu_custom_call" | custom-call | tf_op jit(solution)/shard_map/pack_edges/pallas_call | solution.py:347
  2.0 12.6 %collective-permute-start = (f32[16,256]{1,0:T(8,128)S(1)}, f32[16,256]{1,0:T(8,128)S(1)}, u32[]{:S(2)}, u32[]{:S(2)}) collective-permute-start(f32[16,256]{1,0:T(8,128)S(1)} %get-tuple-element.16), channel_id=1, source_target_pairs={{8,16},{24,32},{40,48},{56,64},{72,80},{88,96},{104,112},{120,128}... | collective-permute-start | bytes 49160 | tf_op jit(solution)/shard_map/ppermute | solution.py:364
  14.6 1.9 %collective-permute-start.1 = (f32[16,256]{1,0:T(8,128)S(1)}, f32[16,256]{1,0:T(8,128)S(1)}, u32[]{:S(2)}, u32[]{:S(2)}) collective-permute-start(f32[16,256]{1,0:T(8,128)S(1)} %get-tuple-element.17), channel_id=1, source_target_pairs={{0,8},{16,24},{32,40},{48,56},{64,72},{80,88},{96,104},{112,120},{... | collective-permute-start | bytes 49160 | tf_op jit(solution)/shard_map/ppermute | solution.py:364
  17.2 0.0 collective-permute-done.off_chip
  17.2 0.5 collective-permute-done.1.on_chip
  17.7 0.7 observe.1.own
  18.3 2.1 %collective-permute-start.3 = (f32[16,128]{1,0:T(8,128)S(1)}, f32[16,128]{1,0:T(8,128)S(1)}, u32[]{:S(2)}, u32[]{:S(2)}) collective-permute-start(f32[16,128]{1,0:T(8,128)S(1)} %observe.1.own), channel_id=1, source_target_pairs={{0,8},{16,24},{32,40},{48,56},{64,72},{80,88},{96,104},{112,120},{... | collective-permute-start | bytes 24584 | tf_op jit(solution)/shard_map/ppermute | solution.py:364
  20.4 5.4 %collective-permute-start.2 = (f32[16,128]{1,0:T(8,128)S(1)}, f32[16,128]{1,0:T(8,128)S(1)}, u32[]{:S(2)}, u32[]{:S(2)}) collective-permute-start(f32[16,128]{1,0:T(8,128)S(1)} %observe.1.own), channel_id=1, source_target_pairs={{8,16},{24,32},{40,48},{56,64},{72,80},{88,96},{104,112},{120,128}... | collective-permute-start | bytes 24584 | tf_op jit(solution)/shard_map/ppermute | solution.py:364
  25.8 4.6 %transport.1.chunks = f32[8,280,128]{2,1,0:T(8,128)S(1)} custom-call(f32[8,8,16,256]{3,2,1,0:T(8,128)S(1)} %get-tuple-element.13.state, f32[8,16,256]{2,1,0:T(8,128)S(1)} %get-tuple-element.14.statics, s32[16,256]{1,0:T(8,128)S(1)} %get-tuple-element.15.wet, f32[16,256]{1,0:T(8,128)S(1)} %collective-permute-done.off_chip, ...), custom_call_target="tpu_custom_call" | custom-call | tf_op jit(solution)/shard_map/transport/pallas_call | solution.py:347
  30.5 0.0 collective-permute-done.3.on_chip
  30.5 0.0 collective-permute-done.2.off_chip
  30.5 18.1 %all_to_all.10.received = f32[8,280,128]{2,1,0:T(8,128)S(1)} all-to-all(f32[8,280,128]{2,1,0:T(8,128)S(1)} %attach.1), channel_id=1, replica_groups=mesh['tile'=64,'mem'=8] {'mem'}, dimensions={0} | all-to-all | bytes 2293760 | tf_op jit(solution)/shard_map/all_to_all | solution.py:373
  48.6 4.9 %analyse.1 = f32[8,256,128]{2,1,0:T(8,128)S(1)} custom-call(f32[8,280,128]{2,1,0:T(8,128)S(1)} %all_to_all.10.received, f32[16,128]{1,0:T(8,128)S(1)} %observe.1.own, f32[16,128]{1,0:T(8,128)S(1)} %collective-permute-done.2.off_chip, f32[16,128]{1,0:T(8,128)S(1)} %collective-permute-done.3.on_chip), custom_call_target="tpu_custom_call" | custom-call | tf_op jit(solution)/shard_map/analyse/pallas_call | solution.py:347
  53.5 14.0 %all_to_all.11 = f32[8,256,128]{2,1,0:T(8,128)S(1)} all-to-all(f32[8,256,128]{2,1,0:T(8,128)S(1)} %analyse.1), channel_id=1, replica_groups=mesh['tile'=64,'mem'=8] {'mem'}, dimensions={0} | all-to-all | bytes 2097152 | tf_op jit(solution)/shard_map/all_to_all | solution.py:373
  67.5 1.1 %unpack.1 = f32[8,8,16,256]{3,2,1,0:T(8,128)} custom-call(f32[8,2,8,16,128]{4,3,2,1,0:T(8,128)S(1)} %bitcast.4), custom_call_target="tpu_custom_call" | custom-call | tf_op jit(solution)/shard_map/unpack/pallas_call | solution.py:347
  (1 shorter events, 0.0 us)
Async XLA Ops:
  2.0 15.2 %collective-permute-start = (f32[16,256]{1,0:T(8,128)S(1)}, f32[16,256]{1,0:T(8,128)S(1)}, u32[]{:S(2)}, u32[]{:S(2)}) collective-permute-start(f32[16,256]{1,0:T(8,128)S(1)} %get-tuple-element.16), channel_id=1, source_target_pairs={{8,16},{24,32},{40,48},{56,64},{72,80},{88,96},{104,112},{120,128}... | collective-permute-start | bytes 49160 | tf_op jit(solution)/shard_map/ppermute | solution.py:364
  14.6 3.1 %collective-permute-start.1 = (f32[16,256]{1,0:T(8,128)S(1)}, f32[16,256]{1,0:T(8,128)S(1)}, u32[]{:S(2)}, u32[]{:S(2)}) collective-permute-start(f32[16,256]{1,0:T(8,128)S(1)} %get-tuple-element.17), channel_id=1, source_target_pairs={{0,8},{16,24},{32,40},{48,56},{64,72},{80,88},{96,104},{112,120},{... | collective-permute-start | bytes 49160 | tf_op jit(solution)/shard_map/ppermute | solution.py:364
  18.3 12.1 %collective-permute-start.3 = (f32[16,128]{1,0:T(8,128)S(1)}, f32[16,128]{1,0:T(8,128)S(1)}, u32[]{:S(2)}, u32[]{:S(2)}) collective-permute-start(f32[16,128]{1,0:T(8,128)S(1)} %observe.1.own), channel_id=1, source_target_pairs={{0,8},{16,24},{32,40},{48,56},{64,72},{80,88},{96,104},{112,120},{... | collective-permute-start | bytes 24584 | tf_op jit(solution)/shard_map/ppermute | solution.py:364
  20.4 10.1 %collective-permute-start.2 = (f32[16,128]{1,0:T(8,128)S(1)}, f32[16,128]{1,0:T(8,128)S(1)}, u32[]{:S(2)}, u32[]{:S(2)}) collective-permute-start(f32[16,128]{1,0:T(8,128)S(1)} %observe.1.own), channel_id=1, source_target_pairs={{8,16},{24,32},{40,48},{56,64},{72,80},{88,96},{104,112},{120,128}... | collective-permute-start | bytes 24584 | tf_op jit(solution)/shard_map/ppermute | solution.py:364

commit v4 on v3

--- a/solution.py
+++ b/solution.py
@@ -75,7 +75,9 @@
     kept = (zeros, zeros)
     for part in range(PARTS):
         copies[part].wait()
-        kept = lax.fori_loop(part * MEMBERS // PARTS, (part + 1) * MEMBERS // PARTS, member, kept)
+        rows = range(part * MEMBERS // PARTS, (part + 1) * MEMBERS // PARTS)
+        for e in rows:
+            kept = member(e, kept)
     hand_out(TRACER_LANES, *kept)
     for copy in copies[PARTS:]:
         copy.wait()
@@ -87,102 +89,177 @@
     hand_out(STATIC_LANES, *kept)
 
 
-def halos(off_chip, on_chip):
-    odd = lax.axis_index("tile") % 2 == 1
-    one, other = on_chip[...], off_chip[...]
-    return jnp.where(odd, one, other), jnp.where(odd, other, one)
-
-
-def from_west(tiles):
+def sides(sent_off, sent_on, off_chip, on_chip, lanes):
+    odd_block = lax.axis_index("tile") % 2 == 1
+    off, on = off_chip[:, lanes], on_chip[:, lanes]
+    west, east = jnp.where(odd_block, on, off), jnp.where(odd_block, off, on)
+    off, on = sent_off[:, lanes], sent_on[:, lanes]
+    own_first, own_last = jnp.where(odd_block, on, off), jnp.where(odd_block, off, on)
+    odd = lane_index((ROWS, LANES)) % 2 == 1
+    inner = jnp.where(odd, pltpu.roll(own_first, 1, 1), pltpu.roll(own_last, LANES - 1, 1))
+    outer = jnp.where(odd, pltpu.roll(west, 1, 1), pltpu.roll(east, LANES - 1, 1))
+    return inner, jnp.where(odd, west, east), outer
+
+
+def repeated(block, start, width):
     lane = lane_index((ROWS, LANES))
-    turned = [pltpu.roll(tile, 1, 1) for tile in tiles]
-    return [jnp.where(lane == 0, turned[i - 1], turned[i]) for i in range(3)]
-
-
-def from_east(tiles):
+    if start:
+        block = pltpu.roll(block, LANES - start, 1)
+    block = jnp.where(lane < width, block, 0.0)
+    while width < LANES:
+        block = block + pltpu.roll(block, width, 1)
+        width *= 2
+    return block
+
+
+def face(wet, speed, diffuse):
+    a = 0.5 * (speed[0] + speed[1])
+    k = 0.5 * (diffuse[0] + diffuse[1])
+    ocean = wet[0] * wet[1]
+    return ocean * (jnp.maximum(a, 0.0) + k), ocean * (jnp.minimum(a, 0.0) - k)
+
+
+def rows_between(wet, diffuse):
+    row = lax.broadcasted_iota(jnp.int32, (ROWS, LANES), 0)
+    both = wet * pltpu.roll(wet, ROWS - 1, 0)
+    k = 0.5 * (diffuse + pltpu.roll(diffuse, ROWS - 1, 0))
+    north = jnp.where(row < ROWS - 1, both * k, 0.0)
+    return pltpu.roll(north, 1, 0), north
+
+
+def five_point(weights, cell, west, east):
+    centre, to_west, to_east, above, north = weights
+    return (
+        centre * cell
+        + to_west * west
+        + to_east * east
+        + above * pltpu.roll(cell, 1, 0)
+        + north * pltpu.roll(cell, ROWS - 1, 0)
+    )
+
+
+def border(edges):
+    odd = lane_index((ROWS, LANES)) % 2 == 1
+    inner, cell, outer = sides(*edges, TRACER_LANES)
+    statics = sides(*edges, STATIC_LANES)
+    diffuse = [repeated(x, 0, 2 * LEVELS) for x in statics]
+    speed = [repeated(x, 2 * LEVELS, 2 * LEVELS) for x in statics]
+    wet = [repeated(x, 4 * LEVELS, 2) for x in statics]
+    in_west, in_east = face(wet[:2], speed[:2], diffuse[:2])
+    out_west, out_east = face(wet[1:], speed[1:], diffuse[1:])
+    above, north = rows_between(wet[1], diffuse[1])
+    zonal = jnp.where(odd, out_east - in_west, in_east - out_west)
+    centre = 1.0 + (zonal - above - north) * wet[1]
+    to_inner = jnp.where(odd, -in_east, in_west)
+    to_outer = jnp.where(odd, out_west, -out_east)
+    stepped = five_point((centre, to_inner, to_outer, above, north), cell, inner, outer)
+    return cell, stepped
+
+
+def neighbours(tiles, halo):
+    return bordered(
+        [pltpu.roll(tile, 1, 1) for tile in tiles],
+        [pltpu.roll(tile, LANES - 1, 1) for tile in tiles],
+        halo,
+    )
+
+
+def bordered(west, east, halo):
     lane = lane_index((ROWS, LANES))
-    turned = [pltpu.roll(tile, LANES - 1, 1) for tile in tiles]
-    return [jnp.where(lane == LANES - 1, turned[(i + 1) % 3], turned[i]) for i in range(3)]
-
-
-def halo_tile(west, east, index):
-    lane = lane_index((ROWS, LANES))
-    east = pltpu.roll(east, (LANES - 2 * index) % LANES, 1)
-    west = pltpu.roll(west, LANES - 2 - 2 * index, 1)
-    return jnp.where(lane < 2, east, jnp.where(lane >= LANES - 2, west, 0.0))
-
-
-def widened(block, west_halo, east_halo, lanes, index):
-    halo = halo_tile(west_halo[:, lanes], east_halo[:, lanes], index)
-    return [block[:, :LANES], block[:, LANES:], halo]
-
-
-def stepper(level, statics, wet, west_halo, east_halo):
-    row = lax.broadcasted_iota(jnp.int32, (ROWS, LANES), 0)
-    halos = (west_halo, east_halo, STATIC_LANES)
-    ocean = widened(wet[...].astype(jnp.float32), *halos, 2 * LEVELS)
-    diffuse = widened(statics[level], *halos, level)
-    speed = widened(statics[LEVELS + level], *halos, LEVELS + level)
-    ocean_west, diffuse_west, speed_west = map(from_west, (ocean, diffuse, speed))
-    face_west, face_east, north = [], [], []
-    for i in range(3):
-        face = ocean_west[i] * ocean[i]
-        a = 0.5 * (speed_west[i] + speed[i])
-        k = 0.5 * (diffuse_west[i] + diffuse[i])
-        face_west.append(face * (jnp.maximum(a, 0.0) + k))
-        face_east.append(face * (jnp.minimum(a, 0.0) - k))
-        k = 0.5 * (diffuse[i] + pltpu.roll(diffuse[i], ROWS - 1, 0))
-        both = ocean[i] * pltpu.roll(ocean[i], ROWS - 1, 0)
-        north.append(jnp.where(row < ROWS - 1, both * k, 0.0))
-    next_west, next_east = from_east(face_west), from_east(face_east)
-    above = [pltpu.roll(x, 1, 0) for x in north]
-    centre = [
-        1.0 + (face_east[i] - next_west[i] - above[i] - north[i]) * ocean[i] for i in range(3)
-    ]
-
-    def advance(tiles, count):
-        west, east = from_west(tiles), from_east(tiles)
-        return [
-            centre[i] * tiles[i]
-            + face_west[i] * west[i]
-            - next_east[i] * east[i]
-            + above[i] * pltpu.roll(tiles[i], 1, 0)
-            + north[i] * pltpu.roll(tiles[i], ROWS - 1, 0)
-            for i in range(count)
-        ]
-
-    return lambda tiles: advance(advance(tiles, 3), 2)
-
-
-def transport(state, statics, wet, off_chip, on_chip, chunks):
-    west_halo, east_halo = halos(off_chip, on_chip)
+    first, last = lane == 0, lane == LANES - 1
+    west = [jnp.where(first, halo, west[0]), jnp.where(first, west[0], west[1])]
+    return west, [jnp.where(last, east[1], east[0]), jnp.where(last, halo, east[1])]
+
+
+def turns():
+    row = lax.broadcasted_iota(jnp.int32, (2 * LANES, 2 * LANES), 0)
+    column = lax.broadcasted_iota(jnp.int32, (2 * LANES, 2 * LANES), 1)
+    source = jnp.where(column < LANES, column + LANES - 1, column + 1) % LANES
+    return (row % LANES == source).astype(jnp.bfloat16)
+
+
+def split(block):
+    high = block.astype(jnp.bfloat16)
+    return high, (block - high.astype(jnp.float32)).astype(jnp.bfloat16)
+
+
+def aligned(block, index):
+    return pltpu.roll(block, LANES - 1 - 2 * index, 1)
+
+
+def halved(block):
+    return [block[:, :LANES], block[:, LANES:]]
+
+
+def stepper(level, statics, wet, edges):
+    cells = sides(*edges, STATIC_LANES)[1]
+    ocean = halved(wet[...].astype(jnp.float32))
+    diffuse, speed = halved(statics[level]), halved(statics[LEVELS + level])
+    (wet_west, wet_east), (diffuse_west, diffuse_east), (speed_west, speed_east) = (
+        neighbours(tiles, aligned(cells, index))
+        for tiles, index in ((ocean, 2 * LEVELS), (diffuse, level), (speed, LEVELS + level))
+    )
+    weights = []
+    for i in range(2):
+        west = face((wet_west[i], ocean[i]), (speed_west[i], speed[i]), (diffuse_west[i], diffuse[i]))
+        east = face((ocean[i], wet_east[i]), (speed[i], speed_east[i]), (diffuse[i], diffuse_east[i]))
+        above, north = rows_between(ocean[i], diffuse[i])
+        centre = 1.0 + (west[1] - east[0] - above - north) * ocean[i]
+        weights.append((centre, west[0], -east[1], above, north))
+
+    return weights
+
+
+def two_steps(weights, turn, planes, borders):
+    count = len(planes)
+    for halos in borders:
+        stacked = jnp.concatenate([tiles[half] for half in range(2) for tiles in planes], 0)
+        moved = jnp.dot(
+            jnp.concatenate(split(stacked), 1), turn, preferred_element_type=jnp.float32
+        )
+        stepped = []
+        for i in range(count):
+            turned = [
+                halved(moved[(half * count + i) * ROWS : (half * count + i + 1) * ROWS])
+                for half in range(2)
+            ]
+            west, east = bordered(*zip(*turned), halos[i])
+            stepped.append(
+                [five_point(weights[h], planes[i][h], west[h], east[h]) for h in range(2)]
+            )
+        planes = stepped
+    return planes
+
+
+def transport(state, statics, wet, sent_off, sent_on, off_chip, on_chip, sides_of, chunks):
+    edges = (sent_off, sent_on, off_chip, on_chip)
+    borders = (sides_of[:ROWS], sides_of[ROWS:])
+    turn = turns()
 
     def level_step(level, carry):
-        steps = stepper(level, statics, wet, west_halo, east_halo)
-
-        def member_step(e, carry):
-            for tracer in range(2):
-                q = tracer * LEVELS + level
-                done = steps(
-                    widened(state[e, q], west_halo, east_halo, TRACER_LANES, e * PLANES + q)
-                )
-                for half in range(2):
-                    rows = pl.ds(half * HALF_ROWS + e, ROWS, stride=MEMBERS)
-                    chunks[q, rows, :] = done[half]
-            return carry
-
-        return lax.fori_loop(0, MEMBERS, member_step, carry, unroll=4)
+        weights = stepper(level, statics, wet, edges)
+        where = [(e, t * LEVELS + level) for e in range(MEMBERS) for t in range(2)]
+        planes = [halved(state[e, q]) for e, q in where]
+        halos = [[aligned(block, e * PLANES + q) for e, q in where] for block in borders]
+        for (e, q), done in zip(where, two_steps(weights, turn, planes, halos)):
+            for half in range(2):
+                rows = pl.ds(half * HALF_ROWS + e, ROWS, stride=MEMBERS)
+                chunks[q, rows, :] = done[half]
+        return carry
 
     lax.fori_loop(0, LEVELS, level_step, 0)
 
 
-def observe(state, statics, wet, off_chip, on_chip, cell, value, error, count, out):
-    west_halo, east_halo = halos(off_chip, on_chip)
-    steps = stepper(0, statics, wet, west_halo, east_halo)
-    surface = []
-    for e in range(MEMBERS):
-        done = steps(widened(state[e, 0], west_halo, east_halo, TRACER_LANES, e * PLANES))
-        surface.append(jnp.concatenate(done, 1))
+def observe(
+    state, statics, wet, sent_off, sent_on, off_chip, on_chip, cell, value, error, count, out, sides_of
+):
+    edges = (sent_off, sent_on, off_chip, on_chip)
+    borders = border(edges)
+    sides_of[:ROWS], sides_of[ROWS:] = borders
+    weights = stepper(0, statics, wet, edges)
+    planes = [halved(state[e, 0]) for e in range(MEMBERS)]
+    halos = [[aligned(block, e * PLANES) for e in range(MEMBERS)] for block in borders]
+    surface = [jnp.concatenate(x, 1) for x in two_steps(weights, turns(), planes, halos)]
     in_use = (lane_index((1, SLOTS)) < count[0]).astype(jnp.float32)
     scale = 1.0 / ((ENSEMBLE - 1) * error[...])
     unused = jnp.zeros((5, SLOTS), jnp.float32)
@@ -298,15 +375,16 @@
     system = identity + gram(received, (own, off_chip, on_chip))
     solved = inverse([system[8 * t : 8 * t + 8] for t in range(SYSTEM_ROWS // 8)])
     weights = 0.5 * (identity + solved)[:ENSEMBLE] - solved[ENSEMBLE : ENSEMBLE + 1]
-    weights = weights[:, :ENSEMBLE]
+    high, low = split(weights[:, :ENSEMBLE])
+    weights = jnp.concatenate([high, low, high], 1)
     for r in range(ROWS):
         halves = [
             received[:, first : first + MEMBERS, :].reshape(ENSEMBLE, LANES)
             for first in (r * MEMBERS, HALF_ROWS + r * MEMBERS)
         ]
+        high, low = split(jnp.concatenate(halves, 1))
         result = jnp.dot(
-            weights, jnp.concatenate(halves, 1), precision=HIGHEST,
-            preferred_element_type=jnp.float32,
+            weights, jnp.concatenate([high, high, low], 0), preferred_element_type=jnp.float32
         )
         for m in range(ENSEMBLE // MEMBERS):
             rows = result[m * MEMBERS : (m + 1) * MEMBERS]
@@ -391,12 +469,16 @@
         fetched=(member_tracer_state, diffusivity, velocity, wet_mask, *slot_rows),
         scratch=[pltpu.SemaphoreType.DMA((PARTS + 6,))],
     )
-    edges = both_neighbours(off_chip, on_chip)
-    (own,) = kernel(
-        observe, (*blocks, *edges, cell, value, error), (2 * MEMBERS, SLOTS), scalars=(obs_count,)
+    edges = (off_chip, on_chip, *both_neighbours(off_chip, on_chip))
+    own, sides_of = kernel(
+        observe,
+        (*blocks, *edges, cell, value, error),
+        (2 * MEMBERS, SLOTS),
+        (2 * ROWS, LANES),
+        scalars=(obs_count,),
     )
     near = (own, *both_neighbours(own, own))
-    (chunks,) = kernel(transport, (*blocks, *edges), (PLANES, CHUNK_ROWS, LANES))
+    (chunks,) = kernel(transport, (*blocks, *edges, sides_of), (PLANES, CHUNK_ROWS, LANES))
     (chunks,) = kernel(attach, (chunks, *near), chunks.shape, aliases={0: 0})
     received = exchanged(chunks)
     (updated,) = kernel(analyse, (received, *near), (PLANES, CELL_ROWS, LANES))

time: 68.9 us -> 69.3 us (level)
  Pallas kernels: 13.2 us -> 10.1 us
  blocking collectives: 32.2 us -> 34.5 us
  waiting for transfers between devices: 0.5 us -> 1.56 us
    pallas_call x6, Pallas kernels: 13.2 us -> 10.1 us  [kernel(): pl.pallas_call(body, out_shape=shapes, in_specs=[vmem()] * len(operands)...]
    all_to_all x2, blocking collectives: 32.2 us -> 34.5 us  [exchanged(): return lax.all_to_all(value, 'mem', split_axis=0, concat_axis=0, tiled=True)]
    ppermute x4, waiting for transfers between devices: 0.5 us -> 1.56 us  [swapped(): return lax.ppermute(value, 'tile', pairs + [(b, a) for a, b in pairs])]
  transfers between devices with their start and end apart: 4 -> 4, of which waited for: 1 -> 2; matrix products, arithmetic and copies ran while one was open for 0% -> 0% of each run, Pallas kernels for 7% -> 3%
where the time goes in v4:
time: 69.3 us; the launch traced here: 69 us
  blocking collectives  34.5 us (50%)
  starting transfers between devices  22 us (32%)
  Pallas kernels  10.1 us (15%)
  waiting for transfers between devices  1.56 us (2%)
  between operations  0.73 us (1%)
    all_to_all x2, blocking collectives, exchanged(): return lax.all_to_all(value, 'mem', split_axis=0, concat_axis=0, tiled=True)  34.5 us
    ppermute x4, starting transfers between devices, swapped(): return lax.ppermute(value, 'tile', pairs + [(b, a) for a, b in pairs])  22 us
    pallas_call x6, Pallas kernels, kernel(): pl.pallas_call(body, out_shape=shapes, in_specs=[vmem()] * len(operands)...  10.1 us
    ppermute x4, waiting for transfers between devices, swapped(): return lax.ppermute(value, 'tile', pairs + [(b, a) for a, b in pairs])  1.56 us
  transfers between devices with their start and end apart: 4, of which 2 were waited for; matrix products, arithmetic and copies ran while one was open for 0% of the time, Pallas kernels for 3%

profile of v4, /device:TPU:8, one launch (start us, length us, event | category | flops | bytes accessed | tf_op | source)
XLA Modules:
  0.0 69.0 jit_solution(14144327380150620866)
XLA Ops:
  0.0 1.7 %pack_edges.1 = (f32[16,256]{1,0:T(8,128)S(1)}, f32[16,256]{1,0:T(8,128)S(1)}, f32[8,8,16,256]{3,2,1,0:T(8,128)S(1)}, f32[8,16,256]{2,1,0:T(8,128)S(1)}, s32[16,...) custom-call(f32[8,8,16,256]{3,2,1,0:T(8,128)} %state.1, ...), custom_call_target="tpu_custom_call" | custom-call | tf_op jit(solution)/shard_map/pack_edges/pallas_call | solution.py:425
  1.7 12.6 %collective-permute-start = (f32[16,256]{1,0:T(8,128)S(1)}, f32[16,256]{1,0:T(8,128)S(1)}, u32[]{:S(2)}, u32[]{:S(2)}) collective-permute-start(f32[16,256]{1,0:T(8,128)S(1)} %get-tuple-element.18.sent_off), channel_id=1, source_target_pairs={{8,16},{24,32},{40,48},{56,64},{72,80},{88,96},{104,112},{120,128}... | collective-permute-start | bytes 49160 | tf_op jit(solution)/shard_map/ppermute | solution.py:442
  14.3 1.9 %collective-permute-start.1 = (f32[16,256]{1,0:T(8,128)S(1)}, f32[16,256]{1,0:T(8,128)S(1)}, u32[]{:S(2)}, u32[]{:S(2)}) collective-permute-start(f32[16,256]{1,0:T(8,128)S(1)} %get-tuple-element.19.sent_on), channel_id=1, source_target_pairs={{0,8},{16,24},{32,40},{48,56},{64,72},{80,88},{96,104},{112,120},{... | collective-permute-start | bytes 49160 | tf_op jit(solution)/shard_map/ppermute | solution.py:442
  16.9 0.0 collective-permute-done.off_chip
  16.9 0.5 collective-permute-done.1.on_chip
  17.4 0.9 %observe.1 = (f32[16,128]{1,0:T(8,128)S(1)}, f32[32,128]{1,0:T(8,128)S(1)}) custom-call(f32[8,8,16,256]{3,2,1,0:T(8,128)S(1)} %get-tuple-element.15.state, f32[8,16,256]{2,1,0:T(8,128)S(1)} %get-tuple-element.16.statics, s32[16,256]{1,0:T(8,128)S(1)} %get-tuple-element.17.wet, f32[16,256]{1,0:T(8,128)S(1)} %get-tuple-element.18.sent_off, ...), custom_call_target="tpu_custom_call" | custom-call | tf_op jit(solution)/shard_map/observe/pallas_call | solution.py:425
  18.3 2.1 %collective-permute-start.3 = (f32[16,128]{1,0:T(8,128)S(1)}, f32[16,128]{1,0:T(8,128)S(1)}, u32[]{:S(2)}, u32[]{:S(2)}) collective-permute-start(f32[16,128]{1,0:T(8,128)S(1)} %get-tuple-element.24.own), channel_id=1, source_target_pairs={{0,8},{16,24},{32,40},{48,56},{64,72},{80,88},{96,104},{112,120},{... | collective-permute-start | bytes 24584 | tf_op jit(solution)/shard_map/ppermute | solution.py:442
  20.4 5.4 %collective-permute-start.2 = (f32[16,128]{1,0:T(8,128)S(1)}, f32[16,128]{1,0:T(8,128)S(1)}, u32[]{:S(2)}, u32[]{:S(2)}) collective-permute-start(f32[16,128]{1,0:T(8,128)S(1)} %get-tuple-element.24.own), channel_id=1, source_target_pairs={{8,16},{24,32},{40,48},{56,64},{72,80},{88,96},{104,112},{120,128}... | collective-permute-start | bytes 24584 | tf_op jit(solution)/shard_map/ppermute | solution.py:442
  25.8 2.2 %transport.1.chunks = f32[8,280,128]{2,1,0:T(8,128)S(1)} custom-call(f32[8,8,16,256]{3,2,1,0:T(8,128)S(1)} %get-tuple-element.15.state, f32[8,16,256]{2,1,0:T(8,128)S(1)} %get-tuple-element.16.statics, s32[16,256]{1,0:T(8,128)S(1)} %get-tuple-element.17.wet, f32[16,256]{1,0:T(8,128)S(1)} %get-tuple-element.18.sent_off, ...), custom_call_target="tpu_custom_call" | custom-call | tf_op jit(solution)/shard_map/transport/pallas_call | solution.py:425
  28.0 0.0 collective-permute-done.3.on_chip
  28.0 1.1 %collective-permute-done.2.off_chip = f32[16,128]{1,0:T(8,128)S(1)} collective-permute-done((f32[16,128]{1,0:T(8,128)S(1)}, f32[16,128]{1,0:T(8,128)S(1)}, u32[]{:S(2)}, u32[]{:S(2)}) %collective-permute-start.2) | collective-permute-done | bytes 8224 | tf_op jit(solution)/shard_map/ppermute | solution.py:442
  29.1 19.4 %all_to_all.10.received = f32[8,280,128]{2,1,0:T(8,128)S(1)} all-to-all(f32[8,280,128]{2,1,0:T(8,128)S(1)} %attach.1), channel_id=1, replica_groups=mesh['tile'=64,'mem'=8] {'mem'}, dimensions={0} | all-to-all | bytes 2293760 | tf_op jit(solution)/shard_map/all_to_all | solution.py:451
  48.5 4.3 %analyse.1 = f32[8,256,128]{2,1,0:T(8,128)S(1)} custom-call(f32[8,280,128]{2,1,0:T(8,128)S(1)} %all_to_all.10.received, f32[16,128]{1,0:T(8,128)S(1)} %get-tuple-element.24.own, f32[16,128]{1,0:T(8,128)S(1)} %collective-permute-done.2.off_chip, f32[16,128]{1,0:T(8,128)S(1)} %collective-permute-done.3.on_chip), custom_call_target="tpu_custom_call" | custom-call | tf_op jit(solution)/shard_map/analyse/pallas_call | solution.py:425
  52.8 15.1 %all_to_all.11 = f32[8,256,128]{2,1,0:T(8,128)S(1)} all-to-all(f32[8,256,128]{2,1,0:T(8,128)S(1)} %analyse.1), channel_id=1, replica_groups=mesh['tile'=64,'mem'=8] {'mem'}, dimensions={0} | all-to-all | bytes 2097152 | tf_op jit(solution)/shard_map/all_to_all | solution.py:451
  67.9 1.1 %unpack.1 = f32[8,8,16,256]{3,2,1,0:T(8,128)} custom-call(f32[8,2,8,16,128]{4,3,2,1,0:T(8,128)S(1)} %bitcast.4), custom_call_target="tpu_custom_call" | custom-call | tf_op jit(solution)/shard_map/unpack/pallas_call | solution.py:425
  (1 shorter events, 0.0 us)
Async XLA Ops:
  1.7 15.2 %collective-permute-start = (f32[16,256]{1,0:T(8,128)S(1)}, f32[16,256]{1,0:T(8,128)S(1)}, u32[]{:S(2)}, u32[]{:S(2)}) collective-permute-start(f32[16,256]{1,0:T(8,128)S(1)} %get-tuple-element.18.sent_off), channel_id=1, source_target_pairs={{8,16},{24,32},{40,48},{56,64},{72,80},{88,96},{104,112},{120,128}... | collective-permute-start | bytes 49160 | tf_op jit(solution)/shard_map/ppermute | solution.py:442
  14.3 3.1 %collective-permute-start.1 = (f32[16,256]{1,0:T(8,128)S(1)}, f32[16,256]{1,0:T(8,128)S(1)}, u32[]{:S(2)}, u32[]{:S(2)}) collective-permute-start(f32[16,256]{1,0:T(8,128)S(1)} %get-tuple-element.19.sent_on), channel_id=1, source_target_pairs={{0,8},{16,24},{32,40},{48,56},{64,72},{80,88},{96,104},{112,120},{... | collective-permute-start | bytes 49160 | tf_op jit(solution)/shard_map/ppermute | solution.py:442
  18.3 9.7 %collective-permute-start.3 = (f32[16,128]{1,0:T(8,128)S(1)}, f32[16,128]{1,0:T(8,128)S(1)}, u32[]{:S(2)}, u32[]{:S(2)}) collective-permute-start(f32[16,128]{1,0:T(8,128)S(1)} %get-tuple-element.24.own), channel_id=1, source_target_pairs={{0,8},{16,24},{32,40},{48,56},{64,72},{80,88},{96,104},{112,120},{... | collective-permute-start | bytes 24584 | tf_op jit(solution)/shard_map/ppermute | solution.py:442
  20.4 8.7 %collective-permute-start.2 = (f32[16,128]{1,0:T(8,128)S(1)}, f32[16,128]{1,0:T(8,128)S(1)}, u32[]{:S(2)}, u32[]{:S(2)}) collective-permute-start(f32[16,128]{1,0:T(8,128)S(1)} %get-tuple-element.24.own), channel_id=1, source_target_pairs={{8,16},{24,32},{40,48},{56,64},{72,80},{88,96},{104,112},{120,128}... | collective-permute-start | bytes 24584 | tf_op jit(solution)/shard_map/ppermute | solution.py:442

commit v5 on v4

--- a/solution.py
+++ b/solution.py
@@ -231,7 +231,7 @@
     return planes
 
 
-def transport(state, statics, wet, sent_off, sent_on, off_chip, on_chip, sides_of, chunks):
+def forecast(state, statics, wet, sent_off, sent_on, off_chip, on_chip, sides_of, chunks):
     edges = (sent_off, sent_on, off_chip, on_chip)
     borders = (sides_of[:ROWS], sides_of[ROWS:])
     turn = turns()
@@ -248,6 +248,17 @@
         return carry
 
     lax.fori_loop(0, LEVELS, level_step, 0)
+
+
+def far():
+    place = lax.axis_index("tile") % 4
+    return (place == 0) | (place == 3)
+
+
+def transport(*refs):
+    @pl.when(jnp.logical_not(far()))
+    def _():
+        forecast(*refs)
 
 
 def observe(
@@ -277,7 +288,13 @@
         out[e : e + 1, :] = jnp.sum(kept, 0, keepdims=True)
 
 
-def attach(chunks, own, off_chip, on_chip, out):
+def attach(chunks, own, off_chip, on_chip, *rest):
+    out = rest[-1]
+
+    @pl.when(far())
+    def _():
+        forecast(*rest)
+
     for i, block in enumerate((own, off_chip, on_chip)):
         values = block[:MEMBERS]
         for q in range(PLANES):
@@ -478,8 +495,9 @@
         scalars=(obs_count,),
     )
     near = (own, *both_neighbours(own, own))
-    (chunks,) = kernel(transport, (*blocks, *edges, sides_of), (PLANES, CHUNK_ROWS, LANES))
-    (chunks,) = kernel(attach, (chunks, *near), chunks.shape, aliases={0: 0})
+    home = (*blocks, *edges, sides_of)
+    (chunks,) = kernel(transport, home, (PLANES, CHUNK_ROWS, LANES))
+    (chunks,) = kernel(attach, (chunks, *near, *home), chunks.shape, aliases={0: 0})
     received = exchanged(chunks)
     (updated,) = kernel(analyse, (received, *near), (PLANES, CELL_ROWS, LANES))
     back = exchanged(updated)

time: 69.3 us -> 68.2 us (0.984)
  blocking collectives: 34.5 us -> 31.4 us
  waiting for transfers between devices: 1.56 us -> 3.6 us
    all_to_all x2, blocking collectives: 34.5 us -> 31.4 us  [exchanged(): return lax.all_to_all(value, 'mem', split_axis=0, concat_axis=0, tiled=True)]
    ppermute x4, waiting for transfers between devices: 1.56 us -> 3.6 us  [swapped(): return lax.ppermute(value, 'tile', pairs + [(b, a) for a, b in pairs])]
  transfers between devices with their start and end apart: 4 -> 4, of which waited for: 2 -> 2; matrix products, arithmetic and copies ran while one was open for 0% -> 0% of each run, Pallas kernels for 3% -> 0%
where the time goes in v5:
time: 68.2 us; the launch traced here: 67.9 us
  blocking collectives  31.4 us (46%)
  starting transfers between devices  22 us (32%)
  Pallas kernels  10.2 us (15%)
  waiting for transfers between devices  3.6 us (5%)
  between operations  0.73 us (1%)
    all_to_all x2, blocking collectives, exchanged(): return lax.all_to_all(value, 'mem', split_axis=0, concat_axis=0, tiled=True)  31.4 us
    ppermute x4, starting transfers between devices, swapped(): return lax.ppermute(value, 'tile', pairs + [(b, a) for a, b in pairs])  22 us
    pallas_call x6, Pallas kernels, kernel(): pl.pallas_call(body, out_shape=shapes, in_specs=[vmem()] * len(operands)...  10.2 us
    ppermute x4, waiting for transfers between devices, swapped(): return lax.ppermute(value, 'tile', pairs + [(b, a) for a, b in pairs])  3.6 us
  transfers between devices with their start and end apart: 4, of which 2 were waited for; matrix products, arithmetic and copies ran while one was open for 0% of the time, Pallas kernels for 0%

profile of v5, /device:TPU:8, one launch (start us, length us, event | category | flops | bytes accessed | tf_op | source)
XLA Modules:
  0.0 67.9 jit_solution(16220434642234149573)
XLA Ops:
  0.0 1.7 %pack_edges.1 = (f32[16,256]{1,0:T(8,128)S(1)}, f32[16,256]{1,0:T(8,128)S(1)}, f32[8,8,16,256]{3,2,1,0:T(8,128)S(1)}, f32[8,16,256]{2,1,0:T(8,128)S(1)}, s32[16,...) custom-call(f32[8,8,16,256]{3,2,1,0:T(8,128)} %state.1, ...), custom_call_target="tpu_custom_call" | custom-call | tf_op jit(solution)/shard_map/pack_edges/pallas_call | solution.py:442
  1.7 12.6 %collective-permute-start = (f32[16,256]{1,0:T(8,128)S(1)}, f32[16,256]{1,0:T(8,128)S(1)}, u32[]{:S(2)}, u32[]{:S(2)}) collective-permute-start(f32[16,256]{1,0:T(8,128)S(1)} %get-tuple-element.18.sent_off.refs_3_.rest_3_), channel_id=1, source_target_pairs={{8,16},{24,32},{40,48},{56,64},{72,80},{88,96},{104,112},{120,128}... | collective-permute-start | bytes 49160 | tf_op jit(solution)/shard_map/ppermute | solution.py:459
  14.3 1.9 %collective-permute-start.1 = (f32[16,256]{1,0:T(8,128)S(1)}, f32[16,256]{1,0:T(8,128)S(1)}, u32[]{:S(2)}, u32[]{:S(2)}) collective-permute-start(f32[16,256]{1,0:T(8,128)S(1)} %get-tuple-element.19.sent_on.refs_4_.rest_4_), channel_id=1, source_target_pairs={{0,8},{16,24},{32,40},{48,56},{64,72},{80,88},{96,104},{112,120},{... | collective-permute-start | bytes 49160 | tf_op jit(solution)/shard_map/ppermute | solution.py:459
  16.9 0.0 collective-permute-done.off_chip.refs_5_.rest_5_
  16.9 0.5 collective-permute-done.1.on_chip.refs_6_.rest_6_
  17.4 0.9 %observe.1 = (f32[16,128]{1,0:T(8,128)S(1)}, f32[32,128]{1,0:T(8,128)S(1)}) custom-call(f32[8,8,16,256]{3,2,1,0:T(8,128)S(1)} %get-tuple-element.15.state.refs_0_.rest_0_, f32[8,16,256]{2,1,0:T(8,128)S(1)} %get-tuple-element.16.statics.refs_1_.rest_1_, s32[16,256]{1,0:T(8,128)S(1)} %get-tuple-element.17.wet.refs_2_.rest_2_, ...), custom_call_target="tpu_custom_call" | custom-call | tf_op jit(solution)/shard_map/observe/pallas_call | solution.py:442
  18.3 2.1 %collective-permute-start.3 = (f32[16,128]{1,0:T(8,128)S(1)}, f32[16,128]{1,0:T(8,128)S(1)}, u32[]{:S(2)}, u32[]{:S(2)}) collective-permute-start(f32[16,128]{1,0:T(8,128)S(1)} %get-tuple-element.24.own), channel_id=1, source_target_pairs={{0,8},{16,24},{32,40},{48,56},{64,72},{80,88},{96,104},{112,120},{... | collective-permute-start | bytes 24584 | tf_op jit(solution)/shard_map/ppermute | solution.py:459
  20.4 5.4 %collective-permute-start.2 = (f32[16,128]{1,0:T(8,128)S(1)}, f32[16,128]{1,0:T(8,128)S(1)}, u32[]{:S(2)}, u32[]{:S(2)}) collective-permute-start(f32[16,128]{1,0:T(8,128)S(1)} %get-tuple-element.24.own), channel_id=1, source_target_pairs={{8,16},{24,32},{40,48},{56,64},{72,80},{88,96},{104,112},{120,128}... | collective-permute-start | bytes 24584 | tf_op jit(solution)/shard_map/ppermute | solution.py:459
  25.9 0.0 collective-permute-done.3.on_chip
  25.9 3.1 %collective-permute-done.2.off_chip = f32[16,128]{1,0:T(8,128)S(1)} collective-permute-done((f32[16,128]{1,0:T(8,128)S(1)}, f32[16,128]{1,0:T(8,128)S(1)}, u32[]{:S(2)}, u32[]{:S(2)}) %collective-permute-start.2) | collective-permute-done | bytes 8224 | tf_op jit(solution)/shard_map/ppermute | solution.py:459
  29.0 2.2 %attach.1 = f32[8,280,128]{2,1,0:T(8,128)S(1)} custom-call(f32[8,280,128]{2,1,0:T(8,128)S(1)} %transport.1.chunks, f32[16,128]{1,0:T(8,128)S(1)} %get-tuple-element.24.own, f32[16,128]{1,0:T(8,128)S(1)} %collective-permute-done.2.off_chip, f32[16,128]{1,0:T(8,128)S(1)} %collective-permute-done.3.on_chip, ...), custom_call_target="tpu_custom_call", output_to_operand_aliasing={{}: (0, {})} | custom-call | tf_op jit(solution)/shard_map/attach/pallas_call | solution.py:442
  31.1 17.4 %all_to_all.10.received = f32[8,280,128]{2,1,0:T(8,128)S(1)} all-to-all(f32[8,280,128]{2,1,0:T(8,128)S(1)} %attach.1), channel_id=1, replica_groups=mesh['tile'=64,'mem'=8] {'mem'}, dimensions={0} | all-to-all | bytes 2293760 | tf_op jit(solution)/shard_map/all_to_all | solution.py:468
  48.5 4.3 %analyse.1 = f32[8,256,128]{2,1,0:T(8,128)S(1)} custom-call(f32[8,280,128]{2,1,0:T(8,128)S(1)} %all_to_all.10.received, f32[16,128]{1,0:T(8,128)S(1)} %get-tuple-element.24.own, f32[16,128]{1,0:T(8,128)S(1)} %collective-permute-done.2.off_chip, f32[16,128]{1,0:T(8,128)S(1)} %collective-permute-done.3.on_chip), custom_call_target="tpu_custom_call" | custom-call | tf_op jit(solution)/shard_map/analyse/pallas_call | solution.py:442
  52.8 14.0 %all_to_all.11 = f32[8,256,128]{2,1,0:T(8,128)S(1)} all-to-all(f32[8,256,128]{2,1,0:T(8,128)S(1)} %analyse.1), channel_id=1, replica_groups=mesh['tile'=64,'mem'=8] {'mem'}, dimensions={0} | all-to-all | bytes 2097152 | tf_op jit(solution)/shard_map/all_to_all | solution.py:468
  66.8 1.1 %unpack.1 = f32[8,8,16,256]{3,2,1,0:T(8,128)} custom-call(f32[8,2,8,16,128]{4,3,2,1,0:T(8,128)S(1)} %bitcast.4), custom_call_target="tpu_custom_call" | custom-call | tf_op jit(solution)/shard_map/unpack/pallas_call | solution.py:442
  (1 shorter events, 0.0 us)
Async XLA Ops:
  1.7 15.2 %collective-permute-start = (f32[16,256]{1,0:T(8,128)S(1)}, f32[16,256]{1,0:T(8,128)S(1)}, u32[]{:S(2)}, u32[]{:S(2)}) collective-permute-start(f32[16,256]{1,0:T(8,128)S(1)} %get-tuple-element.18.sent_off.refs_3_.rest_3_), channel_id=1, source_target_pairs={{8,16},{24,32},{40,48},{56,64},{72,80},{88,96},{104,112},{120,128}... | collective-permute-start | bytes 49160 | tf_op jit(solution)/shard_map/ppermute | solution.py:459
  14.3 3.1 %collective-permute-start.1 = (f32[16,256]{1,0:T(8,128)S(1)}, f32[16,256]{1,0:T(8,128)S(1)}, u32[]{:S(2)}, u32[]{:S(2)}) collective-permute-start(f32[16,256]{1,0:T(8,128)S(1)} %get-tuple-element.19.sent_on.refs_4_.rest_4_), channel_id=1, source_target_pairs={{0,8},{16,24},{32,40},{48,56},{64,72},{80,88},{96,104},{112,120},{... | collective-permute-start | bytes 49160 | tf_op jit(solution)/shard_map/ppermute | solution.py:459
  18.3 7.6 %collective-permute-start.3 = (f32[16,128]{1,0:T(8,128)S(1)}, f32[16,128]{1,0:T(8,128)S(1)}, u32[]{:S(2)}, u32[]{:S(2)}) collective-permute-start(f32[16,128]{1,0:T(8,128)S(1)} %get-tuple-element.24.own), channel_id=1, source_target_pairs={{0,8},{16,24},{32,40},{48,56},{64,72},{80,88},{96,104},{112,120},{... | collective-permute-start | bytes 24584 | tf_op jit(solution)/shard_map/ppermute | solution.py:459
  20.4 8.6 %collective-permute-start.2 = (f32[16,128]{1,0:T(8,128)S(1)}, f32[16,128]{1,0:T(8,128)S(1)}, u32[]{:S(2)}, u32[]{:S(2)}) collective-permute-start(f32[16,128]{1,0:T(8,128)S(1)} %get-tuple-element.24.own), channel_id=1, source_target_pairs={{8,16},{24,32},{40,48},{56,64},{72,80},{88,96},{104,112},{120,128}... | collective-permute-start | bytes 24584 | tf_op jit(solution)/shard_map/ppermute | solution.py:459

commit v6 on v5

--- a/solution.py
+++ b/solution.py
@@ -172,15 +172,18 @@
 
 
 def turns():
-    row = lax.broadcasted_iota(jnp.int32, (2 * LANES, 2 * LANES), 0)
-    column = lax.broadcasted_iota(jnp.int32, (2 * LANES, 2 * LANES), 1)
+    row = lax.broadcasted_iota(jnp.int32, (3 * LANES, 2 * LANES), 0)
+    column = lax.broadcasted_iota(jnp.int32, (3 * LANES, 2 * LANES), 1)
     source = jnp.where(column < LANES, column + LANES - 1, column + 1) % LANES
     return (row % LANES == source).astype(jnp.bfloat16)
 
 
-def split(block):
-    high = block.astype(jnp.bfloat16)
-    return high, (block - high.astype(jnp.float32)).astype(jnp.bfloat16)
+def split(block, count):
+    parts = []
+    for i in range(count):
+        parts.append(block.astype(jnp.bfloat16))
+        block = block - parts[-1].astype(jnp.float32)
+    return parts
 
 
 def aligned(block, index):
@@ -215,7 +218,7 @@
     for halos in borders:
         stacked = jnp.concatenate([tiles[half] for half in range(2) for tiles in planes], 0)
         moved = jnp.dot(
-            jnp.concatenate(split(stacked), 1), turn, preferred_element_type=jnp.float32
+            jnp.concatenate(split(stacked, 3), 1), turn, preferred_element_type=jnp.float32
         )
         stepped = []
         for i in range(count):
@@ -391,16 +394,20 @@
     identity = jnp.where(diagonal & (row < ENSEMBLE), 1.0, 0.0)
     system = identity + gram(received, (own, off_chip, on_chip))
     solved = inverse([system[8 * t : 8 * t + 8] for t in range(SYSTEM_ROWS // 8)])
-    weights = 0.5 * (identity + solved)[:ENSEMBLE] - solved[ENSEMBLE : ENSEMBLE + 1]
-    high, low = split(weights[:, :ENSEMBLE])
+    weights = 0.5 * (solved - identity)[:ENSEMBLE] - solved[ENSEMBLE : ENSEMBLE + 1]
+    high, low = split(weights[:, :ENSEMBLE], 2)
     weights = jnp.concatenate([high, low, high], 1)
     for r in range(ROWS):
-        halves = [
-            received[:, first : first + MEMBERS, :].reshape(ENSEMBLE, LANES)
-            for first in (r * MEMBERS, HALF_ROWS + r * MEMBERS)
-        ]
-        high, low = split(jnp.concatenate(halves, 1))
-        result = jnp.dot(
+        members = jnp.concatenate(
+            [
+                received[:, first : first + MEMBERS, :].reshape(ENSEMBLE, LANES)
+                for first in (r * MEMBERS, HALF_ROWS + r * MEMBERS)
+            ],
+            1,
+        )
+        mean = jnp.sum(members, 0, keepdims=True) / ENSEMBLE
+        high, low = split(members - mean, 2)
+        result = members + jnp.dot(
             weights, jnp.concatenate([high, high, low], 0), preferred_element_type=jnp.float32
         )
         for m in range(ENSEMBLE // MEMBERS):

time: 68.2 us -> 68.5 us (level)
  Pallas kernels: 10.2 us -> 11.4 us
  blocking collectives: 31.4 us -> 30.4 us
    pallas_call x6, Pallas kernels: 10.2 us -> 11.4 us  [kernel(): pl.pallas_call(body, out_shape=shapes, in_specs=[vmem()] * len(operands)...]
    all_to_all x2, blocking collectives: 31.4 us -> 30.4 us  [exchanged(): return lax.all_to_all(value, 'mem', split_axis=0, concat_axis=0, tiled=True)]
where the time goes in v6:
time: 68.5 us; the launch traced here: 68.2 us
  blocking collectives  30.4 us (44%)
  starting transfers between devices  22 us (32%)
  Pallas kernels  11.4 us (17%)
  waiting for transfers between devices  3.59 us (5%)
  between operations  0.73 us (1%)
    all_to_all x2, blocking collectives, exchanged(): return lax.all_to_all(value, 'mem', split_axis=0, concat_axis=0, tiled=True)  30.4 us
    ppermute x4, starting transfers between devices, swapped(): return lax.ppermute(value, 'tile', pairs + [(b, a) for a, b in pairs])  22 us
    pallas_call x6, Pallas kernels, kernel(): pl.pallas_call(body, out_shape=shapes, in_specs=[vmem()] * len(operands)...  11.4 us
    ppermute x4, waiting for transfers between devices, swapped(): return lax.ppermute(value, 'tile', pairs + [(b, a) for a, b in pairs])  3.59 us
  transfers between devices with their start and end apart: 4, of which 2 were waited for; matrix products, arithmetic and copies ran while one was open for 0% of the time, Pallas kernels for 0%

profile of v6, /device:TPU:8, one launch (start us, length us, event | category | flops | bytes accessed | tf_op | source)
XLA Modules:
  0.0 68.2 jit_solution(9353383252165751898)
XLA Ops:
  0.0 1.7 %pack_edges.1 = (f32[16,256]{1,0:T(8,128)S(1)}, f32[16,256]{1,0:T(8,128)S(1)}, f32[8,8,16,256]{3,2,1,0:T(8,128)S(1)}, f32[8,16,256]{2,1,0:T(8,128)S(1)}, s32[16,...) custom-call(f32[8,8,16,256]{3,2,1,0:T(8,128)} %state.1, ...), custom_call_target="tpu_custom_call" | custom-call | tf_op jit(solution)/shard_map/pack_edges/pallas_call | solution.py:449
  1.7 12.6 %collective-permute-start = (f32[16,256]{1,0:T(8,128)S(1)}, f32[16,256]{1,0:T(8,128)S(1)}, u32[]{:S(2)}, u32[]{:S(2)}) collective-permute-start(f32[16,256]{1,0:T(8,128)S(1)} %get-tuple-element.18.sent_off.refs_3_.rest_3_), channel_id=1, source_target_pairs={{8,16},{24,32},{40,48},{56,64},{72,80},{88,96},{104,112},{120,128}... | collective-permute-start | bytes 49160 | tf_op jit(solution)/shard_map/ppermute | solution.py:466
  14.3 1.9 %collective-permute-start.1 = (f32[16,256]{1,0:T(8,128)S(1)}, f32[16,256]{1,0:T(8,128)S(1)}, u32[]{:S(2)}, u32[]{:S(2)}) collective-permute-start(f32[16,256]{1,0:T(8,128)S(1)} %get-tuple-element.19.sent_on.refs_4_.rest_4_), channel_id=1, source_target_pairs={{0,8},{16,24},{32,40},{48,56},{64,72},{80,88},{96,104},{112,120},{... | collective-permute-start | bytes 49160 | tf_op jit(solution)/shard_map/ppermute | solution.py:466
  16.9 0.0 collective-permute-done.off_chip.refs_5_.rest_5_
  16.9 0.5 collective-permute-done.1.on_chip.refs_6_.rest_6_
  17.4 0.9 %observe.1 = (f32[16,128]{1,0:T(8,128)S(1)}, f32[32,128]{1,0:T(8,128)S(1)}) custom-call(f32[8,8,16,256]{3,2,1,0:T(8,128)S(1)} %get-tuple-element.15.state.refs_0_.rest_0_, f32[8,16,256]{2,1,0:T(8,128)S(1)} %get-tuple-element.16.statics.refs_1_.rest_1_, s32[16,256]{1,0:T(8,128)S(1)} %get-tuple-element.17.wet.refs_2_.rest_2_, ...), custom_call_target="tpu_custom_call" | custom-call | tf_op jit(solution)/shard_map/observe/pallas_call | solution.py:449
  18.3 2.1 %collective-permute-start.3 = (f32[16,128]{1,0:T(8,128)S(1)}, f32[16,128]{1,0:T(8,128)S(1)}, u32[]{:S(2)}, u32[]{:S(2)}) collective-permute-start(f32[16,128]{1,0:T(8,128)S(1)} %get-tuple-element.24.own), channel_id=1, source_target_pairs={{0,8},{16,24},{32,40},{48,56},{64,72},{80,88},{96,104},{112,120},{... | collective-permute-start | bytes 24584 | tf_op jit(solution)/shard_map/ppermute | solution.py:466
  20.4 5.4 %collective-permute-start.2 = (f32[16,128]{1,0:T(8,128)S(1)}, f32[16,128]{1,0:T(8,128)S(1)}, u32[]{:S(2)}, u32[]{:S(2)}) collective-permute-start(f32[16,128]{1,0:T(8,128)S(1)} %get-tuple-element.24.own), channel_id=1, source_target_pairs={{8,16},{24,32},{40,48},{56,64},{72,80},{88,96},{104,112},{120,128}... | collective-permute-start | bytes 24584 | tf_op jit(solution)/shard_map/ppermute | solution.py:466
  25.8 0.0 collective-permute-done.3.on_chip
  25.8 3.1 %collective-permute-done.2.off_chip = f32[16,128]{1,0:T(8,128)S(1)} collective-permute-done((f32[16,128]{1,0:T(8,128)S(1)}, f32[16,128]{1,0:T(8,128)S(1)}, u32[]{:S(2)}, u32[]{:S(2)}) %collective-permute-start.2) | collective-permute-done | bytes 8224 | tf_op jit(solution)/shard_map/ppermute | solution.py:466
  28.9 3.3 %attach.1 = f32[8,280,128]{2,1,0:T(8,128)S(1)} custom-call(f32[8,280,128]{2,1,0:T(8,128)S(1)} %transport.1.chunks, f32[16,128]{1,0:T(8,128)S(1)} %get-tuple-element.24.own, f32[16,128]{1,0:T(8,128)S(1)} %collective-permute-done.2.off_chip, f32[16,128]{1,0:T(8,128)S(1)} %collective-permute-done.3.on_chip, ...), custom_call_target="tpu_custom_call", output_to_operand_aliasing={{}: (0, {})} | custom-call | tf_op jit(solution)/shard_map/attach/pallas_call | solution.py:449
  32.3 16.4 %all_to_all.10.received = f32[8,280,128]{2,1,0:T(8,128)S(1)} all-to-all(f32[8,280,128]{2,1,0:T(8,128)S(1)} %attach.1), channel_id=1, replica_groups=mesh['tile'=64,'mem'=8] {'mem'}, dimensions={0} | all-to-all | bytes 2293760 | tf_op jit(solution)/shard_map/all_to_all | solution.py:475
  48.7 4.3 %analyse.1 = f32[8,256,128]{2,1,0:T(8,128)S(1)} custom-call(f32[8,280,128]{2,1,0:T(8,128)S(1)} %all_to_all.10.received, f32[16,128]{1,0:T(8,128)S(1)} %get-tuple-element.24.own, f32[16,128]{1,0:T(8,128)S(1)} %collective-permute-done.2.off_chip, f32[16,128]{1,0:T(8,128)S(1)} %collective-permute-done.3.on_chip), custom_call_target="tpu_custom_call" | custom-call | tf_op jit(solution)/shard_map/analyse/pallas_call | solution.py:449
  53.0 14.0 %all_to_all.11 = f32[8,256,128]{2,1,0:T(8,128)S(1)} all-to-all(f32[8,256,128]{2,1,0:T(8,128)S(1)} %analyse.1), channel_id=1, replica_groups=mesh['tile'=64,'mem'=8] {'mem'}, dimensions={0} | all-to-all | bytes 2097152 | tf_op jit(solution)/shard_map/all_to_all | solution.py:475
  67.1 1.1 %unpack.1 = f32[8,8,16,256]{3,2,1,0:T(8,128)} custom-call(f32[8,2,8,16,128]{4,3,2,1,0:T(8,128)S(1)} %bitcast.4), custom_call_target="tpu_custom_call" | custom-call | tf_op jit(solution)/shard_map/unpack/pallas_call | solution.py:449
  (1 shorter events, 0.0 us)
Async XLA Ops:
  1.7 15.2 %collective-permute-start = (f32[16,256]{1,0:T(8,128)S(1)}, f32[16,256]{1,0:T(8,128)S(1)}, u32[]{:S(2)}, u32[]{:S(2)}) collective-permute-start(f32[16,256]{1,0:T(8,128)S(1)} %get-tuple-element.18.sent_off.refs_3_.rest_3_), channel_id=1, source_target_pairs={{8,16},{24,32},{40,48},{56,64},{72,80},{88,96},{104,112},{120,128}... | collective-permute-start | bytes 49160 | tf_op jit(solution)/shard_map/ppermute | solution.py:466
  14.3 3.1 %collective-permute-start.1 = (f32[16,256]{1,0:T(8,128)S(1)}, f32[16,256]{1,0:T(8,128)S(1)}, u32[]{:S(2)}, u32[]{:S(2)}) collective-permute-start(f32[16,256]{1,0:T(8,128)S(1)} %get-tuple-element.19.sent_on.refs_4_.rest_4_), channel_id=1, source_target_pairs={{0,8},{16,24},{32,40},{48,56},{64,72},{80,88},{96,104},{112,120},{... | collective-permute-start | bytes 49160 | tf_op jit(solution)/shard_map/ppermute | solution.py:466
  18.3 7.6 %collective-permute-start.3 = (f32[16,128]{1,0:T(8,128)S(1)}, f32[16,128]{1,0:T(8,128)S(1)}, u32[]{:S(2)}, u32[]{:S(2)}) collective-permute-start(f32[16,128]{1,0:T(8,128)S(1)} %get-tuple-element.24.own), channel_id=1, source_target_pairs={{0,8},{16,24},{32,40},{48,56},{64,72},{80,88},{96,104},{112,120},{... | collective-permute-start | bytes 24584 | tf_op jit(solution)/shard_map/ppermute | solution.py:466
  20.4 8.6 %collective-permute-start.2 = (f32[16,128]{1,0:T(8,128)S(1)}, f32[16,128]{1,0:T(8,128)S(1)}, u32[]{:S(2)}, u32[]{:S(2)}) collective-permute-start(f32[16,128]{1,0:T(8,128)S(1)} %get-tuple-element.24.own), channel_id=1, source_target_pairs={{8,16},{24,32},{40,48},{56,64},{72,80},{88,96},{104,112},{120,128}... | collective-permute-start | bytes 24584 | tf_op jit(solution)/shard_map/ppermute | solution.py:466

commit v7 on v6

--- a/solution.py
+++ b/solution.py
@@ -214,22 +214,23 @@
 
 
 def two_steps(weights, turn, planes, borders):
-    count = len(planes)
+    count = len(planes) // 2
     for halos in borders:
-        stacked = jnp.concatenate([tiles[half] for half in range(2) for tiles in planes], 0)
+        stacked = jnp.concatenate([tiles[half] for half in range(2) for tiles in planes[:count]], 0)
         moved = jnp.dot(
             jnp.concatenate(split(stacked, 3), 1), turn, preferred_element_type=jnp.float32
         )
         stepped = []
-        for i in range(count):
-            turned = [
-                halved(moved[(half * count + i) * ROWS : (half * count + i + 1) * ROWS])
-                for half in range(2)
-            ]
-            west, east = bordered(*zip(*turned), halos[i])
-            stepped.append(
-                [five_point(weights[h], planes[i][h], west[h], east[h]) for h in range(2)]
-            )
+        for i, tiles in enumerate(planes):
+            if i < count:
+                turned = [
+                    halved(moved[(half * count + i) * ROWS : (half * count + i + 1) * ROWS])
+                    for half in range(2)
+                ]
+                west, east = bordered(*zip(*turned), halos[i])
+            else:
+                west, east = neighbours(tiles, halos[i])
+            stepped.append([five_point(weights[h], tiles[h], west[h], east[h]) for h in range(2)])
         planes = stepped
     return planes
 

time: 68.5 us -> 68.3 us (level)
  Pallas kernels: 11.4 us -> 10.6 us
    pallas_call x6, Pallas kernels: 11.4 us -> 10.6 us  [kernel(): pl.pallas_call(body, out_shape=shapes, in_specs=[vmem()] * len(operands)...]
where the time goes in v7:
time: 68.3 us; the launch traced here: 68 us
  blocking collectives  31 us (45%)
  starting transfers between devices  22 us (32%)
  Pallas kernels  10.6 us (16%)
  waiting for transfers between devices  3.6 us (5%)
  between operations  0.73 us (1%)
    all_to_all x2, blocking collectives, exchanged(): return lax.all_to_all(value, 'mem', split_axis=0, concat_axis=0, tiled=True)  31 us
    ppermute x4, starting transfers between devices, swapped(): return lax.ppermute(value, 'tile', pairs + [(b, a) for a, b in pairs])  22 us
    pallas_call x6, Pallas kernels, kernel(): pl.pallas_call(body, out_shape=shapes, in_specs=[vmem()] * len(operands)...  10.6 us
    ppermute x4, waiting for transfers between devices, swapped(): return lax.ppermute(value, 'tile', pairs + [(b, a) for a, b in pairs])  3.6 us
  transfers between devices with their start and end apart: 4, of which 2 were waited for; matrix products, arithmetic and copies ran while one was open for 0% of the time, Pallas kernels for 0%

profile of v7, /device:TPU:8, one launch (start us, length us, event | category | flops | bytes accessed | tf_op | source)
XLA Modules:
  0.0 68.0 jit_solution(11725470386782954660)
XLA Ops:
  0.0 1.7 %pack_edges.1 = (f32[16,256]{1,0:T(8,128)S(1)}, f32[16,256]{1,0:T(8,128)S(1)}, f32[8,8,16,256]{3,2,1,0:T(8,128)S(1)}, f32[8,16,256]{2,1,0:T(8,128)S(1)}, s32[16,...) custom-call(f32[8,8,16,256]{3,2,1,0:T(8,128)} %state.1, ...), custom_call_target="tpu_custom_call" | custom-call | tf_op jit(solution)/shard_map/pack_edges/pallas_call | solution.py:450
  1.7 12.6 %collective-permute-start = (f32[16,256]{1,0:T(8,128)S(1)}, f32[16,256]{1,0:T(8,128)S(1)}, u32[]{:S(2)}, u32[]{:S(2)}) collective-permute-start(f32[16,256]{1,0:T(8,128)S(1)} %get-tuple-element.18.sent_off.refs_3_.rest_3_), channel_id=1, source_target_pairs={{8,16},{24,32},{40,48},{56,64},{72,80},{88,96},{104,112},{120,128}... | collective-permute-start | bytes 49160 | tf_op jit(solution)/shard_map/ppermute | solution.py:467
  14.3 1.9 %collective-permute-start.1 = (f32[16,256]{1,0:T(8,128)S(1)}, f32[16,256]{1,0:T(8,128)S(1)}, u32[]{:S(2)}, u32[]{:S(2)}) collective-permute-start(f32[16,256]{1,0:T(8,128)S(1)} %get-tuple-element.19.sent_on.refs_4_.rest_4_), channel_id=1, source_target_pairs={{0,8},{16,24},{32,40},{48,56},{64,72},{80,88},{96,104},{112,120},{... | collective-permute-start | bytes 49160 | tf_op jit(solution)/shard_map/ppermute | solution.py:467
  16.9 0.0 collective-permute-done.off_chip.refs_5_.rest_5_
  16.9 0.5 collective-permute-done.1.on_chip.refs_6_.rest_6_
  17.4 0.9 %observe.1 = (f32[16,128]{1,0:T(8,128)S(1)}, f32[32,128]{1,0:T(8,128)S(1)}) custom-call(f32[8,8,16,256]{3,2,1,0:T(8,128)S(1)} %get-tuple-element.15.state.refs_0_.rest_0_, f32[8,16,256]{2,1,0:T(8,128)S(1)} %get-tuple-element.16.statics.refs_1_.rest_1_, s32[16,256]{1,0:T(8,128)S(1)} %get-tuple-element.17.wet.refs_2_.rest_2_, ...), custom_call_target="tpu_custom_call" | custom-call | tf_op jit(solution)/shard_map/observe/pallas_call | solution.py:450
  18.3 2.1 %collective-permute-start.3 = (f32[16,128]{1,0:T(8,128)S(1)}, f32[16,128]{1,0:T(8,128)S(1)}, u32[]{:S(2)}, u32[]{:S(2)}) collective-permute-start(f32[16,128]{1,0:T(8,128)S(1)} %get-tuple-element.24.own), channel_id=1, source_target_pairs={{0,8},{16,24},{32,40},{48,56},{64,72},{80,88},{96,104},{112,120},{... | collective-permute-start | bytes 24584 | tf_op jit(solution)/shard_map/ppermute | solution.py:467
  20.4 5.4 %collective-permute-start.2 = (f32[16,128]{1,0:T(8,128)S(1)}, f32[16,128]{1,0:T(8,128)S(1)}, u32[]{:S(2)}, u32[]{:S(2)}) collective-permute-start(f32[16,128]{1,0:T(8,128)S(1)} %get-tuple-element.24.own), channel_id=1, source_target_pairs={{8,16},{24,32},{40,48},{56,64},{72,80},{88,96},{104,112},{120,128}... | collective-permute-start | bytes 24584 | tf_op jit(solution)/shard_map/ppermute | solution.py:467
  25.9 0.0 collective-permute-done.3.on_chip
  25.9 3.1 %collective-permute-done.2.off_chip = f32[16,128]{1,0:T(8,128)S(1)} collective-permute-done((f32[16,128]{1,0:T(8,128)S(1)}, f32[16,128]{1,0:T(8,128)S(1)}, u32[]{:S(2)}, u32[]{:S(2)}) %collective-permute-start.2) | collective-permute-done | bytes 8224 | tf_op jit(solution)/shard_map/ppermute | solution.py:467
  29.0 2.5 %attach.1 = f32[8,280,128]{2,1,0:T(8,128)S(1)} custom-call(f32[8,280,128]{2,1,0:T(8,128)S(1)} %transport.1.chunks, f32[16,128]{1,0:T(8,128)S(1)} %get-tuple-element.24.own, f32[16,128]{1,0:T(8,128)S(1)} %collective-permute-done.2.off_chip, f32[16,128]{1,0:T(8,128)S(1)} %collective-permute-done.3.on_chip, ...), custom_call_target="tpu_custom_call", output_to_operand_aliasing={{}: (0, {})} | custom-call | tf_op jit(solution)/shard_map/attach/pallas_call | solution.py:450
  31.5 17.0 %all_to_all.10.received = f32[8,280,128]{2,1,0:T(8,128)S(1)} all-to-all(f32[8,280,128]{2,1,0:T(8,128)S(1)} %attach.1), channel_id=1, replica_groups=mesh['tile'=64,'mem'=8] {'mem'}, dimensions={0} | all-to-all | bytes 2293760 | tf_op jit(solution)/shard_map/all_to_all | solution.py:476
  48.5 4.3 %analyse.1 = f32[8,256,128]{2,1,0:T(8,128)S(1)} custom-call(f32[8,280,128]{2,1,0:T(8,128)S(1)} %all_to_all.10.received, f32[16,128]{1,0:T(8,128)S(1)} %get-tuple-element.24.own, f32[16,128]{1,0:T(8,128)S(1)} %collective-permute-done.2.off_chip, f32[16,128]{1,0:T(8,128)S(1)} %collective-permute-done.3.on_chip), custom_call_target="tpu_custom_call" | custom-call | tf_op jit(solution)/shard_map/analyse/pallas_call | solution.py:450
  52.9 14.0 %all_to_all.11 = f32[8,256,128]{2,1,0:T(8,128)S(1)} all-to-all(f32[8,256,128]{2,1,0:T(8,128)S(1)} %analyse.1), channel_id=1, replica_groups=mesh['tile'=64,'mem'=8] {'mem'}, dimensions={0} | all-to-all | bytes 2097152 | tf_op jit(solution)/shard_map/all_to_all | solution.py:476
  66.9 1.1 %unpack.1 = f32[8,8,16,256]{3,2,1,0:T(8,128)} custom-call(f32[8,2,8,16,128]{4,3,2,1,0:T(8,128)S(1)} %bitcast.4), custom_call_target="tpu_custom_call" | custom-call | tf_op jit(solution)/shard_map/unpack/pallas_call | solution.py:450
  (1 shorter events, 0.0 us)
Async XLA Ops:
  1.7 15.2 %collective-permute-start = (f32[16,256]{1,0:T(8,128)S(1)}, f32[16,256]{1,0:T(8,128)S(1)}, u32[]{:S(2)}, u32[]{:S(2)}) collective-permute-start(f32[16,256]{1,0:T(8,128)S(1)} %get-tuple-element.18.sent_off.refs_3_.rest_3_), channel_id=1, source_target_pairs={{8,16},{24,32},{40,48},{56,64},{72,80},{88,96},{104,112},{120,128}... | collective-permute-start | bytes 49160 | tf_op jit(solution)/shard_map/ppermute | solution.py:467
  14.3 3.1 %collective-permute-start.1 = (f32[16,256]{1,0:T(8,128)S(1)}, f32[16,256]{1,0:T(8,128)S(1)}, u32[]{:S(2)}, u32[]{:S(2)}) collective-permute-start(f32[16,256]{1,0:T(8,128)S(1)} %get-tuple-element.19.sent_on.refs_4_.rest_4_), channel_id=1, source_target_pairs={{0,8},{16,24},{32,40},{48,56},{64,72},{80,88},{96,104},{112,120},{... | collective-permute-start | bytes 49160 | tf_op jit(solution)/shard_map/ppermute | solution.py:467
  18.3 7.6 %collective-permute-start.3 = (f32[16,128]{1,0:T(8,128)S(1)}, f32[16,128]{1,0:T(8,128)S(1)}, u32[]{:S(2)}, u32[]{:S(2)}) collective-permute-start(f32[16,128]{1,0:T(8,128)S(1)} %get-tuple-element.24.own), channel_id=1, source_target_pairs={{0,8},{16,24},{32,40},{48,56},{64,72},{80,88},{96,104},{112,120},{... | collective-permute-start | bytes 24584 | tf_op jit(solution)/shard_map/ppermute | solution.py:467
  20.4 8.6 %collective-permute-start.2 = (f32[16,128]{1,0:T(8,128)S(1)}, f32[16,128]{1,0:T(8,128)S(1)}, u32[]{:S(2)}, u32[]{:S(2)}) collective-permute-start(f32[16,128]{1,0:T(8,128)S(1)} %get-tuple-element.24.own), channel_id=1, source_target_pairs={{8,16},{24,32},{40,48},{56,64},{72,80},{88,96},{104,112},{120,128}... | collective-permute-start | bytes 24584 | tf_op jit(solution)/shard_map/ppermute | solution.py:467

commit v8 on v7

--- a/solution.py
+++ b/solution.py
@@ -292,15 +292,15 @@
         out[e : e + 1, :] = jnp.sum(kept, 0, keepdims=True)
 
 
-def attach(chunks, own, off_chip, on_chip, *rest):
+def attach(chunks, own, last_chip, off_chip, on_chip, *rest):
     out = rest[-1]
 
     @pl.when(far())
     def _():
         forecast(*rest)
 
-    for i, block in enumerate((own, off_chip, on_chip)):
-        values = block[:MEMBERS]
+    near = (own[:MEMBERS], off_chip[:MEMBERS], on_chip[:MEMBERS] + last_chip[:MEMBERS])
+    for i, values in enumerate(near):
         for q in range(PLANES):
             out[q, pl.ds(CELL_ROWS + i * MEMBERS, MEMBERS), :] = values
 
@@ -389,11 +389,11 @@
     return jnp.concatenate(tiles, 0)
 
 
-def analyse(received, own, off_chip, on_chip, out):
+def analyse(received, own, last_chip, off_chip, on_chip, out):
     row = lax.broadcasted_iota(jnp.int32, (SYSTEM_ROWS, LANES), 0)
     diagonal = row == lane_index((SYSTEM_ROWS, LANES))
     identity = jnp.where(diagonal & (row < ENSEMBLE), 1.0, 0.0)
-    system = identity + gram(received, (own, off_chip, on_chip))
+    system = identity + gram(received, (own[...], off_chip[...], on_chip[...] + last_chip[...]))
     solved = inverse([system[8 * t : 8 * t + 8] for t in range(SYSTEM_ROWS // 8)])
     weights = 0.5 * (solved - identity)[:ENSEMBLE] - solved[ENSEMBLE : ENSEMBLE + 1]
     high, low = split(weights[:, :ENSEMBLE], 2)
@@ -461,15 +461,10 @@
     )(*operands, *scalars, *fetched)
 
 
-def swapped(value, start):
+def swapped(value, start, stop):
     count = lax.axis_size("tile")
-    pairs = [((i + start) % count, (i + 1 + start) % count) for i in range(0, count, 2)]
+    pairs = [(i, (i + 1) % count) for i in range(start, stop, 2)]
     return lax.ppermute(value, "tile", pairs + [(b, a) for a, b in pairs])
-
-
-def both_neighbours(off_chip, on_chip):
-    far = swapped(off_chip, 1)
-    return far, swapped(on_chip, 0)
 
 
 def exchanged(value):
@@ -494,7 +489,8 @@
         fetched=(member_tracer_state, diffusivity, velocity, wet_mask, *slot_rows),
         scratch=[pltpu.SemaphoreType.DMA((PARTS + 6,))],
     )
-    edges = (off_chip, on_chip, *both_neighbours(off_chip, on_chip))
+    count = lax.axis_size("tile")
+    edges = (off_chip, on_chip, swapped(off_chip, 1, count), swapped(on_chip, 0, count))
     own, sides_of = kernel(
         observe,
         (*blocks, *edges, cell, value, error),
@@ -502,7 +498,9 @@
         (2 * ROWS, LANES),
         scalars=(obs_count,),
     )
-    near = (own, *both_neighbours(own, own))
+    last_chip = swapped(own, count - 2, count)
+    off_chip = swapped(own, 1, count)
+    near = (own, last_chip, off_chip, swapped(own, 0, count - 2))
     home = (*blocks, *edges, sides_of)
     (chunks,) = kernel(transport, home, (PLANES, CHUNK_ROWS, LANES))
     (chunks,) = kernel(attach, (chunks, *near, *home), chunks.shape, aliases={0: 0})

time: 68.3 us -> 68.3 us (level)
    ppermute x4 -> x5, starting transfers between devices: 22 us -> 21.4 us  [swapped(): return lax.ppermute(value, 'tile', pairs + [(b, a) for a, b in pairs])]
    ppermute x4 -> x5, waiting for transfers between devices: 3.6 us -> 4.19 us  [swapped(): return lax.ppermute(value, 'tile', pairs + [(b, a) for a, b in pairs])]
  transfers between devices with their start and end apart: 4 -> 5, of which waited for: 2 -> 2; matrix products, arithmetic and copies ran while one was open for 0% -> 0% of each run, Pallas kernels for 0% -> 0%
where the time goes in v8:
time: 68.3 us; the launch traced here: 68 us
  blocking collectives  31 us (45%)
  starting transfers between devices  21.4 us (31%)
  Pallas kernels  10.6 us (16%)
  waiting for transfers between devices  4.19 us (6%)
  between operations  0.74 us (1%)
    all_to_all x2, blocking collectives, exchanged(): return lax.all_to_all(value, 'mem', split_axis=0, concat_axis=0, tiled=True)  31 us
    ppermute x5, starting transfers between devices, swapped(): return lax.ppermute(value, 'tile', pairs + [(b, a) for a, b in pairs])  21.4 us
    pallas_call x6, Pallas kernels, kernel(): pl.pallas_call(body, out_shape=shapes, in_specs=[vmem()] * len(operands)...  10.6 us
    ppermute x5, waiting for transfers between devices, swapped(): return lax.ppermute(value, 'tile', pairs + [(b, a) for a, b in pairs])  4.19 us
  transfers between devices with their start and end apart: 5, of which 2 were waited for; matrix products, arithmetic and copies ran while one was open for 0% of the time, Pallas kernels for 0%

profile of v8, /device:TPU:8, one launch (start us, length us, event | category | flops | bytes accessed | tf_op | source)
XLA Modules:
  0.0 68.0 jit_solution(18146034708654759482)
XLA Ops:
  0.0 1.7 %pack_edges.1 = (f32[16,256]{1,0:T(8,128)S(1)}, f32[16,256]{1,0:T(8,128)S(1)}, f32[8,8,16,256]{3,2,1,0:T(8,128)S(1)}, f32[8,16,256]{2,1,0:T(8,128)S(1)}, s32[16,...) custom-call(f32[8,8,16,256]{3,2,1,0:T(8,128)} %state.1, ...), custom_call_target="tpu_custom_call" | custom-call | tf_op jit(solution)/shard_map/pack_edges/pallas_call | solution.py:450
  1.7 12.6 %collective-permute-start = (f32[16,256]{1,0:T(8,128)S(1)}, f32[16,256]{1,0:T(8,128)S(1)}, u32[]{:S(2)}, u32[]{:S(2)}) collective-permute-start(f32[16,256]{1,0:T(8,128)S(1)} %get-tuple-element.18.sent_off.refs_3_.rest_3_), channel_id=1, source_target_pairs={{8,16},{24,32},{40,48},{56,64},{72,80},{88,96},{104,112},{120,128}... | collective-permute-start | bytes 49160 | tf_op jit(solution)/shard_map/ppermute | solution.py:467
  14.3 1.9 %collective-permute-start.1 = (f32[16,256]{1,0:T(8,128)S(1)}, f32[16,256]{1,0:T(8,128)S(1)}, u32[]{:S(2)}, u32[]{:S(2)}) collective-permute-start(f32[16,256]{1,0:T(8,128)S(1)} %get-tuple-element.19.sent_on.refs_4_.rest_4_), channel_id=1, source_target_pairs={{0,8},{16,24},{32,40},{48,56},{64,72},{80,88},{96,104},{112,120},{... | collective-permute-start | bytes 49160 | tf_op jit(solution)/shard_map/ppermute | solution.py:467
  16.9 0.0 collective-permute-done.off_chip.refs_5_.rest_5_
  16.9 0.5 collective-permute-done.1.on_chip.refs_6_.rest_6_
  17.4 0.9 %observe.1 = (f32[16,128]{1,0:T(8,128)S(1)}, f32[32,128]{1,0:T(8,128)S(1)}) custom-call(f32[8,8,16,256]{3,2,1,0:T(8,128)S(1)} %get-tuple-element.15.state.refs_0_.rest_0_, f32[8,16,256]{2,1,0:T(8,128)S(1)} %get-tuple-element.16.statics.refs_1_.rest_1_, s32[16,256]{1,0:T(8,128)S(1)} %get-tuple-element.17.wet.refs_2_.rest_2_, ...), custom_call_target="tpu_custom_call" | custom-call | tf_op jit(solution)/shard_map/observe/pallas_call | solution.py:450
  18.3 2.1 %collective-permute-start.4 = (f32[16,128]{1,0:T(8,128)S(1)}, f32[16,128]{1,0:T(8,128)S(1)}, u32[]{:S(2)}, u32[]{:S(2)}) collective-permute-start(f32[16,128]{1,0:T(8,128)S(1)} %get-tuple-element.24.own), channel_id=1, source_target_pairs={{0,8},{16,24},{32,40},{48,56},{64,72},{80,88},{96,104},{112,120},{... | collective-permute-start | bytes 24584 | tf_op jit(solution)/shard_map/ppermute | solution.py:467
  20.4 4.2 %collective-permute-start.3 = (f32[16,128]{1,0:T(8,128)S(1)}, f32[16,128]{1,0:T(8,128)S(1)}, u32[]{:S(2)}, u32[]{:S(2)}) collective-permute-start(f32[16,128]{1,0:T(8,128)S(1)} %get-tuple-element.24.own), channel_id=1, source_target_pairs={{8,16},{24,32},{40,48},{56,64},{72,80},{88,96},{104,112},{120,128}... | collective-permute-start | bytes 24584 | tf_op jit(solution)/shard_map/ppermute | solution.py:467
  24.6 0.7 collective-permute-start.2
  25.3 0.0 collective-permute-done.4.on_chip
  25.3 3.7 %collective-permute-done.3.off_chip = f32[16,128]{1,0:T(8,128)S(1)} collective-permute-done((f32[16,128]{1,0:T(8,128)S(1)}, f32[16,128]{1,0:T(8,128)S(1)}, u32[]{:S(2)}, u32[]{:S(2)}) %collective-permute-start.3) | collective-permute-done | bytes 8224 | tf_op jit(solution)/shard_map/ppermute | solution.py:467
  29.0 0.0 collective-permute-done.2.last_chip
  29.0 2.5 %attach.1 = f32[8,280,128]{2,1,0:T(8,128)S(1)} custom-call(f32[8,280,128]{2,1,0:T(8,128)S(1)} %transport.1.chunks, f32[16,128]{1,0:T(8,128)S(1)} %get-tuple-element.24.own, f32[16,128]{1,0:T(8,128)S(1)} %collective-permute-done.2.last_chip, f32[16,128]{1,0:T(8,128)S(1)} %collective-permute-done.3.off_chip, ...), custom_call_target="tpu_custom_call", output_to_operand_aliasing={{}: (0, {})} | custom-call | tf_op jit(solution)/shard_map/attach/pallas_call | solution.py:450
  31.5 17.0 %all_to_all.10.received = f32[8,280,128]{2,1,0:T(8,128)S(1)} all-to-all(f32[8,280,128]{2,1,0:T(8,128)S(1)} %attach.1), channel_id=1, replica_groups=mesh['tile'=64,'mem'=8] {'mem'}, dimensions={0} | all-to-all | bytes 2293760 | tf_op jit(solution)/shard_map/all_to_all | solution.py:471
  48.5 4.3 %analyse.1 = f32[8,256,128]{2,1,0:T(8,128)S(1)} custom-call(f32[8,280,128]{2,1,0:T(8,128)S(1)} %all_to_all.10.received, f32[16,128]{1,0:T(8,128)S(1)} %get-tuple-element.24.own, f32[16,128]{1,0:T(8,128)S(1)} %collective-permute-done.2.last_chip, f32[16,128]{1,0:T(8,128)S(1)} %collective-permute-done.3.off_chip, f32[16,128]{1,0:T(8,128)S(1)} %collective-permute-done.4.on_chip), custom_call_target="tpu_custom_call" | custom-call | tf_op jit(solution)/shard_map/analyse/pallas_call | solution.py:450
  52.9 14.0 %all_to_all.11 = f32[8,256,128]{2,1,0:T(8,128)S(1)} all-to-all(f32[8,256,128]{2,1,0:T(8,128)S(1)} %analyse.1), channel_id=1, replica_groups=mesh['tile'=64,'mem'=8] {'mem'}, dimensions={0} | all-to-all | bytes 2097152 | tf_op jit(solution)/shard_map/all_to_all | solution.py:471
  66.9 1.1 %unpack.1 = f32[8,8,16,256]{3,2,1,0:T(8,128)} custom-call(f32[8,2,8,16,128]{4,3,2,1,0:T(8,128)S(1)} %bitcast.4), custom_call_target="tpu_custom_call" | custom-call | tf_op jit(solution)/shard_map/unpack/pallas_call | solution.py:450
  (1 shorter events, 0.0 us)
Async XLA Ops:
  1.7 15.2 %collective-permute-start = (f32[16,256]{1,0:T(8,128)S(1)}, f32[16,256]{1,0:T(8,128)S(1)}, u32[]{:S(2)}, u32[]{:S(2)}) collective-permute-start(f32[16,256]{1,0:T(8,128)S(1)} %get-tuple-element.18.sent_off.refs_3_.rest_3_), channel_id=1, source_target_pairs={{8,16},{24,32},{40,48},{56,64},{72,80},{88,96},{104,112},{120,128}... | collective-permute-start | bytes 49160 | tf_op jit(solution)/shard_map/ppermute | solution.py:467
  14.3 3.1 %collective-permute-start.1 = (f32[16,256]{1,0:T(8,128)S(1)}, f32[16,256]{1,0:T(8,128)S(1)}, u32[]{:S(2)}, u32[]{:S(2)}) collective-permute-start(f32[16,256]{1,0:T(8,128)S(1)} %get-tuple-element.19.sent_on.refs_4_.rest_4_), channel_id=1, source_target_pairs={{0,8},{16,24},{32,40},{48,56},{64,72},{80,88},{96,104},{112,120},{... | collective-permute-start | bytes 49160 | tf_op jit(solution)/shard_map/ppermute | solution.py:467
  18.3 7.0 %collective-permute-start.4 = (f32[16,128]{1,0:T(8,128)S(1)}, f32[16,128]{1,0:T(8,128)S(1)}, u32[]{:S(2)}, u32[]{:S(2)}) collective-permute-start(f32[16,128]{1,0:T(8,128)S(1)} %get-tuple-element.24.own), channel_id=1, source_target_pairs={{0,8},{16,24},{32,40},{48,56},{64,72},{80,88},{96,104},{112,120},{... | collective-permute-start | bytes 24584 | tf_op jit(solution)/shard_map/ppermute | solution.py:467
  20.4 8.6 %collective-permute-start.3 = (f32[16,128]{1,0:T(8,128)S(1)}, f32[16,128]{1,0:T(8,128)S(1)}, u32[]{:S(2)}, u32[]{:S(2)}) collective-permute-start(f32[16,128]{1,0:T(8,128)S(1)} %get-tuple-element.24.own), channel_id=1, source_target_pairs={{8,16},{24,32},{40,48},{56,64},{72,80},{88,96},{104,112},{120,128}... | collective-permute-start | bytes 24584 | tf_op jit(solution)/shard_map/ppermute | solution.py:467
  24.6 4.4 %collective-permute-start.2 = (f32[16,128]{1,0:T(8,128)S(1)}, f32[16,128]{1,0:T(8,128)S(1)}, u32[]{:S(2)}, u32[]{:S(2)}) collective-permute-start(f32[16,128]{1,0:T(8,128)S(1)} %get-tuple-element.24.own), channel_id=1, source_target_pairs={{496,504},{504,496},{497,505},{505,497},{498,506},{506,498},{499,5... | collective-permute-start | bytes 24584 | tf_op jit(solution)/shard_map/ppermute | solution.py:467

commit v9 on v8

--- a/solution.py
+++ b/solution.py
@@ -350,7 +350,7 @@
     ]
 
 
-def inverse(tiles):
+def inverse(tiles, beside):
     row = lax.broadcasted_iota(jnp.int32, (8, LANES), 0)
     lane = lane_index((8, LANES))
     size = 4
@@ -360,6 +360,7 @@
 
     for k in range(0, ENSEMBLE, size):
         home, start = k // 8, k % 8
+        beside(k // size)
         columns = [[everywhere(tile[:, k + j : k + j + 1]) for tile in tiles] for j in range(size)]
         rows = [everywhere(tiles[home][start + i : start + i + 1]) for i in range(size)]
         pivots = pivot_inverse(
@@ -389,27 +390,32 @@
     return jnp.concatenate(tiles, 0)
 
 
-def analyse(received, own, last_chip, off_chip, on_chip, out):
+def analyse(received, own, last_chip, off_chip, on_chip, out, parts):
     row = lax.broadcasted_iota(jnp.int32, (SYSTEM_ROWS, LANES), 0)
     diagonal = row == lane_index((SYSTEM_ROWS, LANES))
     identity = jnp.where(diagonal & (row < ENSEMBLE), 1.0, 0.0)
     system = identity + gram(received, (own[...], off_chip[...], on_chip[...] + last_chip[...]))
-    solved = inverse([system[8 * t : 8 * t + 8] for t in range(SYSTEM_ROWS // 8)])
+
+    def members_of(r):
+        halves = [
+            received[:, first : first + MEMBERS, :].reshape(ENSEMBLE, LANES)
+            for first in (r * MEMBERS, HALF_ROWS + r * MEMBERS)
+        ]
+        return jnp.concatenate(halves, 1)
+
+    def prepare(r):
+        members = members_of(r)
+        mean = jnp.sum(members, 0, keepdims=True) / ENSEMBLE
+        high, low = split(members - mean, 2)
+        parts[r] = jnp.concatenate([high, high, low], 0)
+
+    solved = inverse([system[8 * t : 8 * t + 8] for t in range(SYSTEM_ROWS // 8)], prepare)
     weights = 0.5 * (solved - identity)[:ENSEMBLE] - solved[ENSEMBLE : ENSEMBLE + 1]
     high, low = split(weights[:, :ENSEMBLE], 2)
     weights = jnp.concatenate([high, low, high], 1)
     for r in range(ROWS):
-        members = jnp.concatenate(
-            [
-                received[:, first : first + MEMBERS, :].reshape(ENSEMBLE, LANES)
-                for first in (r * MEMBERS, HALF_ROWS + r * MEMBERS)
-            ],
-            1,
-        )
-        mean = jnp.sum(members, 0, keepdims=True) / ENSEMBLE
-        high, low = split(members - mean, 2)
-        result = members + jnp.dot(
-            weights, jnp.concatenate([high, high, low], 0), preferred_element_type=jnp.float32
+        result = members_of(r) + jnp.dot(
+            weights, parts[r], preferred_element_type=jnp.float32
         )
         for m in range(ENSEMBLE // MEMBERS):
             rows = result[m * MEMBERS : (m + 1) * MEMBERS]
@@ -505,7 +511,12 @@
     (chunks,) = kernel(transport, home, (PLANES, CHUNK_ROWS, LANES))
     (chunks,) = kernel(attach, (chunks, *near, *home), chunks.shape, aliases={0: 0})
     received = exchanged(chunks)
-    (updated,) = kernel(analyse, (received, *near), (PLANES, CELL_ROWS, LANES))
+    (updated,) = kernel(
+        analyse,
+        (received, *near),
+        (PLANES, CELL_ROWS, LANES),
+        scratch=[pltpu.VMEM((ROWS, 3 * ENSEMBLE, COLUMNS), jnp.bfloat16)],
+    )
     back = exchanged(updated)
     (analysis,) = kernel(
         unpack,

time: 68.3 us -> 68.3 us (level)
  no operation moved by 1% of the time
where the time goes in v9:
time: 68.3 us; the launch traced here: 68 us
  blocking collectives  31 us (45%)
  starting transfers between devices  21.4 us (31%)
  Pallas kernels  10.6 us (16%)
  waiting for transfers between devices  4.19 us (6%)
  between operations  0.74 us (1%)
    all_to_all x2, blocking collectives, exchanged(): return lax.all_to_all(value, 'mem', split_axis=0, concat_axis=0, tiled=True)  31 us
    ppermute x5, starting transfers between devices, swapped(): return lax.ppermute(value, 'tile', pairs + [(b, a) for a, b in pairs])  21.4 us
    pallas_call x6, Pallas kernels, kernel(): pl.pallas_call(body, out_shape=shapes, in_specs=[vmem()] * len(operands)...  10.6 us
    ppermute x5, waiting for transfers between devices, swapped(): return lax.ppermute(value, 'tile', pairs + [(b, a) for a, b in pairs])  4.19 us
  transfers between devices with their start and end apart: 5, of which 2 were waited for; matrix products, arithmetic and copies ran while one was open for 0% of the time, Pallas kernels for 0%

profile of v9, /device:TPU:8, one launch (start us, length us, event | category | flops | bytes accessed | tf_op | source)
XLA Modules:
  0.0 68.0 jit_solution(4775600361799419943)
XLA Ops:
  0.0 1.7 %pack_edges.1 = (f32[16,256]{1,0:T(8,128)S(1)}, f32[16,256]{1,0:T(8,128)S(1)}, f32[8,8,16,256]{3,2,1,0:T(8,128)S(1)}, f32[8,16,256]{2,1,0:T(8,128)S(1)}, s32[16,...) custom-call(f32[8,8,16,256]{3,2,1,0:T(8,128)} %state.1, ...), custom_call_target="tpu_custom_call" | custom-call | tf_op jit(solution)/shard_map/pack_edges/pallas_call | solution.py:456
  1.7 12.6 %collective-permute-start = (f32[16,256]{1,0:T(8,128)S(1)}, f32[16,256]{1,0:T(8,128)S(1)}, u32[]{:S(2)}, u32[]{:S(2)}) collective-permute-start(f32[16,256]{1,0:T(8,128)S(1)} %get-tuple-element.18.sent_off.refs_3_.rest_3_), channel_id=1, source_target_pairs={{8,16},{24,32},{40,48},{56,64},{72,80},{88,96},{104,112},{120,128}... | collective-permute-start | bytes 49160 | tf_op jit(solution)/shard_map/ppermute | solution.py:473
  14.3 1.9 %collective-permute-start.1 = (f32[16,256]{1,0:T(8,128)S(1)}, f32[16,256]{1,0:T(8,128)S(1)}, u32[]{:S(2)}, u32[]{:S(2)}) collective-permute-start(f32[16,256]{1,0:T(8,128)S(1)} %get-tuple-element.19.sent_on.refs_4_.rest_4_), channel_id=1, source_target_pairs={{0,8},{16,24},{32,40},{48,56},{64,72},{80,88},{96,104},{112,120},{... | collective-permute-start | bytes 49160 | tf_op jit(solution)/shard_map/ppermute | solution.py:473
  16.9 0.0 collective-permute-done.off_chip.refs_5_.rest_5_
  16.9 0.5 collective-permute-done.1.on_chip.refs_6_.rest_6_
  17.4 0.9 %observe.1 = (f32[16,128]{1,0:T(8,128)S(1)}, f32[32,128]{1,0:T(8,128)S(1)}) custom-call(f32[8,8,16,256]{3,2,1,0:T(8,128)S(1)} %get-tuple-element.15.state.refs_0_.rest_0_, f32[8,16,256]{2,1,0:T(8,128)S(1)} %get-tuple-element.16.statics.refs_1_.rest_1_, s32[16,256]{1,0:T(8,128)S(1)} %get-tuple-element.17.wet.refs_2_.rest_2_, ...), custom_call_target="tpu_custom_call" | custom-call | tf_op jit(solution)/shard_map/observe/pallas_call | solution.py:456
  18.3 2.1 %collective-permute-start.4 = (f32[16,128]{1,0:T(8,128)S(1)}, f32[16,128]{1,0:T(8,128)S(1)}, u32[]{:S(2)}, u32[]{:S(2)}) collective-permute-start(f32[16,128]{1,0:T(8,128)S(1)} %get-tuple-element.24.own), channel_id=1, source_target_pairs={{0,8},{16,24},{32,40},{48,56},{64,72},{80,88},{96,104},{112,120},{... | collective-permute-start | bytes 24584 | tf_op jit(solution)/shard_map/ppermute | solution.py:473
  20.4 4.2 %collective-permute-start.3 = (f32[16,128]{1,0:T(8,128)S(1)}, f32[16,128]{1,0:T(8,128)S(1)}, u32[]{:S(2)}, u32[]{:S(2)}) collective-permute-start(f32[16,128]{1,0:T(8,128)S(1)} %get-tuple-element.24.own), channel_id=1, source_target_pairs={{8,16},{24,32},{40,48},{56,64},{72,80},{88,96},{104,112},{120,128}... | collective-permute-start | bytes 24584 | tf_op jit(solution)/shard_map/ppermute | solution.py:473
  24.6 0.7 collective-permute-start.2
  25.3 0.0 collective-permute-done.4.on_chip
  25.3 3.7 %collective-permute-done.3.off_chip = f32[16,128]{1,0:T(8,128)S(1)} collective-permute-done((f32[16,128]{1,0:T(8,128)S(1)}, f32[16,128]{1,0:T(8,128)S(1)}, u32[]{:S(2)}, u32[]{:S(2)}) %collective-permute-start.3) | collective-permute-done | bytes 8224 | tf_op jit(solution)/shard_map/ppermute | solution.py:473
  29.0 0.0 collective-permute-done.2.last_chip
  29.0 2.5 %attach.1 = f32[8,280,128]{2,1,0:T(8,128)S(1)} custom-call(f32[8,280,128]{2,1,0:T(8,128)S(1)} %transport.1.chunks, f32[16,128]{1,0:T(8,128)S(1)} %get-tuple-element.24.own, f32[16,128]{1,0:T(8,128)S(1)} %collective-permute-done.2.last_chip, f32[16,128]{1,0:T(8,128)S(1)} %collective-permute-done.3.off_chip, ...), custom_call_target="tpu_custom_call", output_to_operand_aliasing={{}: (0, {})} | custom-call | tf_op jit(solution)/shard_map/attach/pallas_call | solution.py:456
  31.5 17.0 %all_to_all.10.received = f32[8,280,128]{2,1,0:T(8,128)S(1)} all-to-all(f32[8,280,128]{2,1,0:T(8,128)S(1)} %attach.1), channel_id=1, replica_groups=mesh['tile'=64,'mem'=8] {'mem'}, dimensions={0} | all-to-all | bytes 2293760 | tf_op jit(solution)/shard_map/all_to_all | solution.py:477
  48.5 4.3 %analyse.1 = f32[8,256,128]{2,1,0:T(8,128)S(1)} custom-call(f32[8,280,128]{2,1,0:T(8,128)S(1)} %all_to_all.10.received, f32[16,128]{1,0:T(8,128)S(1)} %get-tuple-element.24.own, f32[16,128]{1,0:T(8,128)S(1)} %collective-permute-done.2.last_chip, f32[16,128]{1,0:T(8,128)S(1)} %collective-permute-done.3.off_chip, f32[16,128]{1,0:T(8,128)S(1)} %collective-permute-done.4.on_chip), custom_call_target="tpu_custom_call" | custom-call | tf_op jit(solution)/shard_map/analyse/pallas_call | solution.py:456
  52.9 14.0 %all_to_all.11 = f32[8,256,128]{2,1,0:T(8,128)S(1)} all-to-all(f32[8,256,128]{2,1,0:T(8,128)S(1)} %analyse.1), channel_id=1, replica_groups=mesh['tile'=64,'mem'=8] {'mem'}, dimensions={0} | all-to-all | bytes 2097152 | tf_op jit(solution)/shard_map/all_to_all | solution.py:477
  66.9 1.1 %unpack.1 = f32[8,8,16,256]{3,2,1,0:T(8,128)} custom-call(f32[8,2,8,16,128]{4,3,2,1,0:T(8,128)S(1)} %bitcast.4), custom_call_target="tpu_custom_call" | custom-call | tf_op jit(solution)/shard_map/unpack/pallas_call | solution.py:456
  (1 shorter events, 0.0 us)
Async XLA Ops:
  1.7 15.2 %collective-permute-start = (f32[16,256]{1,0:T(8,128)S(1)}, f32[16,256]{1,0:T(8,128)S(1)}, u32[]{:S(2)}, u32[]{:S(2)}) collective-permute-start(f32[16,256]{1,0:T(8,128)S(1)} %get-tuple-element.18.sent_off.refs_3_.rest_3_), channel_id=1, source_target_pairs={{8,16},{24,32},{40,48},{56,64},{72,80},{88,96},{104,112},{120,128}... | collective-permute-start | bytes 49160 | tf_op jit(solution)/shard_map/ppermute | solution.py:473
  14.3 3.1 %collective-permute-start.1 = (f32[16,256]{1,0:T(8,128)S(1)}, f32[16,256]{1,0:T(8,128)S(1)}, u32[]{:S(2)}, u32[]{:S(2)}) collective-permute-start(f32[16,256]{1,0:T(8,128)S(1)} %get-tuple-element.19.sent_on.refs_4_.rest_4_), channel_id=1, source_target_pairs={{0,8},{16,24},{32,40},{48,56},{64,72},{80,88},{96,104},{112,120},{... | collective-permute-start | bytes 49160 | tf_op jit(solution)/shard_map/ppermute | solution.py:473
  18.3 7.0 %collective-permute-start.4 = (f32[16,128]{1,0:T(8,128)S(1)}, f32[16,128]{1,0:T(8,128)S(1)}, u32[]{:S(2)}, u32[]{:S(2)}) collective-permute-start(f32[16,128]{1,0:T(8,128)S(1)} %get-tuple-element.24.own), channel_id=1, source_target_pairs={{0,8},{16,24},{32,40},{48,56},{64,72},{80,88},{96,104},{112,120},{... | collective-permute-start | bytes 24584 | tf_op jit(solution)/shard_map/ppermute | solution.py:473
  20.4 8.6 %collective-permute-start.3 = (f32[16,128]{1,0:T(8,128)S(1)}, f32[16,128]{1,0:T(8,128)S(1)}, u32[]{:S(2)}, u32[]{:S(2)}) collective-permute-start(f32[16,128]{1,0:T(8,128)S(1)} %get-tuple-element.24.own), channel_id=1, source_target_pairs={{8,16},{24,32},{40,48},{56,64},{72,80},{88,96},{104,112},{120,128}... | collective-permute-start | bytes 24584 | tf_op jit(solution)/shard_map/ppermute | solution.py:473
  24.6 4.4 %collective-permute-start.2 = (f32[16,128]{1,0:T(8,128)S(1)}, f32[16,128]{1,0:T(8,128)S(1)}, u32[]{:S(2)}, u32[]{:S(2)}) collective-permute-start(f32[16,128]{1,0:T(8,128)S(1)} %get-tuple-element.24.own), channel_id=1, source_target_pairs={{496,504},{504,496},{497,505},{505,497},{498,506},{506,498},{499,5... | collective-permute-start | bytes 24584 | tf_op jit(solution)/shard_map/ppermute | solution.py:473
